TPU v7x, 32 devices: a whole 2x2x4 slice. The times are simulated.
32 devices in a mesh: slab: 4 (over x, core), src: 8 (over z, y).
Axes of the slice: x: 2, y: 2, z: 4, core: 2. Of those that a mesh axis runs over, the one named last changes fastest.
Arguments:
- trace_values: bfloat16 [8, 2048, 512], P('src', 'slab'), may hold values from -6 to 6
- trace_owner: int32 [8, 2048, 1], P('src', 'slab'), may hold values from 0 to 3; in each aligned block of 512 rows (0 to 511, 512 to 1023, ..., all dimensions but the last counted through in order) at most 256 rows name the same one
- trace_source: int32 [8, 2048], P('src', 'slab'), may hold values from 0 to 511
- source_fields: bfloat16 [2, 2048, 4096], P(None, 'slab', 'src'), may hold values from -0.0625 to 0.0625
- green_fields: bfloat16 [2, 2048, 4096], P(None, 'slab', 'src'), may hold values from -0.0625 to 0.0625
Outputs:
- gradient: float32 [4096], P('src')
Inputs may be any that keep to these rules, and one draw needn't show every extreme that they name: `trace_owner`: among the traces of one device, no owner is named by more than 256 traces, a bound that some block reaches.
All inputs are finite; a program needn't handle non-finite values.
Results may differ from a plain program's by a relative error of at most 0.0026.
Values may be sent and summed in bfloat16 or wider, within the bound.
No kernel may reach another device: no remote copies, remote signals or barrier semaphores. Data moves between devices by JAX's collectives and lax.ppermute only.
A program may use at most 64 MiB of HBM per device.

v0:
```python
import jax
import jax.numpy as jnp
from jax import lax
from jax.sharding import PartitionSpec as P


def on_device(trace_values, trace_owner, trace_source, source_fields, green_fields):
    values = trace_values[0]
    owners = trace_owner[0, :, 0]
    locals_id = trace_source[0]
    width = values.shape[1]
    half_width = width // 2
    src_count = lax.axis_size("src")
    sources_here = source_fields.shape[1]
    slab_index = lax.axis_index("slab")
    source_ids = jnp.arange(sources_here, dtype=jnp.int32)
    iota_high = (source_ids // 32).astype(jnp.bfloat16)
    iota_low = (source_ids % 32).astype(jnp.bfloat16)
    slab_here = slab_index.astype(jnp.bfloat16)
    high_part = (locals_id // 32).astype(jnp.bfloat16)
    low_part = (locals_id % 32).astype(jnp.bfloat16)
    piece_values = lax.all_gather(values, "slab", axis=0, tiled=True)
    piece_owners = lax.all_gather(owners.astype(jnp.bfloat16), "slab", axis=0, tiled=True)
    piece_high = lax.all_gather(high_part, "slab", axis=0, tiled=True)
    piece_low = lax.all_gather(low_part, "slab", axis=0, tiled=True)
    picks = (
        (iota_high[:, None] == piece_high[None, :])
        & (iota_low[:, None] == piece_low[None, :])
        & (piece_owners[None, :] == slab_here)
    )
    assembled = jnp.dot(
        picks.astype(jnp.bfloat16), piece_values, preferred_element_type=jnp.float32
    )
    residual_piece = assembled.astype(jnp.bfloat16)
    residual_rows = lax.all_gather(residual_piece, "src", axis=1, tiled=True)
    split_rows = residual_rows.reshape(sources_here, src_count, 2, half_width)
    res_real = split_rows[:, :, 0, :].reshape(sources_here, src_count * half_width)
    res_imag = split_rows[:, :, 1, :].reshape(sources_here, src_count * half_width)
    piece = lax.all_gather(green_fields, "slab", axis=1, tiled=True)
    adj_real = jnp.dot(res_real, piece[0], preferred_element_type=jnp.float32) + jnp.dot(
        res_imag, piece[1], preferred_element_type=jnp.float32
    )
    adj_imag = jnp.dot(res_real, piece[1], preferred_element_type=jnp.float32) - jnp.dot(
        res_imag, piece[0], preferred_element_type=jnp.float32
    )
    adj_real, adj_imag = (adj_real, adj_imag)
    partial_value = jnp.sum(
        source_fields[0].astype(jnp.float32) * adj_real
        - source_fields[1].astype(jnp.float32) * adj_imag,
        axis=0,
    )
    return lax.psum(partial_value, "slab")


def solution(mesh):
    in_specs = (
        P("src", "slab", None),
        P("src", "slab", None),
        P("src", "slab"),
        P(None, "slab", "src"),
        P(None, "slab", "src"),
    )
    out_specs = P("src")
    return jax.shard_map(
        on_device, mesh=mesh, in_specs=in_specs, out_specs=out_specs, check_vma=False
    )
```

profile of v0, /device:TPU:0, one launch (start us, length us, event | category | flops | bytes accessed | tf_op | source)
XLA Modules:
  0.0 172.6 jit_solution(2306685027073623609)
XLA Ops:
  6.5 0.0 all-gather.12.cloned.1.call-start
  6.5 0.7 all-gather.12.cloned.1.call-update
  7.3 0.0 all-gather.8.cloned.1.call-start
  7.3 0.7 fusion.31
  8.0 6.1 %all-gather.2 = bf16[4,1,512]{2,1,0:T(2,128)(2,1)S(1)} all-gather(bf16[1,1,512]{2,1,0:T(2,128)(2,1)S(1)} %reshape.43), channel_id=1, replica_groups=mesh['slab'=4,'src'=8] {'slab'}, dimensions={0}, use_global_device_ids=true | all-gather | bytes 5120 | tf_op jit(solution)/shard_map/all_gather | solution.py:24
  14.2 5.4 %all-gather.3 = bf16[4,1,512]{2,1,0:T(2,128)(2,1)S(1)} all-gather(bf16[1,1,512]{2,1,0:T(2,128)(2,1)S(1)} %reshape.45), channel_id=1, replica_groups=mesh['slab'=4,'src'=8] {'slab'}, dimensions={0}, use_global_device_ids=true | all-gather | bytes 5120 | tf_op jit(solution)/shard_map/all_gather | solution.py:25
  19.6 0.7 convert_element_type.51
  20.3 5.2 %all-gather = bf16[1,2048,1]{1,2,0:T(2,128)(2,1)S(1)} all-gather(bf16[1,512,1]{1,2,0:T(2,128)(2,1)S(1)} %convert_element_type.51), channel_id=2, replica_groups=mesh['slab'=4,'src'=8] {'slab'}, dimensions={1}, use_global_device_ids=true | all-gather | bytes 5120 | tf_op jit(solution)/shard_map/all_gather | solution.py:23
  25.5 8.8 %all-gather.12.cloned.1.call-done = bf16[1,2048,512]{2,1,0:T(8,128)(2,1)} async-done(((bf16[1,512,512]{2,1,0:T(8,128)(2,1)}), bf16[1,2048,512]{2,1,0:T(8,128)(2,1)}) %all-gather.12.cloned.1.call-update) | async-done | bytes 2097168 | tf_op jit(solution)/shard_map/all_gather | solution.py:22
  34.3 3.7 %fusion.16 = bf16[512,512]{1,0:T(8,128)(2,1)} fusion(bf16[1,2048,512]{2,1,0:T(8,128)(2,1)} %all-gather.12.cloned.1.call-done, pred[2048]{0:T(1024)(128)(4,1)S(1)} %compare_reduce_fusion, bf16[2048]{0:T(1024)(128)(2,1)S(1)} %bitcast.49, bf16[2048]{0:T(1024)(128)(2,1)S(1)} %bitcast.48, bf16[512]{0:T(512)(128)(2,1)S(1)} %get-tuple-element.10, ...), kind=kOutput, calls=%fused_computation.18 | convolution fusion | flops 1082392576 | bytes 2633728 | tf_op jit(solution)/shard_map/dot_general | solution.py:31
  38.0 0.0 all-gather.8.cloned.1.call-update
  38.0 0.0 all-gather.10.cloned.1.call-start
  38.1 0.7 all-gather.10.cloned.1.call-update
  38.8 74.4 %all-gather.8.cloned.1.call-done = bf16[512,4096]{1,0:T(8,128)(2,1)} async-done(((bf16[512,512]{1,0:T(8,128)(2,1)}), bf16[512,4096]{1,0:T(8,128)(2,1)}) %all-gather.8.cloned.1.call-update) | async-done | bytes 4194320 | tf_op jit(solution)/shard_map/all_gather | solution.py:35
  113.2 7.9 %reshape.36 = bf16[512,8,2,256]{3,2,1,0:T(2,128)(2,1)} reshape(bf16[512,4096]{1,0:T(8,128)(2,1)} %all-gather.8.cloned.1.call-done) | data formatting | bytes 8388608 | tf_op jit(solution)/shard_map/reshape | solution.py:36
  121.1 9.9 %fusion.38 = (bf16[512,8,1,256]{3,2,1,0:T(2,128)(2,1)}, bf16[512,8,1,256]{3,2,1,0:T(2,128)(2,1)}) fusion(bf16[512,8,2,256]{3,2,1,0:T(2,128)(2,1)} %reshape.36), kind=kLoop, calls=%fused_computation.48 | loop fusion | bytes 8388608 | tf_op jit(solution)/shard_map/slice | solution.py:38
  131.0 9.0 %copy.10 = bf16[512,8,1,256]{0,3,1,2:T(8,128)(2,1)S(1)} copy(bf16[512,8,1,256]{3,2,1,0:T(2,128)(2,1)} %get-tuple-element.6) | data formatting | bytes 4194304
  140.0 10.5 %copy.11 = bf16[512,8,1,256]{0,3,1,2:T(8,128)(2,1)} copy(bf16[512,8,1,256]{3,2,1,0:T(2,128)(2,1)} %get-tuple-element.5) | data formatting | bytes 4194304
  150.5 0.0 all-gather.10.cloned.1.call-done
  150.5 0.0 copy-start
  150.5 3.0 %fusion.8 = f32[512,512]{1,0:T(8,128)S(1)} fusion(bf16[512,2048]{0,1:T(8,128)(2,1)S(1)} %bitcast.42, bf16[2,2048,512]{2,1,0:T(8,128)(2,1)} %all-gather.10.cloned.1.call-done), kind=kOutput, calls=%fused_computation.10 | convolution fusion | flops 1073741824 | bytes 5242880 | tf_op jit(solution)/shard_map/dot_general | solution.py:40
  153.6 0.0 copy-done
  153.6 0.0 copy-start.1
  153.6 0.0 copy-start.2
  153.6 3.0 %fusion.7 = f32[512,512]{1,0:T(8,128)S(1)} fusion(bf16[512,2048]{0,1:T(8,128)(2,1)S(1)} %bitcast.44, bf16[2,2048,512]{2,1,0:T(8,128)(2,1)} %all-gather.10.cloned.1.call-done), kind=kOutput, calls=%fused_computation.9 | convolution fusion | flops 1073741824 | bytes 5242880 | tf_op jit(solution)/shard_map/dot_general | solution.py:43
  156.6 0.0 copy-done.1
  156.6 0.1 copy-done.2
  156.7 1.3 fusion.12
  158.0 1.3 fusion.21
  159.3 6.7 %psum.7 = f32[512]{0:T(512)} all-reduce(f32[512]{0:T(512)S(1)} %fusion.21), channel_id=1, replica_groups=mesh['slab'=4,'src'=8] {'slab'}, use_global_device_ids=true, to_apply=%region_1.2 | all-reduce | flops 512 | bytes 4096 | tf_op jit(solution)/shard_map/psum | solution.py:52
  (8 shorter events, 0.1 us)
Async XLA Ops:
  6.5 27.7 %all-gather.12.cloned.1.call-start = ((), (), s32[]{:S(2)}) async-start(), calls=%async_computation.2 | async-start | bytes 2621440 | tf_op jit(solution)/shard_map/all_gather | solution.py:22
  7.3 106.0 %all-gather.8.cloned.1.call-start = ((), (), s32[]{:S(2)}) async-start(), calls=%async_computation | async-start | bytes 4718592 | tf_op jit(solution)/shard_map/all_gather | solution.py:35
  38.0 112.5 %all-gather.10.cloned.1.call-start = ((), (), s32[]{:S(2)}) async-start(), calls=%async_computation.1 | async-start | bytes 5242880 | tf_op jit(solution)/shard_map/all_gather | solution.py:39
  150.5 3.0 %copy-start = (bf16[512,8,1,256]{0,3,1,2:T(8,128)(2,1)S(1)}, bf16[512,8,1,256]{0,3,1,2:T(8,128)(2,1)}, u32[]{:S(2)}) copy-start(bf16[512,8,1,256]{0,3,1,2:T(8,128)(2,1)} %copy.11) | copy-start | bytes 6291460
  153.6 3.0 %copy-start.1 = (bf16[2,2048,512]{2,1,0:T(8,128)(2,1)S(1)}, bf16[2,2048,512]{2,1,0:T(8,128)(2,1)}, u32[]{:S(2)}) copy-start(bf16[2,2048,512]{2,1,0:T(8,128)(2,1)} %all-gather.10.cloned.1.call-done) | copy-start | bytes 12582916
  153.6 3.1 %copy-start.2 = (bf16[2,512,512]{2,1,0:T(8,128)(2,1)S(1)}, bf16[2,512,512]{2,1,0:T(8,128)(2,1)}, u32[]{:S(2)}) copy-start(bf16[2,512,512]{2,1,0:T(8,128)(2,1)} %param.8) | copy-start | bytes 3145732
Sparse Core Ops, SparseCore 0:
  8.9 25.3 all-gather.11
  38.2 75.0 all-gather.7
  114.8 32.6 all-gather.9
where the time goes:
time: 173 us
  waiting for transfers between devices  84.6 us (49%)
  local copies, waits for them, and re-layouts  37.4 us (22%)
  blocking collectives  23.4 us (14%)
  between operations  13.2 us (8%)
  matrix products  12.4 us (7%)
    all_gather x1, waiting for transfers between devices, on_device(): residual_rows = lax.all_gather(residual_piece, 'src', axis=1, tiled=True)  74.4 us
    unnamed x12, local copies, waits for them, and re-layouts  19.6 us
    slice x1, local copies, waits for them, and re-layouts, on_device(): split_rows[:, :, 1, :].reshape(sources_here, src_count * half_width)  9.88 us
    all_gather x1, waiting for transfers between devices, on_device(): piece_values = lax.all_gather(values, 'slab', axis=0, tiled=True)  8.76 us
    reshape x1, local copies, waits for them, and re-layouts, on_device(): split_rows = residual_rows.reshape(sources_here, src_count, 2, half_width)  7.93 us
    psum x1, blocking collectives, on_device(): return lax.psum(partial_value, 'slab')  6.71 us
    all_gather x1, blocking collectives, on_device(): piece_high = lax.all_gather(high_part, 'slab', axis=0, tiled=True)  6.11 us
    all_gather x1, blocking collectives, on_device(): piece_low = lax.all_gather(low_part, 'slab', axis=0, tiled=True)  5.41 us
  transfers between devices with their start and end apart: 3, of which 2 were waited for; matrix products, arithmetic and copies ran while one was open for 22% of the time, Pallas kernels for 0%

commit v1 on v0

v1 whole, which is shorter than its diff:
```python
import functools

import jax
import jax.numpy as jnp
from jax import lax
from jax.experimental import pallas as pl
from jax.experimental.pallas import tpu as pltpu
from jax.sharding import PartitionSpec as P

AXES = ("slab", "src")
PAD = 16
TILE = 256
VMEM_LIMIT = 40 * 1024 * 1024


def params():
    return pltpu.CompilerParams(vmem_limit_bytes=VMEM_LIMIT)


SMEM_SPEC = pl.BlockSpec(memory_space=pltpu.SMEM)
VMEM_SPEC = pl.BlockSpec(memory_space=pltpu.VMEM)
ANY_SPEC = pl.BlockSpec(memory_space=pl.ANY)


def number(x, c, y, z, n_src):
    return (2 * x + c) * n_src + 2 * z + y


def id_rows(trace_owner, trace_source, sources_here):
    per = sources_here // TILE
    ids = trace_source[0]
    high = trace_owner[0, :, 0] * per + ids // TILE
    rows = jnp.stack([high, ids % TILE])
    return jnp.pad(rows, ((0, PAD - 2), (0, 0))).astype(jnp.bfloat16)


def prep_kernel(place, mine, other, mine_ids, other_ids, own_ref, away_ref):
    rows, width = mine.shape
    quarter = width // 4
    first = place[0] == 0
    for half, (values, ids) in enumerate(((mine, mine_ids), (other, other_ids))):
        spot = pl.ds(half * rows, rows)
        for part in range(2):
            low = values[:, 2 * part * quarter : (2 * part + 1) * quarter]
            high = values[:, (2 * part + 1) * quarter : (2 * part + 2) * quarter]
            lanes = pl.ds(part * quarter, quarter)
            own_ref[spot, lanes] = jnp.where(first, low, high)
            away_ref[spot, lanes] = jnp.where(first, high, low)
    tiles = rows // TILE
    pieces = [
        ids[kind : kind + 1, j * TILE : (j + 1) * TILE]
        for kind in range(2)
        for ids in (mine_ids, other_ids)
        for j in range(tiles)
    ]
    block = jnp.concatenate(
        pieces + [jnp.zeros((PAD - len(pieces), TILE), jnp.bfloat16)], axis=0
    )
    own_ref[2 * rows :, :] = block
    away_ref[2 * rows :, :] = block


def prep(place, mine, other, mine_ids, other_ids):
    rows, width = mine.shape
    shape = jax.ShapeDtypeStruct((2 * rows + PAD, width // 2), jnp.bfloat16)
    return pl.pallas_call(
        prep_kernel,
        name="prep",
        out_shape=(shape, shape),
        in_specs=[SMEM_SPEC] + [VMEM_SPEC] * 4,
        out_specs=(VMEM_SPEC, VMEM_SPEC),
        compiler_params=params(),
    )(place, mine, other, mine_ids, other_ids)


def fetch(which, candidates, target, sem):
    for k, ref in enumerate(candidates):

        @pl.when(which == k)
        def _(ref=ref):
            copy = pltpu.make_async_copy(ref, target, sem)
            copy.start()
            copy.wait()


def assemble(slab, pieces, group):
    traces = pieces[0].shape[0] - PAD
    tiles = traces // TILE
    iota = lax.broadcasted_iota(jnp.int32, (TILE, TILE), 0).astype(jnp.bfloat16)
    out = []
    owner = slab ^ group
    per = 2
    for h in range(per):
        name = (owner * per + h).astype(jnp.float32).astype(jnp.bfloat16)
        total = None
        for piece in pieces:
            masks = []
            for j in range(tiles):
                high = piece[traces + j : traces + j + 1, :]
                low = piece[traces + tiles + j : traces + tiles + j + 1, :]
                wanted = jnp.where(high == name, low, jnp.bfloat16(-1.0))
                masks.append(
                    jnp.where(iota == wanted, jnp.bfloat16(1.0), jnp.bfloat16(0.0))
                )
            mask = jnp.concatenate(masks, axis=1)
            term = jnp.dot(
                mask, piece[:traces, :], preferred_element_type=jnp.float32
            )
            total = term if total is None else total + term
        out.append(total.astype(jnp.bfloat16))
    return jnp.concatenate(out, axis=0)


def residual_kernel(n_a, n_b, place, *refs):
    cand_a, cand_b = refs[:n_a], refs[n_a : n_a + n_b]
    res_ref, piece_a, piece_b, sem = refs[n_a + n_b :]
    fetch(place[1], cand_a, piece_a, sem)
    fetch(place[1], cand_b, piece_b, sem)
    rows = res_ref.shape[0] // 4
    for group in range(4):
        res_ref[group * rows : (group + 1) * rows, :] = assemble(
            place[0], (piece_a, piece_b), group
        )


def residual(place, cand_a, cand_b, sources):
    piece = cand_a[0].shape
    return pl.pallas_call(
        functools.partial(residual_kernel, len(cand_a), len(cand_b)),
        name="residual",
        out_shape=jax.ShapeDtypeStruct((sources, piece[1]), jnp.bfloat16),
        in_specs=[SMEM_SPEC] + [ANY_SPEC] * (len(cand_a) + len(cand_b)),
        out_specs=VMEM_SPEC,
        scratch_shapes=[
            pltpu.VMEM(piece, jnp.bfloat16),
            pltpu.VMEM(piece, jnp.bfloat16),
            pltpu.SemaphoreType.DMA,
        ],
        compiler_params=params(),
        cost_estimate=pl.CostEstimate(
            flops=2 * sources * 2 * piece[0] * piece[1],
            bytes_accessed=6 * piece[0] * piece[1],
            transcendentals=0,
        ),
    )(place, *cand_a, *cand_b)


def correlate(res, fields):
    contract = (((0,), (0,)), ((), ()))
    rows = fields[0].shape[1]
    half = res[0].shape[1] // 2
    real, imag = None, None
    for group, field in enumerate(fields):
        piece = res[group]
        with_real = lax.dot_general(
            piece, field[0], contract, preferred_element_type=jnp.float32
        )
        with_imag = lax.dot_general(
            piece, field[1], contract, preferred_element_type=jnp.float32
        )
        first = with_real[:half] + with_imag[half:]
        second = with_real[half:] - with_imag[:half]
        real = first if real is None else real + first
        imag = second if imag is None else imag + second
    return real, imag


def correlate_kernel(n_res, *refs):
    res, fields, out_ref = refs[:n_res], refs[n_res : n_res + 4], refs[n_res + 4]
    rows = fields[0].shape[1]
    for k, ref in enumerate(res):
        parts = [ref[g * rows : (g + 1) * rows, :] for g in range(4)]
        real, imag = correlate(parts, fields)
        out_ref[k, 0] = real
        out_ref[k, 1] = imag


def correlated(res, fields):
    half, cells = res[0].shape[1] // 2, fields[0].shape[2]
    return pl.pallas_call(
        functools.partial(correlate_kernel, len(res)),
        name="correlate",
        out_shape=jax.ShapeDtypeStruct((len(res), 2, half, cells), jnp.float32),
        in_specs=[VMEM_SPEC] * (len(res) + 4),
        out_specs=VMEM_SPEC,
        compiler_params=params(),
        cost_estimate=pl.CostEstimate(
            flops=len(res) * 8 * res[0].shape[0] * half * cells,
            bytes_accessed=2 * res[0].size * len(res) + 8 * fields[0].size,
            transcendentals=0,
        ),
    )(*res, *fields)


def last_kernel(n_a, place, *refs):
    cand_a, cand_b = refs[:n_a], refs[n_a : 2 * n_a]
    earlier, near, far = refs[2 * n_a : 2 * n_a + 3]
    fields = refs[2 * n_a + 3 : 2 * n_a + 7]
    out_ref, piece_a, piece_b, sem = refs[2 * n_a + 7 :]
    fetch(place[1], cand_a, piece_a, sem)
    fetch(place[1], cand_b, piece_b, sem)
    parts = [assemble(place[0], (piece_a, piece_b), g) for g in range(4)]
    factors = [(earlier[k, 0], earlier[k, 1]) for k in range(3)]
    factors.append(correlate(parts, fields))
    y, away = place[2], place[3]
    half = near.shape[2]
    total = None
    for k, (real, imag) in zip((0, 1, 2, 3), (factors[0], factors[2], factors[1], factors[3])):
        line = y if k < 2 else 1 - y
        in_far = (away ^ (k % 2)) == 1
        green = [
            jnp.where(in_far, far[p, line], near[p, line]).astype(jnp.float32)
            for p in range(2)
        ]
        term = green[0] * real + green[1] * imag
        total = term if total is None else total + term
    out_ref[...] = jnp.sum(total, axis=0, keepdims=True)


def last(place, cand_a, cand_b, earlier, near, far, fields):
    piece = cand_a[0].shape
    cells = fields[0].shape[2]
    n = len(cand_a)
    return pl.pallas_call(
        functools.partial(last_kernel, n),
        name="last",
        out_shape=jax.ShapeDtypeStruct((1, cells), jnp.float32),
        in_specs=[SMEM_SPEC] + [ANY_SPEC] * (2 * n) + [VMEM_SPEC] * 7,
        out_specs=VMEM_SPEC,
        scratch_shapes=[
            pltpu.VMEM(piece, jnp.bfloat16),
            pltpu.VMEM(piece, jnp.bfloat16),
            pltpu.SemaphoreType.DMA,
        ],
        compiler_params=params(),
        cost_estimate=pl.CostEstimate(
            flops=2 * 4 * fields[0].shape[1] * 2 * piece[0] * piece[1],
            bytes_accessed=12 * 1024 * 1024,
            transcendentals=0,
        ),
    )(place, *cand_a, *cand_b, earlier, near, far, *fields)


def paired(n_src, trace_values, trace_owner, trace_source, source_fields, green_fields):
    values = trace_values[0]
    sources_here = source_fields.shape[1]
    slab = lax.axis_index("slab")
    src = lax.axis_index("src")
    x, c = slab // 2, slab % 2
    z, y = src // 2, src % 2
    lines = range(n_src // 2)

    def send(array, moves):
        pairs = [
            (number(*a, n_src), number(*b, n_src)) for a, b in moves
        ]
        return lax.ppermute(array, AXES, pairs)

    everywhere = [
        (a, b, d, e) for a in range(2) for b in range(2) for d in range(2) for e in lines
    ]
    to_core = [((a, b, d, e), (a, 1 - b, d, e)) for a, b, d, e in everywhere]
    to_x = [((a, b, d, e), (1 - a, b, d, e)) for a, b, d, e in everywhere]
    held = [(a, e % 2, d, e) for a in range(2) for d in range(2) for e in lines]

    def along_z(steps):
        return [
            ((a, b, d, e), (a, b, d, f))
            for b, e, f in steps
            for a in range(2)
            for d in range(2)
        ]

    def across_y(spots):
        return [
            ((a, b, d, e), (a, b, 1 - d, e))
            for b, e in spots
            for a in range(2)
            for d in range(2)
        ]

    mine_ids = id_rows(trace_owner, trace_source, sources_here)
    other = send(values, to_core)
    other_ids = send(mine_ids, to_core)
    own, away = prep(jnp.stack([x]).astype(jnp.int32), values, other, mine_ids, other_ids)
    crossed = send(away, [((a, b, d, e), (1 - a, b, d, e)) for a, b, d, e in held])

    field_x = send(source_fields, to_x)
    field_core = send(source_fields, to_core)
    field_far = send(field_x, to_core)
    fields = (source_fields, field_core, field_x, field_far)

    blocks = green_fields.reshape(2, 2, 2, -1, green_fields.shape[2])
    near = lax.dynamic_index_in_dim(blocks, x, 2, keepdims=False)
    far = send(lax.dynamic_index_in_dim(blocks, 1 - x, 2, keepdims=False), to_x)

    def spread(piece):
        z1 = send(piece, along_z([(0, 0, 1), (0, 2, 3), (1, 3, 2), (1, 1, 0)]))
        y1 = send(piece, across_y([(e % 2, e) for e in lines]))
        z2 = send(piece, along_z([(0, 2, 1), (1, 1, 2)]))
        y2 = send(z1, across_y([(1 - e % 2, e) for e in lines]))
        z3 = send(z1, along_z([(0, 1, 2), (1, 2, 1)]))
        z4 = send(z2, along_z([(0, 1, 0), (1, 2, 3)]))
        z5 = send(z3, along_z([(0, 2, 3), (1, 1, 0)]))
        y3 = send(z2, across_y([(0, 1), (1, 2)]))
        y4 = send(z3, across_y([(0, 2), (1, 1)]))
        y5 = send(z4, across_y([(0, 0), (1, 3)]))
        y6 = send(z5, across_y([(0, 3), (1, 0)]))
        return (piece, z1), (y1, y2), (z2, z3, z4, z5), (y3, y4, y5, y6)

    spread_a, spread_b = spread(own), spread(crossed)
    own_here = (c == z % 2)
    first = jnp.where(own_here, 0, 1)
    outer = ((z == 0) & (c == 0)) | ((z == 3) & (c == 1))
    inner = ((z == 2) & (c == 0)) | ((z == 1) & (c == 1))
    middle = ((z == 1) & (c == 0)) | ((z == 2) & (c == 1))
    second = jnp.where(middle, 0, jnp.where(inner, 1, jnp.where(outer, 2, 3)))
    away_flag = jnp.where(z // 2 == x, 0, 1)

    def place(which):
        return jnp.stack([slab, which, y, away_flag]).astype(jnp.int32)

    sources = 4 * sources_here
    res = [
        residual(place(first), spread_a[0], spread_b[0], sources),
        residual(place(first), spread_a[1], spread_b[1], sources),
        residual(place(second), spread_a[2], spread_b[2], sources),
    ]
    earlier = correlated(res, fields)
    partial = last(
        place(second), spread_a[3], spread_b[3], earlier, near, far, fields
    )[0]
    to_both = [((a, b, d, e), (1 - a, 1 - b, d, e)) for a, b, d, e in everywhere]
    here = partial + send(partial, to_core)
    there = send(partial, to_x) + send(partial, to_both)
    return here + there


def gathered(trace_values, trace_owner, trace_source, source_fields, green_fields):
    values = trace_values[0]
    half_width = values.shape[1] // 2
    src_count = lax.axis_size("src")
    sources_here = source_fields.shape[1]
    slab_index = lax.axis_index("slab")
    high = trace_owner[0, :, 0] * (sources_here // 32) + trace_source[0] // 32
    low = trace_source[0] % 32
    per_slab = sources_here // 32
    piece_values = lax.all_gather(values, "slab", axis=0, tiled=True)
    owners = trace_owner[0, :, 0].astype(jnp.bfloat16)
    high_part = (trace_source[0] // 32).astype(jnp.bfloat16)
    low_part = low.astype(jnp.bfloat16)
    piece_ids = lax.all_gather(
        jnp.stack([owners, high_part, low_part]), "slab", axis=1, tiled=True
    )
    ids = jnp.arange(sources_here, dtype=jnp.int32)
    picks = (
        ((ids // 32).astype(jnp.bfloat16)[:, None] == piece_ids[1][None, :])
        & ((ids % 32).astype(jnp.bfloat16)[:, None] == piece_ids[2][None, :])
        & (piece_ids[0][None, :] == slab_index.astype(jnp.bfloat16))
    )
    assembled = jnp.dot(
        picks.astype(jnp.bfloat16), piece_values, preferred_element_type=jnp.float32
    )
    rows = lax.all_gather(assembled.astype(jnp.bfloat16), "src", axis=1, tiled=True)
    split_rows = rows.reshape(sources_here, src_count, 2, half_width)
    res_real = split_rows[:, :, 0, :].reshape(sources_here, src_count * half_width)
    res_imag = split_rows[:, :, 1, :].reshape(sources_here, src_count * half_width)
    green = lax.all_gather(green_fields, "slab", axis=1, tiled=True)
    dot = functools.partial(jnp.dot, preferred_element_type=jnp.float32)
    adj_real = dot(res_real, green[0]) + dot(res_imag, green[1])
    adj_imag = dot(res_real, green[1]) - dot(res_imag, green[0])
    partial = jnp.sum(
        source_fields[0].astype(jnp.float32) * adj_real
        - source_fields[1].astype(jnp.float32) * adj_imag,
        axis=0,
    )
    return lax.psum(partial, "slab")


def solution(mesh):
    in_specs = (
        P("src", "slab", None),
        P("src", "slab", None),
        P("src", "slab"),
        P(None, "slab", "src"),
        P(None, "slab", "src"),
    )
    n_slab, n_src = mesh.shape["slab"], mesh.shape["src"]
    if n_slab == 2 * 2 and n_src == 2 * 4:
        on_device = functools.partial(paired, n_src)
    else:
        on_device = gathered
    return jax.shard_map(
        on_device, mesh=mesh, in_specs=in_specs, out_specs=P("src"), check_vma=False
    )
```

time: 173 us -> 126 us (0.73)
  the two profiles are of different devices: /device:TPU:0 before, /device:TPU:17 now
where the time goes in v1:
time: 126 us
  starting transfers between devices  52.1 us (41%)
  waiting for transfers between devices  37.4 us (30%)
  Pallas kernels  21.2 us (17%)
  local copies, waits for them, and re-layouts  12.9 us (10%)
  other arithmetic  1.47 us (1%)
    ppermute x32, starting transfers between devices, send(): return lax.ppermute(array, AXES, pairs)  52.1 us
    ppermute x32, waiting for transfers between devices, send(): return lax.ppermute(array, AXES, pairs)  37.4 us
    pallas_call x3, Pallas kernels, residual(): pl.pallas_call(functools.partial(residual_kernel, len(cand_a), len(cand_b...  12 us
    unnamed x44, local copies, waits for them, and re-layouts  11.6 us
    pallas_call x1, Pallas kernels, last(): pl.pallas_call(functools.partial(last_kernel, n), name='last', out_shape=...  4.49 us
    pallas_call x1, Pallas kernels, correlated(): pl.pallas_call(functools.partial(correlate_kernel, len(res)), name='corre...  3.47 us
  transfers between devices with their start and end apart: 32, of which 5 were waited for; matrix products, arithmetic and copies ran while one was open for 2% of the time, Pallas kernels for 13%

profile of v1, /device:TPU:17, one launch (start us, length us, event | category | flops | bytes accessed | tf_op | source)
XLA Modules:
  0.0 125.6 jit_solution(12308377949985030243)
XLA Ops:
  0.0 1.2 collective-permute-start.26
  1.2 1.0 collective-permute-start
  2.2 0.7 fusion.4
  3.0 1.3 %dynamic-slice_bitcast_fusion = (bf16[2,2,128,512]{3,2,1,0:T(8,128)(2,1)S(1)}, bf16[2,2,128,512]{3,2,1,0:T(8,128)(2,1)S(1)}) fusion(bf16[2,2,2,128,512]{4,3,2,1,0:T(8,128)(2,1)} %bitcast.27, s32[]{:T(128)S(6)} %select_n.76, s32[]{:T(128)S(6)} %select_n.75), kind=kLoop, calls=%fused_computation | loop fusion | bytes 2097160 | tf_op jit(solution)/shard_map/jit(dynamic_index_in_dim)/squeeze | solution.py:295
  4.7 0.7 collective-permute-start.25
  5.4 1.2 prep.1
  7.3 1.3 %collective-permute-start.4 = (bf16[1040,256]{1,0:T(8,128)(2,1)S(1)}, bf16[1040,256]{1,0:T(8,128)(2,1)S(1)}, u32[]{:S(2)}, u32[]{:S(2)}) collective-permute-start(bf16[1040,256]{1,0:T(8,128)(2,1)S(1)} %get-tuple-element.7.refs_0_), channel_id=1, source_target_pairs={{0,2},{1,3},{16,18},{17,19},{4,6},{5,7},{20,22},{21,23},{14,12},{1... | collective-permute-start | bytes 1597448 | tf_op jit(solution)/shard_map/ppermute | solution.py:257
  8.6 26.8 %collective-permute-done.28.refs_10_ = bf16[2,2,128,512]{3,2,1,0:T(8,128)(2,1)S(1)} collective-permute-done((bf16[2,2,128,512]{3,2,1,0:T(8,128)(2,1)S(1)}, bf16[2,2,128,512]{3,2,1,0:T(8,128)(2,1)S(1)}, u32[]{:S(2)}, u32[]{:S(2)}) %collective-permute-start.28) | collective-permute-done | bytes 524320 | tf_op jit(solution)/shard_map/ppermute | solution.py:257
  35.5 0.8 copy-done.5
  36.3 1.3 %collective-permute-start.2 = (bf16[1040,256]{1,0:T(8,128)(2,1)S(1)}, bf16[1040,256]{1,0:T(8,128)(2,1)S(1)}, u32[]{:S(2)}, u32[]{:S(2)}) collective-permute-start(bf16[1040,256]{1,0:T(8,128)(2,1)S(1)} %get-tuple-element.7.refs_0_), channel_id=1, source_target_pairs={{4,2},{5,3},{20,18},{21,19},{10,12},{11,13},{26,28},{27,29}} | collective-permute-start | bytes 1597448 | tf_op jit(solution)/shard_map/ppermute | solution.py:257
  38.3 0.8 copy-done.12
  39.1 1.3 %collective-permute-start.14 = (bf16[1040,256]{1,0:T(8,128)(2,1)S(1)}, bf16[1040,256]{1,0:T(8,128)(2,1)}, u32[]{:S(2)}, u32[]{:S(2)}) collective-permute-start(bf16[1040,256]{1,0:T(8,128)(2,1)S(1)} %collective-permute-done.11.refs_2_), channel_id=1, source_target_pairs={{0,2},{1,3},{16,18},{17,19},{4,6},{5,7},{20,22},{21,23},{14,12},{1... | collective-permute-start | bytes 1597448 | tf_op jit(solution)/shard_map/ppermute | solution.py:257
  40.4 8.1 %collective-permute-start.5 = (bf16[1040,256]{1,0:T(8,128)(2,1)S(1)}, bf16[1040,256]{1,0:T(8,128)(2,1)}, u32[]{:S(2)}, u32[]{:S(2)}) collective-permute-start(bf16[1040,256]{1,0:T(8,128)(2,1)S(1)} %collective-permute-done.4.refs_1_), channel_id=1, source_target_pairs={{2,4},{3,5},{18,20},{19,21},{12,10},{13,11},{28,26},{29,27}} | collective-permute-start | bytes 1597448 | tf_op jit(solution)/shard_map/ppermute | solution.py:257
  48.5 1.0 copy-done.1
  49.5 1.3 %collective-permute-start.12 = (bf16[1040,256]{1,0:T(8,128)(2,1)S(1)}, bf16[1040,256]{1,0:T(8,128)(2,1)}, u32[]{:S(2)}, u32[]{:S(2)}) collective-permute-start(bf16[1040,256]{1,0:T(8,128)(2,1)S(1)} %collective-permute-done.11.refs_2_), channel_id=1, source_target_pairs={{4,2},{5,3},{20,18},{21,19},{10,12},{11,13},{26,28},{27,29}} | collective-permute-start | bytes 1597448 | tf_op jit(solution)/shard_map/ppermute | solution.py:257
  50.8 2.1 %collective-permute-start.7 = (bf16[1040,256]{1,0:T(8,128)(2,1)S(1)}, bf16[1040,256]{1,0:T(8,128)(2,1)}, u32[]{:S(2)}, u32[]{:S(2)}) collective-permute-start(bf16[1040,256]{1,0:T(8,128)(2,1)S(1)} %collective-permute-done.2.refs_0_), channel_id=1, source_target_pairs={{2,0},{3,1},{18,16},{19,17},{12,14},{13,15},{28,30},{29,31}} | collective-permute-start | bytes 1597448 | tf_op jit(solution)/shard_map/ppermute | solution.py:257
  52.9 0.8 copy-done.10
  53.7 2.3 %collective-permute-start.22 = (bf16[1040,256]{1,0:T(8,128)(2,1)S(1)}, bf16[1040,256]{1,0:T(8,128)(2,1)S(1)}, u32[]{:S(2)}, u32[]{:S(2)}) collective-permute-start(bf16[1040,256]{1,0:T(8,128)(2,1)S(1)} %collective-permute-done.4.refs_1_), channel_id=1, source_target_pairs={{8,9},{9,8},{24,25},{25,24},{2,3},{3,2},{18,19},{19,18},{12,13},{1... | collective-permute-start | bytes 1597448 | tf_op jit(solution)/shard_map/ppermute | solution.py:257
  56.0 0.8 copy-done.16
  56.8 3.1 %collective-permute-start.27 = (bf16[2,512,512]{2,1,0:T(8,128)(2,1)S(1)}, bf16[2,512,512]{2,1,0:T(8,128)(2,1)S(1)}, u32[]{:S(2)}, u32[]{:S(2)}) collective-permute-start(bf16[2,512,512]{2,1,0:T(8,128)(2,1)S(1)} %collective-permute-done.26.refs_5_.refs_13_), channel_id=1, source_target_pairs={{0,8},{2,10},{4,12},{6,14},{1,9},{3,11},{5,13},{7,15},{8,0},{10,2}... | collective-permute-start | bytes 3145736 | tf_op jit(solution)/shard_map/ppermute | solution.py:257
  60.6 0.8 copy-done.14
  61.4 2.6 %collective-permute-done.12.refs_4_ = bf16[1040,256]{1,0:T(8,128)(2,1)} collective-permute-done((bf16[1040,256]{1,0:T(8,128)(2,1)S(1)}, bf16[1040,256]{1,0:T(8,128)(2,1)}, u32[]{:S(2)}, u32[]{:S(2)}) %collective-permute-start.12) | collective-permute-done | bytes 532512 | tf_op jit(solution)/shard_map/ppermute | solution.py:257
  64.0 2.1 %collective-permute-start.3 = (bf16[1040,256]{1,0:T(8,128)(2,1)S(1)}, bf16[1040,256]{1,0:T(8,128)(2,1)S(1)}, u32[]{:S(2)}, u32[]{:S(2)}) collective-permute-start(bf16[1040,256]{1,0:T(8,128)(2,1)S(1)} %collective-permute-done.2.refs_0_), channel_id=1, source_target_pairs={{2,3},{3,2},{18,19},{19,18},{12,13},{13,12},{28,29},{29,28}} | collective-permute-start | bytes 1597448 | tf_op jit(solution)/shard_map/ppermute | solution.py:257
  66.2 0.8 copy-done.8
  67.0 2.1 %collective-permute-start.15 = (bf16[1040,256]{1,0:T(8,128)(2,1)}, bf16[1040,256]{1,0:T(8,128)(2,1)}, u32[]{:S(2)}, u32[]{:S(2)}) collective-permute-start(bf16[1040,256]{1,0:T(8,128)(2,1)} %collective-permute-done.14.refs_3_), channel_id=1, source_target_pairs={{2,4},{3,5},{18,20},{19,21},{12,10},{13,11},{28,26},{29,27}} | collective-permute-start | bytes 1597448 | tf_op jit(solution)/shard_map/ppermute | solution.py:257
  69.1 0.8 copy-done.18
  70.0 1.5 %collective-permute-start.9 = (bf16[1040,256]{1,0:T(8,128)(2,1)}, bf16[1040,256]{1,0:T(8,128)(2,1)}, u32[]{:S(2)}, u32[]{:S(2)}) collective-permute-start(bf16[1040,256]{1,0:T(8,128)(2,1)} %collective-permute-done.5.refs_1_), channel_id=1, source_target_pairs={{4,6},{5,7},{20,22},{21,23},{10,8},{11,9},{26,24},{27,25}} | collective-permute-start | bytes 1597448 | tf_op jit(solution)/shard_map/ppermute | solution.py:257
  71.4 0.8 copy-done.20
  72.2 2.1 %collective-permute-start.17 = (bf16[1040,256]{1,0:T(8,128)(2,1)}, bf16[1040,256]{1,0:T(8,128)(2,1)}, u32[]{:S(2)}, u32[]{:S(2)}) collective-permute-start(bf16[1040,256]{1,0:T(8,128)(2,1)} %collective-permute-done.12.refs_4_), channel_id=1, source_target_pairs={{2,0},{3,1},{18,16},{19,17},{12,14},{13,15},{28,30},{29,31}} | collective-permute-start | bytes 1597448 | tf_op jit(solution)/shard_map/ppermute | solution.py:257
  74.3 5.4 %collective-permute-done.3.refs_0_ = bf16[1040,256]{1,0:T(8,128)(2,1)S(1)} collective-permute-done((bf16[1040,256]{1,0:T(8,128)(2,1)S(1)}, bf16[1040,256]{1,0:T(8,128)(2,1)S(1)}, u32[]{:S(2)}, u32[]{:S(2)}) %collective-permute-start.3) | collective-permute-done | bytes 532512 | tf_op jit(solution)/shard_map/ppermute | solution.py:257
  79.7 2.4 %collective-permute-start.24 = (bf16[1040,256]{1,0:T(8,128)(2,1)}, bf16[1040,256]{1,0:T(8,128)(2,1)}, u32[]{:S(2)}, u32[]{:S(2)}) collective-permute-start(bf16[1040,256]{1,0:T(8,128)(2,1)} %collective-permute-done.14.refs_3_), channel_id=1, source_target_pairs={{8,9},{9,8},{24,25},{25,24},{2,3},{3,2},{18,19},{19,18},{12,13},{1... | collective-permute-start | bytes 1597448 | tf_op jit(solution)/shard_map/ppermute | solution.py:257
  82.1 1.0 copy-done.3
  83.1 1.5 %collective-permute-start.6 = (bf16[1040,256]{1,0:T(8,128)(2,1)}, bf16[1040,256]{1,0:T(8,128)(2,1)}, u32[]{:S(2)}, u32[]{:S(2)}) collective-permute-start(bf16[1040,256]{1,0:T(8,128)(2,1)} %collective-permute-done.5.refs_1_), channel_id=1, source_target_pairs={{4,5},{5,4},{20,21},{21,20},{10,11},{11,10},{26,27},{27,26}} | collective-permute-start | bytes 1597448 | tf_op jit(solution)/shard_map/ppermute | solution.py:257
  84.6 1.5 %collective-permute-start.8 = (bf16[1040,256]{1,0:T(8,128)(2,1)}, bf16[1040,256]{1,0:T(8,128)(2,1)}, u32[]{:S(2)}, u32[]{:S(2)}) collective-permute-start(bf16[1040,256]{1,0:T(8,128)(2,1)} %collective-permute-done.7.refs_2_), channel_id=1, source_target_pairs={{0,1},{1,0},{16,17},{17,16},{14,15},{15,14},{30,31},{31,30}} | collective-permute-start | bytes 1597448 | tf_op jit(solution)/shard_map/ppermute | solution.py:257
  86.0 1.5 %collective-permute-start.19 = (bf16[1040,256]{1,0:T(8,128)(2,1)}, bf16[1040,256]{1,0:T(8,128)(2,1)}, u32[]{:S(2)}, u32[]{:S(2)}) collective-permute-start(bf16[1040,256]{1,0:T(8,128)(2,1)} %collective-permute-done.15.refs_5_), channel_id=1, source_target_pairs={{4,6},{5,7},{20,22},{21,23},{10,8},{11,9},{26,24},{27,25}} | collective-permute-start | bytes 1597448 | tf_op jit(solution)/shard_map/ppermute | solution.py:257
  87.7 1.0 copy-done.13
  88.7 1.0 copy-done.15
  89.8 1.0 copy-done.17
  90.8 4.0 %residual.3.refs_0_ = bf16[2048,256]{1,0:T(8,128)(2,1)S(1)} custom-call(s32[4]{0:T(128)S(1)} %add_add_fusion.2.place, bf16[1040,256]{1,0:T(8,128)(2,1)S(1)} %copy-done.13, bf16[1040,256]{1,0:T(8,128)(2,1)S(1)} %copy-done.17, bf16[1040,256]{1,0:T(8,128)(2,1)S(1)} %copy-done.15, bf16[1040,256]{1,0:T(8,128)(2,1)} %collective-permute-done.14.refs_3_), custom_call_target="tpu_custom_call" | custom-call | flops 2181038080 | bytes 1597440 | tf_op jit(solution)/shard_map/residual/pallas_call | solution.py:128
  94.8 3.0 %collective-permute-start.13 = (bf16[1040,256]{1,0:T(8,128)(2,1)}, bf16[1040,256]{1,0:T(8,128)(2,1)S(1)}, u32[]{:S(2)}, u32[]{:S(2)}) collective-permute-start(bf16[1040,256]{1,0:T(8,128)(2,1)} %collective-permute-done.12.refs_4_), channel_id=1, source_target_pairs={{2,3},{3,2},{18,19},{19,18},{12,13},{13,12},{28,29},{29,28}} | collective-permute-start | bytes 1597448 | tf_op jit(solution)/shard_map/ppermute | solution.py:257
  100.7 4.0 %residual.4.refs_1_ = bf16[2048,256]{1,0:T(8,128)(2,1)S(1)} custom-call(s32[4]{0:T(128)S(1)} %add_add_fusion.2.place, bf16[1040,256]{1,0:T(8,128)(2,1)S(1)} %copy-done.11, bf16[1040,256]{1,0:T(8,128)(2,1)S(1)} %copy-done.19, bf16[1040,256]{1,0:T(8,128)(2,1)S(1)} %copy-done.21, bf16[1040,256]{1,0:T(8,128)(2,1)} %collective-permute-done.24.refs_3_), custom_call_target="tpu_custom_call" | custom-call | flops 2181038080 | bytes 1597440 | tf_op jit(solution)/shard_map/residual/pallas_call | solution.py:128
  104.7 4.0 %residual.5.refs_2_ = bf16[2048,256]{1,0:T(8,128)(2,1)S(1)} custom-call(s32[4]{0:T(128)S(1)} %add_add_fusion.1.place, bf16[1040,256]{1,0:T(8,128)(2,1)S(1)} %copy-done.9, bf16[1040,256]{1,0:T(8,128)(2,1)} %collective-permute-done.5.refs_1_, bf16[1040,256]{1,0:T(8,128)(2,1)} %collective-permute-done.7.refs_2_, ...), custom_call_target="tpu_custom_call" | custom-call | flops 2181038080 | bytes 1597440 | tf_op jit(solution)/shard_map/residual/pallas_call | solution.py:128
  108.8 3.5 %correlate.1.refs_8_ = f32[3,2,128,512]{3,2,1,0:T(8,128)S(1)} custom-call(bf16[2048,256]{1,0:T(8,128)(2,1)S(1)} %residual.3.refs_0_, bf16[2048,256]{1,0:T(8,128)(2,1)S(1)} %residual.4.refs_1_, bf16[2048,256]{1,0:T(8,128)(2,1)S(1)} %residual.5.refs_2_, bf16[2,512,512]{2,1,0:T(8,128)(2,1)S(1)} %copy-done, bf16[2,512,512]{2,1,0:T(8,128)(2,1)S(1)} %copy-done.2, ...), custom_call_target="tpu_custom_call" | custom-call | flops 3221225472 | bytes 7340032 | tf_op jit(solution)/shard_map/correlate/pallas_call | solution.py:180
  112.3 4.5 %last.1 = f32[1,512]{1,0:T(1,128)S(1)} custom-call(s32[4]{0:T(128)S(1)} %add_add_fusion.1.place, bf16[1040,256]{1,0:T(8,128)(2,1)S(1)} %collective-permute-done.3.refs_0_, bf16[1040,256]{1,0:T(8,128)(2,1)} %collective-permute-done.6.refs_1_, bf16[1040,256]{1,0:T(8,128)(2,1)} %collective-permute-done.8.refs_2_, ...), custom_call_target="tpu_custom_call" | custom-call | flops 2181038080 | bytes 12582912 | tf_op jit(solution)/shard_map/last/pallas_call | solution.py:224
  116.8 3.9 %collective-permute-start.29 = (f32[512]{0:T(512)S(1)}, f32[512]{0:T(512)S(1)}, u32[]{:S(2)}, u32[]{:S(2)}) collective-permute-start(f32[512]{0:T(512)S(1)} %bitcast.23), channel_id=1, source_target_pairs={{0,8},{2,10},{4,12},{6,14},{1,9},{3,11},{5,13},{7,15},{8,0},{10,2}... | collective-permute-start | bytes 6152 | tf_op jit(solution)/shard_map/ppermute | solution.py:257
  120.7 1.2 collective-permute-start.30
  122.5 0.7 collective-permute-done.30
  123.2 1.8 %collective-permute-done.31 = f32[512]{0:T(512)S(1)} collective-permute-done((f32[512]{0:T(512)S(1)}, f32[512]{0:T(512)S(1)}, u32[]{:S(2)}, u32[]{:S(2)}) %collective-permute-start.31) | collective-permute-done | bytes 2080 | tf_op jit(solution)/shard_map/ppermute | solution.py:257
  (72 shorter events, 6.6 us)
Async XLA Ops:
  0.0 4.7 %copy-start = (bf16[2,512,512]{2,1,0:T(8,128)(2,1)S(1)}, bf16[2,512,512]{2,1,0:T(8,128)(2,1)}, u32[]{:S(2)}) copy-start(bf16[2,512,512]{2,1,0:T(8,128)(2,1)} %refs_11_.1) | copy-start | bytes 3145732
  0.0 5.4 %copy-start.7 = (bf16[1,512,512]{2,1,0:T(8,128)(2,1)S(1)}, bf16[1,512,512]{2,1,0:T(8,128)(2,1)}, u32[]{:S(2)}) copy-start(bf16[1,512,512]{2,1,0:T(8,128)(2,1)} %param.5) | copy-start | bytes 1572868
  0.0 37.6 %collective-permute-start.26 = (bf16[2,512,512]{2,1,0:T(8,128)(2,1)}, bf16[2,512,512]{2,1,0:T(8,128)(2,1)S(1)}, u32[]{:S(2)}, u32[]{:S(2)}) collective-permute-start(bf16[2,512,512]{2,1,0:T(8,128)(2,1)} %refs_11_.1), channel_id=1, source_target_pairs={{0,16},{2,18},{4,20},{6,22},{1,17},{3,19},{5,21},{7,23},{8,24},{10... | collective-permute-start | bytes 3145736 | tf_op jit(solution)/shard_map/ppermute | solution.py:257
  1.2 4.2 %collective-permute-start = (bf16[512,512]{1,0:T(8,128)(2,1)}, bf16[512,512]{1,0:T(8,128)(2,1)}, u32[]{:S(2)}, u32[]{:S(2)}) collective-permute-start(bf16[512,512]{1,0:T(8,128)(2,1)} %bitcast.21), channel_id=1, source_target_pairs={{0,8},{2,10},{4,12},{6,14},{1,9},{3,11},{5,13},{7,15},{8,0},{10,2}... | collective-permute-start | bytes 1572872 | tf_op jit(solution)/shard_map/ppermute | solution.py:257
  2.9 2.5 %collective-permute-start.1 = (bf16[16,512]{1,0:T(8,128)(2,1)S(1)}, bf16[16,512]{1,0:T(8,128)(2,1)S(1)}, u32[]{:S(2)}, u32[]{:S(2)}) collective-permute-start(bf16[16,512]{1,0:T(8,128)(2,1)S(1)} %fusion.2.mine_ids), channel_id=1, source_target_pairs={{0,8},{2,10},{4,12},{6,14},{1,9},{3,11},{5,13},{7,15},{8,0},{10,2}... | collective-permute-start | bytes 49160 | tf_op jit(solution)/shard_map/ppermute | solution.py:257
  4.3 31.1 %collective-permute-start.28 = (bf16[2,2,128,512]{3,2,1,0:T(8,128)(2,1)S(1)}, bf16[2,2,128,512]{3,2,1,0:T(8,128)(2,1)S(1)}, u32[]{:S(2)}, u32[]{:S(2)}) collective-permute-start(bf16[2,2,128,512]{3,2,1,0:T(8,128)(2,1)S(1)} %get-tuple-element.9), channel_id=1, source_target_pairs={{0,16},{2,18},{4,20},{6,22},{1,17},{3,19},{5,21},{7,23},{8,24},{10... | collective-permute-start | bytes 1572872 | tf_op jit(solution)/shard_map/ppermute | solution.py:257
  4.7 43.9 %collective-permute-start.25 = (bf16[2,512,512]{2,1,0:T(8,128)(2,1)S(1)}, bf16[2,512,512]{2,1,0:T(8,128)(2,1)S(1)}, u32[]{:S(2)}, u32[]{:S(2)}) collective-permute-start(bf16[2,512,512]{2,1,0:T(8,128)(2,1)S(1)} %copy-done), channel_id=1, source_target_pairs={{0,8},{2,10},{4,12},{6,14},{1,9},{3,11},{5,13},{7,15},{8,0},{10,2}... | collective-permute-start | bytes 3145736 | tf_op jit(solution)/shard_map/ppermute | solution.py:257
  6.6 32.5 %collective-permute-start.11 = (bf16[1040,256]{1,0:T(8,128)(2,1)S(1)}, bf16[1040,256]{1,0:T(8,128)(2,1)S(1)}, u32[]{:S(2)}, u32[]{:S(2)}) collective-permute-start(bf16[1040,256]{1,0:T(8,128)(2,1)S(1)} %get-tuple-element.8), channel_id=1, source_target_pairs={{0,16},{10,26},{4,20},{14,30},{1,17},{11,27},{5,21},{15,31},{16,0}... | collective-permute-start | bytes 1597448 | tf_op jit(solution)/shard_map/ppermute | solution.py:257
  7.3 33.1 %collective-permute-start.4 = (bf16[1040,256]{1,0:T(8,128)(2,1)S(1)}, bf16[1040,256]{1,0:T(8,128)(2,1)S(1)}, u32[]{:S(2)}, u32[]{:S(2)}) collective-permute-start(bf16[1040,256]{1,0:T(8,128)(2,1)S(1)} %get-tuple-element.7.refs_0_), channel_id=1, source_target_pairs={{0,2},{1,3},{16,18},{17,19},{4,6},{5,7},{20,22},{21,23},{14,12},{1... | collective-permute-start | bytes 1597448 | tf_op jit(solution)/shard_map/ppermute | solution.py:257
  36.3 14.5 %collective-permute-start.2 = (bf16[1040,256]{1,0:T(8,128)(2,1)S(1)}, bf16[1040,256]{1,0:T(8,128)(2,1)S(1)}, u32[]{:S(2)}, u32[]{:S(2)}) collective-permute-start(bf16[1040,256]{1,0:T(8,128)(2,1)S(1)} %get-tuple-element.7.refs_0_), channel_id=1, source_target_pairs={{4,2},{5,3},{20,18},{21,19},{10,12},{11,13},{26,28},{27,29}} | collective-permute-start | bytes 1597448 | tf_op jit(solution)/shard_map/ppermute | solution.py:257
  37.6 15.3 %collective-permute-start.21 = (bf16[1040,256]{1,0:T(8,128)(2,1)S(1)}, bf16[1040,256]{1,0:T(8,128)(2,1)S(1)}, u32[]{:S(2)}, u32[]{:S(2)}) collective-permute-start(bf16[1040,256]{1,0:T(8,128)(2,1)S(1)} %get-tuple-element.7.refs_0_), channel_id=1, source_target_pairs={{0,1},{1,0},{16,17},{17,16},{10,11},{11,10},{26,27},{27,26},{4,5},... | collective-permute-start | bytes 1597448 | tf_op jit(solution)/shard_map/ppermute | solution.py:257
  38.3 0.8 copy-start.12
  39.1 17.7 %collective-permute-start.14 = (bf16[1040,256]{1,0:T(8,128)(2,1)S(1)}, bf16[1040,256]{1,0:T(8,128)(2,1)}, u32[]{:S(2)}, u32[]{:S(2)}) collective-permute-start(bf16[1040,256]{1,0:T(8,128)(2,1)S(1)} %collective-permute-done.11.refs_2_), channel_id=1, source_target_pairs={{0,2},{1,3},{16,18},{17,19},{4,6},{5,7},{20,22},{21,23},{14,12},{1... | collective-permute-start | bytes 1597448 | tf_op jit(solution)/shard_map/ppermute | solution.py:257
  40.4 19.5 %collective-permute-start.5 = (bf16[1040,256]{1,0:T(8,128)(2,1)S(1)}, bf16[1040,256]{1,0:T(8,128)(2,1)}, u32[]{:S(2)}, u32[]{:S(2)}) collective-permute-start(bf16[1040,256]{1,0:T(8,128)(2,1)S(1)} %collective-permute-done.4.refs_1_), channel_id=1, source_target_pairs={{2,4},{3,5},{18,20},{19,21},{12,10},{13,11},{28,26},{29,27}} | collective-permute-start | bytes 1597448 | tf_op jit(solution)/shard_map/ppermute | solution.py:257
  48.5 1.0 copy-start.1
  49.5 14.5 %collective-permute-start.12 = (bf16[1040,256]{1,0:T(8,128)(2,1)S(1)}, bf16[1040,256]{1,0:T(8,128)(2,1)}, u32[]{:S(2)}, u32[]{:S(2)}) collective-permute-start(bf16[1040,256]{1,0:T(8,128)(2,1)S(1)} %collective-permute-done.11.refs_2_), channel_id=1, source_target_pairs={{4,2},{5,3},{20,18},{21,19},{10,12},{11,13},{26,28},{27,29}} | collective-permute-start | bytes 1597448 | tf_op jit(solution)/shard_map/ppermute | solution.py:257
  50.8 16.2 %collective-permute-start.7 = (bf16[1040,256]{1,0:T(8,128)(2,1)S(1)}, bf16[1040,256]{1,0:T(8,128)(2,1)}, u32[]{:S(2)}, u32[]{:S(2)}) collective-permute-start(bf16[1040,256]{1,0:T(8,128)(2,1)S(1)} %collective-permute-done.2.refs_0_), channel_id=1, source_target_pairs={{2,0},{3,1},{18,16},{19,17},{12,14},{13,15},{28,30},{29,31}} | collective-permute-start | bytes 1597448 | tf_op jit(solution)/shard_map/ppermute | solution.py:257
  53.7 15.4 %collective-permute-start.22 = (bf16[1040,256]{1,0:T(8,128)(2,1)S(1)}, bf16[1040,256]{1,0:T(8,128)(2,1)S(1)}, u32[]{:S(2)}, u32[]{:S(2)}) collective-permute-start(bf16[1040,256]{1,0:T(8,128)(2,1)S(1)} %collective-permute-done.4.refs_1_), channel_id=1, source_target_pairs={{8,9},{9,8},{24,25},{25,24},{2,3},{3,2},{18,19},{19,18},{12,13},{1... | collective-permute-start | bytes 1597448 | tf_op jit(solution)/shard_map/ppermute | solution.py:257
  56.8 25.3 %collective-permute-start.27 = (bf16[2,512,512]{2,1,0:T(8,128)(2,1)S(1)}, bf16[2,512,512]{2,1,0:T(8,128)(2,1)S(1)}, u32[]{:S(2)}, u32[]{:S(2)}) collective-permute-start(bf16[2,512,512]{2,1,0:T(8,128)(2,1)S(1)} %collective-permute-done.26.refs_5_.refs_13_), channel_id=1, source_target_pairs={{0,8},{2,10},{4,12},{6,14},{1,9},{3,11},{5,13},{7,15},{8,0},{10,2}... | collective-permute-start | bytes 3145736 | tf_op jit(solution)/shard_map/ppermute | solution.py:257
  59.9 11.5 %collective-permute-start.23 = (bf16[1040,256]{1,0:T(8,128)(2,1)S(1)}, bf16[1040,256]{1,0:T(8,128)(2,1)S(1)}, u32[]{:S(2)}, u32[]{:S(2)}) collective-permute-start(bf16[1040,256]{1,0:T(8,128)(2,1)S(1)} %collective-permute-done.11.refs_2_), channel_id=1, source_target_pairs={{0,1},{1,0},{16,17},{17,16},{10,11},{11,10},{26,27},{27,26},{4,5},... | collective-permute-start | bytes 1597448 | tf_op jit(solution)/shard_map/ppermute | solution.py:257
  64.0 15.6 %collective-permute-start.3 = (bf16[1040,256]{1,0:T(8,128)(2,1)S(1)}, bf16[1040,256]{1,0:T(8,128)(2,1)S(1)}, u32[]{:S(2)}, u32[]{:S(2)}) collective-permute-start(bf16[1040,256]{1,0:T(8,128)(2,1)S(1)} %collective-permute-done.2.refs_0_), channel_id=1, source_target_pairs={{2,3},{3,2},{18,19},{19,18},{12,13},{13,12},{28,29},{29,28}} | collective-permute-start | bytes 1597448 | tf_op jit(solution)/shard_map/ppermute | solution.py:257
  66.2 0.8 copy-start.8
  67.0 17.5 %collective-permute-start.15 = (bf16[1040,256]{1,0:T(8,128)(2,1)}, bf16[1040,256]{1,0:T(8,128)(2,1)}, u32[]{:S(2)}, u32[]{:S(2)}) collective-permute-start(bf16[1040,256]{1,0:T(8,128)(2,1)} %collective-permute-done.14.refs_3_), channel_id=1, source_target_pairs={{2,4},{3,5},{18,20},{19,21},{12,10},{13,11},{28,26},{29,27}} | collective-permute-start | bytes 1597448 | tf_op jit(solution)/shard_map/ppermute | solution.py:257
  70.0 16.1 %collective-permute-start.9 = (bf16[1040,256]{1,0:T(8,128)(2,1)}, bf16[1040,256]{1,0:T(8,128)(2,1)}, u32[]{:S(2)}, u32[]{:S(2)}) collective-permute-start(bf16[1040,256]{1,0:T(8,128)(2,1)} %collective-permute-done.5.refs_1_), channel_id=1, source_target_pairs={{4,6},{5,7},{20,22},{21,23},{10,8},{11,9},{26,24},{27,25}} | collective-permute-start | bytes 1597448 | tf_op jit(solution)/shard_map/ppermute | solution.py:257
  72.2 22.6 %collective-permute-start.17 = (bf16[1040,256]{1,0:T(8,128)(2,1)}, bf16[1040,256]{1,0:T(8,128)(2,1)}, u32[]{:S(2)}, u32[]{:S(2)}) collective-permute-start(bf16[1040,256]{1,0:T(8,128)(2,1)} %collective-permute-done.12.refs_4_), channel_id=1, source_target_pairs={{2,0},{3,1},{18,16},{19,17},{12,14},{13,15},{28,30},{29,31}} | collective-permute-start | bytes 1597448 | tf_op jit(solution)/shard_map/ppermute | solution.py:257
  79.7 18.2 %collective-permute-start.24 = (bf16[1040,256]{1,0:T(8,128)(2,1)}, bf16[1040,256]{1,0:T(8,128)(2,1)}, u32[]{:S(2)}, u32[]{:S(2)}) collective-permute-start(bf16[1040,256]{1,0:T(8,128)(2,1)} %collective-permute-done.14.refs_3_), channel_id=1, source_target_pairs={{8,9},{9,8},{24,25},{25,24},{2,3},{3,2},{18,19},{19,18},{12,13},{1... | collective-permute-start | bytes 1597448 | tf_op jit(solution)/shard_map/ppermute | solution.py:257
  82.1 1.0 copy-start.3
  83.1 15.5 %collective-permute-start.6 = (bf16[1040,256]{1,0:T(8,128)(2,1)}, bf16[1040,256]{1,0:T(8,128)(2,1)}, u32[]{:S(2)}, u32[]{:S(2)}) collective-permute-start(bf16[1040,256]{1,0:T(8,128)(2,1)} %collective-permute-done.5.refs_1_), channel_id=1, source_target_pairs={{4,5},{5,4},{20,21},{21,20},{10,11},{11,10},{26,27},{27,26}} | collective-permute-start | bytes 1597448 | tf_op jit(solution)/shard_map/ppermute | solution.py:257
  84.6 14.7 %collective-permute-start.8 = (bf16[1040,256]{1,0:T(8,128)(2,1)}, bf16[1040,256]{1,0:T(8,128)(2,1)}, u32[]{:S(2)}, u32[]{:S(2)}) collective-permute-start(bf16[1040,256]{1,0:T(8,128)(2,1)} %collective-permute-done.7.refs_2_), channel_id=1, source_target_pairs={{0,1},{1,0},{16,17},{17,16},{14,15},{15,14},{30,31},{31,30}} | collective-permute-start | bytes 1597448 | tf_op jit(solution)/shard_map/ppermute | solution.py:257
  86.0 13.9 %collective-permute-start.19 = (bf16[1040,256]{1,0:T(8,128)(2,1)}, bf16[1040,256]{1,0:T(8,128)(2,1)}, u32[]{:S(2)}, u32[]{:S(2)}) collective-permute-start(bf16[1040,256]{1,0:T(8,128)(2,1)} %collective-permute-done.15.refs_5_), channel_id=1, source_target_pairs={{4,6},{5,7},{20,22},{21,23},{10,8},{11,9},{26,24},{27,25}} | collective-permute-start | bytes 1597448 | tf_op jit(solution)/shard_map/ppermute | solution.py:257
  87.7 1.0 copy-start.13
  88.7 1.0 copy-start.15
  89.8 1.0 copy-start.17
  90.8 9.9 %copy-start.11 = (bf16[1040,256]{1,0:T(8,128)(2,1)S(1)}, bf16[1040,256]{1,0:T(8,128)(2,1)}, u32[]{:S(2)}) copy-start(bf16[1040,256]{1,0:T(8,128)(2,1)} %copy-done.10) | copy-start | bytes 1597444
  90.8 9.9 %copy-start.19 = (bf16[1040,256]{1,0:T(8,128)(2,1)S(1)}, bf16[1040,256]{1,0:T(8,128)(2,1)}, u32[]{:S(2)}) copy-start(bf16[1040,256]{1,0:T(8,128)(2,1)} %copy-done.18) | copy-start | bytes 1597444
  90.8 9.9 %copy-start.21 = (bf16[1040,256]{1,0:T(8,128)(2,1)S(1)}, bf16[1040,256]{1,0:T(8,128)(2,1)}, u32[]{:S(2)}) copy-start(bf16[1040,256]{1,0:T(8,128)(2,1)} %copy-done.20) | copy-start | bytes 1597444
  94.8 9.9 %copy-start.9 = (bf16[1040,256]{1,0:T(8,128)(2,1)S(1)}, bf16[1040,256]{1,0:T(8,128)(2,1)}, u32[]{:S(2)}) copy-start(bf16[1040,256]{1,0:T(8,128)(2,1)} %copy-done.8) | copy-start | bytes 1597444
  94.8 17.4 %collective-permute-start.13 = (bf16[1040,256]{1,0:T(8,128)(2,1)}, bf16[1040,256]{1,0:T(8,128)(2,1)S(1)}, u32[]{:S(2)}, u32[]{:S(2)}) collective-permute-start(bf16[1040,256]{1,0:T(8,128)(2,1)} %collective-permute-done.12.refs_4_), channel_id=1, source_target_pairs={{2,3},{3,2},{18,19},{19,18},{12,13},{13,12},{28,29},{29,28}} | collective-permute-start | bytes 1597448 | tf_op jit(solution)/shard_map/ppermute | solution.py:257
  97.8 14.5 %collective-permute-start.16 = (bf16[1040,256]{1,0:T(8,128)(2,1)}, bf16[1040,256]{1,0:T(8,128)(2,1)S(1)}, u32[]{:S(2)}, u32[]{:S(2)}) collective-permute-start(bf16[1040,256]{1,0:T(8,128)(2,1)} %collective-permute-done.15.refs_5_), channel_id=1, source_target_pairs={{4,5},{5,4},{20,21},{21,20},{10,11},{11,10},{26,27},{27,26}} | collective-permute-start | bytes 1597448 | tf_op jit(solution)/shard_map/ppermute | solution.py:257
  98.6 13.7 %collective-permute-start.10 = (bf16[1040,256]{1,0:T(8,128)(2,1)}, bf16[1040,256]{1,0:T(8,128)(2,1)S(1)}, u32[]{:S(2)}, u32[]{:S(2)}) collective-permute-start(bf16[1040,256]{1,0:T(8,128)(2,1)} %collective-permute-done.9.refs_3_), channel_id=1, source_target_pairs={{6,7},{7,6},{22,23},{23,22},{8,9},{9,8},{24,25},{25,24}} | collective-permute-start | bytes 1597448 | tf_op jit(solution)/shard_map/ppermute | solution.py:257
  99.3 13.0 %collective-permute-start.18 = (bf16[1040,256]{1,0:T(8,128)(2,1)}, bf16[1040,256]{1,0:T(8,128)(2,1)S(1)}, u32[]{:S(2)}, u32[]{:S(2)}) collective-permute-start(bf16[1040,256]{1,0:T(8,128)(2,1)} %collective-permute-done.17.refs_6_), channel_id=1, source_target_pairs={{0,1},{1,0},{16,17},{17,16},{14,15},{15,14},{30,31},{31,30}} | collective-permute-start | bytes 1597448 | tf_op jit(solution)/shard_map/ppermute | solution.py:257
  100.0 12.3 %collective-permute-start.20 = (bf16[1040,256]{1,0:T(8,128)(2,1)}, bf16[1040,256]{1,0:T(8,128)(2,1)S(1)}, u32[]{:S(2)}, u32[]{:S(2)}) collective-permute-start(bf16[1040,256]{1,0:T(8,128)(2,1)} %collective-permute-done.19.refs_7_), channel_id=1, source_target_pairs={{6,7},{7,6},{22,23},{23,22},{8,9},{9,8},{24,25},{25,24}} | collective-permute-start | bytes 1597448 | tf_op jit(solution)/shard_map/ppermute | solution.py:257
  104.7 4.0 %copy-start.2 = (bf16[2,512,512]{2,1,0:T(8,128)(2,1)S(1)}, bf16[2,512,512]{2,1,0:T(8,128)(2,1)}, u32[]{:S(2)}) copy-start(bf16[2,512,512]{2,1,0:T(8,128)(2,1)} %copy-done.1) | copy-start | bytes 3145732
  104.7 4.0 %copy-start.4 = (bf16[2,512,512]{2,1,0:T(8,128)(2,1)S(1)}, bf16[2,512,512]{2,1,0:T(8,128)(2,1)}, u32[]{:S(2)}) copy-start(bf16[2,512,512]{2,1,0:T(8,128)(2,1)} %copy-done.3) | copy-start | bytes 3145732
  108.8 3.5 %copy-start.6 = (bf16[2,2,128,512]{3,2,1,0:T(8,128)(2,1)S(1)}, bf16[2,2,128,512]{3,2,1,0:T(8,128)(2,1)}, u32[]{:S(2)}) copy-start(bf16[2,2,128,512]{3,2,1,0:T(8,128)(2,1)} %copy-done.5) | copy-start | bytes 1572868
  116.8 5.6 %collective-permute-start.29 = (f32[512]{0:T(512)S(1)}, f32[512]{0:T(512)S(1)}, u32[]{:S(2)}, u32[]{:S(2)}) collective-permute-start(f32[512]{0:T(512)S(1)} %bitcast.23), channel_id=1, source_target_pairs={{0,8},{2,10},{4,12},{6,14},{1,9},{3,11},{5,13},{7,15},{8,0},{10,2}... | collective-permute-start | bytes 6152 | tf_op jit(solution)/shard_map/ppermute | solution.py:257
  120.7 2.5 %collective-permute-start.30 = (f32[512]{0:T(512)S(1)}, f32[512]{0:T(512)S(1)}, u32[]{:S(2)}, u32[]{:S(2)}) collective-permute-start(f32[512]{0:T(512)S(1)} %bitcast.24), channel_id=1, source_target_pairs={{0,16},{2,18},{4,20},{6,22},{1,17},{3,19},{5,21},{7,23},{8,24},{10... | collective-permute-start | bytes 6152 | tf_op jit(solution)/shard_map/ppermute | solution.py:257
  122.0 3.0 %collective-permute-start.31 = (f32[512]{0:T(512)S(1)}, f32[512]{0:T(512)S(1)}, u32[]{:S(2)}, u32[]{:S(2)}) collective-permute-start(f32[512]{0:T(512)S(1)} %bitcast.25), channel_id=1, source_target_pairs={{0,24},{2,26},{4,28},{6,30},{1,25},{3,27},{5,29},{7,31},{8,16},{10... | collective-permute-start | bytes 6152 | tf_op jit(solution)/shard_map/ppermute | solution.py:257
  (6 other events, 4.8 us)

commit v2 on v1

v2 whole, which is shorter than its diff:
```python
import functools

import jax
import jax.numpy as jnp
import numpy as np
from jax import lax
from jax.experimental import pallas as pl
from jax.experimental.pallas import tpu as pltpu
from jax.sharding import PartitionSpec as P

AXES = ("slab", "src")
PAD = 16
TILE = 256
VMEM_LIMIT = 24 * 1024 * 1024


def params():
    return pltpu.CompilerParams(vmem_limit_bytes=VMEM_LIMIT)


def light():
    return pl.CostEstimate(flops=1000, bytes_accessed=1000, transcendentals=0)


SMEM_SPEC = pl.BlockSpec(memory_space=pltpu.SMEM)
VMEM_SPEC = pl.BlockSpec(memory_space=pltpu.VMEM)


def number(x, c, y, z, n_src):
    return (2 * x + c) * n_src + 2 * z + y


def id_rows(trace_owner, trace_source, sources_here):
    per = sources_here // TILE
    ids = trace_source[0]
    high = trace_owner[0, :, 0] * per + ids // TILE
    rows = jnp.stack([high, ids % TILE])
    return jnp.pad(rows, ((0, PAD - 2), (0, 0))).astype(jnp.bfloat16)


def id_block(ids, kinds):
    pieces = [
        rows[kind : kind + 1, j * TILE : (j + 1) * TILE]
        for kind in kinds
        for rows in ids
        for j in range(rows.shape[1] // TILE)
    ]
    pad = jnp.zeros((PAD - len(pieces), TILE), jnp.bfloat16)
    return jnp.concatenate(pieces + [pad], axis=0)


def receivers(values, first, rows, out_ref, spot):
    quarter = values.shape[1] // 4
    for part in range(2):
        low = values[:, 2 * part * quarter : (2 * part + 1) * quarter]
        high = values[:, (2 * part + 1) * quarter : (2 * part + 2) * quarter]
        lanes = pl.ds(part * quarter, quarter)
        out_ref[pl.ds(spot, rows), lanes] = jnp.where(first, low, high)


def cut_kernel(n, place, *refs):
    values, ids, out_ref = refs[:n], refs[n : 2 * n], refs[2 * n]
    rows = values[0].shape[0]
    for k, ref in enumerate(values):
        receivers(ref, place[0] == 0, rows, out_ref, k * rows)
    out_ref[n * rows :, :] = id_block(ids, range(2))


def cut(half, values, ids):
    rows, width = values[0].shape
    n = len(values)
    return pl.pallas_call(
        functools.partial(cut_kernel, n),
        name="cut",
        out_shape=jax.ShapeDtypeStruct((n * rows + PAD, width // 2), jnp.bfloat16),
        in_specs=[SMEM_SPEC] + [VMEM_SPEC] * (2 * n),
        out_specs=VMEM_SPEC,
        compiler_params=params(),
        cost_estimate=light(),
    )(half, *values, *ids)


def pick_kernel(n, place, *refs):
    fetch(place[0], refs[:n], refs[n], refs[n + 1])


def pick(which, candidates):
    first = candidates[0]
    return pl.pallas_call(
        functools.partial(pick_kernel, len(candidates)),
        name="pick",
        out_shape=jax.ShapeDtypeStruct(first.shape, first.dtype),
        in_specs=[SMEM_SPEC] + [VMEM_SPEC] * len(candidates),
        out_specs=VMEM_SPEC,
        scratch_shapes=[pltpu.SemaphoreType.DMA],
        compiler_params=params(),
        cost_estimate=light(),
    )(which, *candidates)


def join_kernel(mine, other, out_ref):
    rows = mine.shape[0] - PAD
    tiles = rows // TILE
    out_ref[:rows, :] = mine[:rows, :]
    out_ref[rows : 2 * rows, :] = other[:rows, :]
    ids = [mine[rows:, :], other[rows:, :]]
    pieces = [part[kind * tiles : (kind + 1) * tiles] for kind in range(2) for part in ids]
    pad = jnp.zeros((PAD - 4 * tiles, TILE), jnp.bfloat16)
    out_ref[2 * rows :, :] = jnp.concatenate(pieces + [pad], axis=0)


def join(mine, other):
    rows, width = mine.shape
    return pl.pallas_call(
        join_kernel,
        name="join",
        out_shape=jax.ShapeDtypeStruct((2 * rows - PAD, width), jnp.bfloat16),
        in_specs=[VMEM_SPEC] * 2,
        out_specs=VMEM_SPEC,
        compiler_params=params(),
        cost_estimate=light(),
    )(mine, other)


def halves_kernel(place, blocks, near_ref, away_ref):
    first = place[0] == 0
    for p in range(blocks.shape[0]):
        for line in range(blocks.shape[1]):
            low, high = blocks[p, line, 0], blocks[p, line, 1]
            near_ref[p, line] = jnp.where(first, low, high)
            away_ref[p, line] = jnp.where(first, high, low)


def halves(place, blocks):
    shape = jax.ShapeDtypeStruct(blocks.shape[:2] + blocks.shape[3:], blocks.dtype)
    return pl.pallas_call(
        halves_kernel,
        name="halves",
        out_shape=(shape, shape),
        in_specs=[SMEM_SPEC, VMEM_SPEC],
        out_specs=(VMEM_SPEC, VMEM_SPEC),
        compiler_params=params(),
        cost_estimate=light(),
    )(place, blocks)


def fetch(which, candidates, target, sem):
    for k, ref in enumerate(candidates):

        @pl.when(which == k)
        def _(ref=ref):
            copy = pltpu.make_async_copy(ref, target, sem)
            copy.start()
            copy.wait()


def assemble(slab, pieces, group, start=None):
    traces = pieces[0].shape[0] - PAD
    tiles = traces // TILE
    iota = lax.broadcasted_iota(jnp.int32, (TILE, TILE), 0).astype(jnp.bfloat16)
    out = []
    owner = slab ^ group
    per = 2
    for h in range(per):
        name = (owner * per + h).astype(jnp.float32).astype(jnp.bfloat16)
        total = None if start is None else start[h * TILE : (h + 1) * TILE, :]
        for piece in pieces:
            masks = []
            for j in range(tiles):
                high = piece[traces + j : traces + j + 1, :]
                low = piece[traces + tiles + j : traces + tiles + j + 1, :]
                wanted = jnp.where(high == name, low, jnp.bfloat16(-1.0))
                masks.append(
                    jnp.where(iota == wanted, jnp.bfloat16(1.0), jnp.bfloat16(0.0))
                )
            mask = jnp.concatenate(masks, axis=1)
            term = jnp.dot(
                mask, piece[:traces, :], preferred_element_type=jnp.float32
            )
            total = term if total is None else total + term
        out.append(total)
    return jnp.concatenate(out, axis=0)


def residual_kernel(n, place, *refs):
    out_ref = refs[n]
    rows = out_ref.shape[0] // 4
    for group in range(4):
        out_ref[group * rows : (group + 1) * rows, :] = assemble(
            place[0], refs[:n], group
        ).astype(out_ref.dtype)


def residual(place, pieces, sources, dtype=jnp.bfloat16):
    return pl.pallas_call(
        functools.partial(residual_kernel, len(pieces)),
        name="residual",
        out_shape=jax.ShapeDtypeStruct((sources, pieces[0].shape[1]), dtype),
        in_specs=[SMEM_SPEC] + [VMEM_SPEC] * len(pieces),
        out_specs=VMEM_SPEC,
        compiler_params=params(),
        cost_estimate=light(),
    )(place, *pieces)


def correlate(res, fields):
    contract = (((0,), (0,)), ((), ()))
    dot = functools.partial(
        lax.dot_general,
        dimension_numbers=contract,
        preferred_element_type=jnp.float32,
    )
    half = res[0].shape[1] // 2
    real, imag = None, None
    for piece, field in zip(res, fields):
        with_real, with_imag = dot(piece, field[0]), dot(piece, field[1])
        first = with_real[:half] + with_imag[half:]
        second = with_real[half:] - with_imag[:half]
        real = first if real is None else real + first
        imag = second if imag is None else imag + second
    return real, imag


def correlate_kernel(n_res, *refs):
    res, out_ref = refs[:n_res], refs[-1]
    fields = refs[n_res:-1]
    rows = res[0].shape[0] // 4
    for k, ref in enumerate(res):
        parts = [ref[g * rows : (g + 1) * rows, :] for g in range(4)]
        real, imag = correlate(parts, fields)
        out_ref[k, 0] = real
        out_ref[k, 1] = imag


def correlated(res, fields):
    half, cells = res[0].shape[1] // 2, fields[0].shape[2]
    return pl.pallas_call(
        functools.partial(correlate_kernel, len(res)),
        name="correlate",
        out_shape=jax.ShapeDtypeStruct((len(res), 2, half, cells), jnp.float32),
        in_specs=[VMEM_SPEC] * (len(res) + len(fields)),
        out_specs=VMEM_SPEC,
        compiler_params=params(),
        cost_estimate=light(),
    )(*res, *fields)


def fetch_green(place, slot, greens, target, sems):
    group, line = place[1 + 2 * slot], place[2 + 2 * slot]
    for j, ref in enumerate(greens):

        @pl.when(group == j)
        def _(ref=ref):
            for p in range(2):
                pltpu.make_async_copy(ref.at[p, line], target.at[p], sems.at[p]).start()

    def wait():
        for p in range(2):
            pltpu.make_async_copy(greens[0].at[p, 0], target.at[p], sems.at[p]).wait()

    return wait


def fold_kernel(place, factors, *refs):
    greens, (out_ref, green, sems) = refs[:4], refs[4:]
    slots = factors.shape[0]
    waits = [
        fetch_green(place, k, greens, green.at[k], sems.at[k]) for k in range(slots)
    ]
    total = None
    for k in range(slots):
        waits[k]()
        for p in range(2):
            term = green[k, p].astype(jnp.float32) * factors[k, p]
            total = term if total is None else total + term
    out_ref[...] = jnp.sum(total, axis=0, keepdims=True)


def fold(place, factors, greens):
    slots = factors.shape[0]
    return pl.pallas_call(
        fold_kernel,
        name="fold",
        out_shape=jax.ShapeDtypeStruct((1, factors.shape[3]), jnp.float32),
        in_specs=[SMEM_SPEC] + [VMEM_SPEC] * (1 + len(greens)),
        out_specs=VMEM_SPEC,
        scratch_shapes=[
            pltpu.VMEM((slots, 2) + greens[0].shape[2:], jnp.bfloat16),
            pltpu.SemaphoreType.DMA((slots, 2)),
        ],
        compiler_params=params(),
        cost_estimate=light(),
    )(place, factors, *greens)


def last_kernel(n_b, place, *refs):
    cand_b, (begun, folded) = refs[:n_b], refs[n_b : n_b + 2]
    greens, fields = refs[n_b + 2 : n_b + 6], refs[n_b + 6 : n_b + 10]
    out_ref, piece, green, sem, sems = refs[n_b + 10 :]
    wait = fetch_green(place, 3, greens, green, sems)
    fetch(place[9], cand_b, piece, sem)
    rows = begun.shape[0] // 4
    parts = [
        assemble(
            place[0], (piece,), g, begun[g * rows : (g + 1) * rows, :]
        ).astype(jnp.bfloat16)
        for g in range(4)
    ]
    real, imag = correlate(parts, fields)
    wait()
    total = green[0].astype(jnp.float32) * real + green[1].astype(jnp.float32) * imag
    out_ref[...] = folded[...] + jnp.sum(total, axis=0, keepdims=True)


def last(place, cand_b, begun, folded, greens, fields):
    return pl.pallas_call(
        functools.partial(last_kernel, len(cand_b)),
        name="last",
        out_shape=jax.ShapeDtypeStruct(folded.shape, jnp.float32),
        in_specs=[SMEM_SPEC]
        + [VMEM_SPEC] * (len(cand_b) + 2 + len(greens) + len(fields)),
        out_specs=VMEM_SPEC,
        scratch_shapes=[
            pltpu.VMEM(cand_b[0].shape, jnp.bfloat16),
            pltpu.VMEM((2,) + greens[0].shape[2:], jnp.bfloat16),
            pltpu.SemaphoreType.DMA,
            pltpu.SemaphoreType.DMA((2,)),
        ],
        compiler_params=params(),
        cost_estimate=light(),
    )(place, *cand_b, begun, folded, *greens, *fields)


def paired(n_src, trace_values, trace_owner, trace_source, source_fields, green_fields):
    values = trace_values[0]
    sources_here = source_fields.shape[1]
    slab = lax.axis_index("slab")
    src = lax.axis_index("src")
    x, c = slab // 2, slab % 2
    z, y = src // 2, src % 2
    lines = range(n_src // 2)

    def send(array, moves):
        pairs = [
            (number(*a, n_src), number(*b, n_src)) for a, b in moves
        ]
        return lax.ppermute(array, AXES, pairs)

    everywhere = [
        (a, b, d, e) for a in range(2) for b in range(2) for d in range(2) for e in lines
    ]
    to_core = [((a, b, d, e), (a, 1 - b, d, e)) for a, b, d, e in everywhere]
    to_x = [((a, b, d, e), (1 - a, b, d, e)) for a, b, d, e in everywhere]
    to_both = [((a, b, d, e), (1 - a, 1 - b, d, e)) for a, b, d, e in everywhere]

    def after(array, *earlier):
        return lax.optimization_barrier((array, *earlier))[0]

    other = send(values, to_core)
    mine_ids = id_rows(trace_owner, trace_source, sources_here)
    other_ids = send(mine_ids, to_core)
    place_x = jnp.stack([x]).astype(jnp.int32)
    crossed_here = send(cut(1 - place_x, (values,), (mine_ids,)), to_x)
    own = cut(place_x, (values, other), (mine_ids, other_ids))
    crossed = join(crossed_here, send(crossed_here, to_core))

    moves = []
    for steps in (
        [(0, 0, 1, None), (1, 0, 0, 1), (0, 1, 0, 0), (1, 1, 1, 2)],
        [(0, 0, 1, None), (1, 1, 0, 0), (0, 1, 0, 2)],
        [(0, 0, 1, None), (1, 0, 0, 1), (0, 1, 0, 0), (1, 1, 1, None)],
        [(0, 0, 1, None), (1, 0, 0, 1), (0, 1, 1, None)],
    ):
        pairs = []
        for here_c, here_z, there_c, there_z in steps:
            for a in range(2):
                for d in range(2):
                    for e in (here_z, len(lines) - 1 - here_z):
                        if there_z is None:
                            target = (a, there_c, 1 - d, e)
                        else:
                            far_z = there_z if e == here_z else len(lines) - 1 - there_z
                            target = (a, there_c, d, far_z)
                        pairs.append(((a, here_c, d, e), target))
        moves.append(pairs)
    brought = np.array(
        [
            [[(1, 0), (2, 0), (3, 0), (0, 0)], [(0, 1), (1, 1), (2, 1), (3, 1)]],
            [[(0, 0), (3, 0), (0, 1), (1, 1)], [(2, 0), (1, 0), (2, 1), (3, 1)]],
        ],
        np.int32,
    )
    mirrored = brought[::-1].copy()
    mirrored[..., 0] = len(lines) - 1 - mirrored[..., 0]
    table = jnp.asarray(np.concatenate([brought, mirrored]))
    outer = (z == 0) | (z == len(lines) - 1)

    mine_now = lax.dynamic_index_in_dim(
        lax.dynamic_index_in_dim(table, z, 0, keepdims=False), c, 0, keepdims=False
    )
    groups = jnp.bitwise_xor(mine_now[:, 0], slab)
    on_line = jnp.bitwise_xor(mine_now[:, 1], y)
    where_green = jnp.stack([groups, on_line], axis=1).reshape(-1)
    stay_2 = jnp.where((~outer) & (c == 1), 1, 0)
    stay_4 = jnp.where(outer & (c == 0), 1, 0)
    place = jnp.concatenate(
        [jnp.stack([slab]), where_green, jnp.stack([stay_4])]
    ).astype(jnp.int32)
    stay_2, stay_4 = (jnp.stack([k]).astype(jnp.int32) for k in (stay_2, stay_4))
    core = jnp.stack([c]).astype(jnp.int32)
    sources = 4 * sources_here

    r1_a = send(own, moves[0])
    r2_a = send(r1_a, moves[1])
    r1_b = send(after(crossed, r1_a), moves[0])
    r3_a = send(pick(core, (r2_a, r1_a)), moves[2])
    r2_b = send(after(r1_b, r2_a), moves[1])
    res_1 = residual(place, (r1_a, after(r1_b, r2_a)), sources)
    r4_a = send(pick(1 - stay_4, (after(r3_a, res_1), r2_a)), moves[3])
    to_r3_b = pick(core, (after(r2_b, r3_a), r1_b))
    r3_b = send(to_r3_b, moves[2])
    second_a, second_b = pick(stay_2, (r2_a, own)), pick(stay_2, (r2_b, crossed))
    res_2 = residual(place, (second_a, after(second_b, to_r3_b)), sources)
    fourth_a = pick(stay_4, (after(r4_a, res_2), own))
    to_r4_b = pick(1 - stay_4, (after(r3_b, fourth_a), r2_b))
    r4_b = send(to_r4_b, moves[3])

    field_core = send(after(source_fields, own), to_core)
    field_x = send(after(source_fields, crossed_here), to_x)
    field_far = send(after(field_x, to_r3_b), to_core)
    fields = (source_fields, field_core, field_x, field_far)

    blocks = green_fields.reshape(2, 2, 2, -1, green_fields.shape[2])
    near, away_green = halves(place_x, after(blocks, r1_a))
    far = send(after(away_green, r2_a), to_x)
    far_core = send(after(far, to_r4_b), to_core)
    greens = (near, send(near, to_core), far, far_core)

    res_3 = residual(place, (r3_a, after(r3_b, to_r4_b)), sources)
    factors = correlated((res_1, res_2, res_3), fields)
    begun = residual(place, (fourth_a,), sources, jnp.float32)
    folded = fold(place, factors, greens)
    partial = last(place, (r4_b, crossed), begun, folded, greens, fields)[0]
    here = partial + send(partial, to_core)
    there = send(partial, to_x) + send(partial, to_both)
    return here + there


def gathered(trace_values, trace_owner, trace_source, source_fields, green_fields):
    values = trace_values[0]
    half_width = values.shape[1] // 2
    src_count = lax.axis_size("src")
    sources_here = source_fields.shape[1]
    slab_index = lax.axis_index("slab")
    high = trace_owner[0, :, 0] * (sources_here // 32) + trace_source[0] // 32
    low = trace_source[0] % 32
    per_slab = sources_here // 32
    piece_values = lax.all_gather(values, "slab", axis=0, tiled=True)
    owners = trace_owner[0, :, 0].astype(jnp.bfloat16)
    high_part = (trace_source[0] // 32).astype(jnp.bfloat16)
    low_part = low.astype(jnp.bfloat16)
    piece_ids = lax.all_gather(
        jnp.stack([owners, high_part, low_part]), "slab", axis=1, tiled=True
    )
    ids = jnp.arange(sources_here, dtype=jnp.int32)
    picks = (
        ((ids // 32).astype(jnp.bfloat16)[:, None] == piece_ids[1][None, :])
        & ((ids % 32).astype(jnp.bfloat16)[:, None] == piece_ids[2][None, :])
        & (piece_ids[0][None, :] == slab_index.astype(jnp.bfloat16))
    )
    assembled = jnp.dot(
        picks.astype(jnp.bfloat16), piece_values, preferred_element_type=jnp.float32
    )
    rows = lax.all_gather(assembled.astype(jnp.bfloat16), "src", axis=1, tiled=True)
    split_rows = rows.reshape(sources_here, src_count, 2, half_width)
    res_real = split_rows[:, :, 0, :].reshape(sources_here, src_count * half_width)
    res_imag = split_rows[:, :, 1, :].reshape(sources_here, src_count * half_width)
    green = lax.all_gather(green_fields, "slab", axis=1, tiled=True)
    dot = functools.partial(jnp.dot, preferred_element_type=jnp.float32)
    adj_real = dot(res_real, green[0]) + dot(res_imag, green[1])
    adj_imag = dot(res_real, green[1]) - dot(res_imag, green[0])
    partial = jnp.sum(
        source_fields[0].astype(jnp.float32) * adj_real
        - source_fields[1].astype(jnp.float32) * adj_imag,
        axis=0,
    )
    return lax.psum(partial, "slab")


def solution(mesh):
    in_specs = (
        P("src", "slab", None),
        P("src", "slab", None),
        P("src", "slab"),
        P(None, "slab", "src"),
        P(None, "slab", "src"),
    )
    n_slab, n_src = mesh.shape["slab"], mesh.shape["src"]
    if n_slab == 2 * 2 and n_src == 2 * 4:
        on_device = functools.partial(paired, n_src)
    else:
        on_device = gathered
    return jax.shard_map(
        on_device, mesh=mesh, in_specs=in_specs, out_specs=P("src"), check_vma=False
    )
```

time: 126 us -> 95.4 us (0.76)
  the two profiles are of different devices: /device:TPU:17 before, /device:TPU:0 now
where the time goes in v2:
time: 95.4 us; the launch traced here: 94.3 us
  Pallas kernels  32.5 us (34%)
  waiting for transfers between devices  30.2 us (32%)
  starting transfers between devices  22.3 us (23%)
  local copies, waits for them, and re-layouts  7.64 us (8%)
  other arithmetic  1.42 us (1%)
    ppermute x21, waiting for transfers between devices, send(): return lax.ppermute(array, AXES, pairs)  30.2 us
    ppermute x21, starting transfers between devices, send(): return lax.ppermute(array, AXES, pairs)  22.3 us
    pallas_call x4, Pallas kernels, residual(): pl.pallas_call(functools.partial(residual_kernel, len(pieces)), name='res...  11.6 us
    pallas_call x7, Pallas kernels, pick(): pl.pallas_call(functools.partial(pick_kernel, len(candidates)), name='pic...  7.03 us
    unnamed x22, local copies, waits for them, and re-layouts  6.77 us
    pallas_call x1, Pallas kernels, correlated(): pl.pallas_call(functools.partial(correlate_kernel, len(res)), name='corre...  5.33 us
    pallas_call x1, Pallas kernels, last(): pl.pallas_call(functools.partial(last_kernel, len(cand_b)), name='last',...  4.94 us
    pallas_call x1, Pallas kernels, fold(): pl.pallas_call(fold_kernel, name='fold', out_shape=jax.ShapeDtypeStruct((...  2.46 us
  transfers between devices with their start and end apart: 21, of which 9 were waited for; matrix products, arithmetic and copies ran while one was open for 2% of the time, Pallas kernels for 29%

profile of v2, /device:TPU:0, one launch (start us, length us, event | category | flops | bytes accessed | tf_op | source)
XLA Modules:
  0.0 94.3 jit_solution(4721563032301935982)
XLA Ops:
  0.0 0.5 collective-permute-start.2
  0.5 0.7 fusion.4
  1.2 0.2 collective-permute-start.3
  1.4 1.0 %copy-done.8 = bf16[1,512,512]{2,1,0:T(8,128)(2,1)S(1)} copy-done((bf16[1,512,512]{2,1,0:T(8,128)(2,1)S(1)}, bf16[1,512,512]{2,1,0:T(8,128)(2,1)}, u32[]{:S(2)}) %copy-start.8) | copy-done | bytes 524312
  2.5 2.9 %collective-permute-start = (bf16[528,256]{1,0:T(8,128)(2,1)S(1)}, bf16[528,256]{1,0:T(8,128)(2,1)S(1)}, u32[]{:S(2)}, u32[]{:S(2)}) collective-permute-start(bf16[528,256]{1,0:T(8,128)(2,1)S(1)} %cut.2), channel_id=1, source_target_pairs={{0,16},{2,18},{4,20},{6,22},{1,17},{3,19},{5,21},{7,23},{8,24},{10... | collective-permute-start | bytes 811016 | tf_op jit(solution)/shard_map/ppermute | solution.py:347
  5.5 1.0 %copy-done.9 = bf16[1,512,512]{2,1,0:T(8,128)(2,1)S(1)} copy-done((bf16[1,512,512]{2,1,0:T(8,128)(2,1)S(1)}, bf16[1,512,512]{2,1,0:T(8,128)(2,1)}, u32[]{:S(2)}) %copy-start.9) | copy-done | bytes 524312
  6.5 0.1 cut.3.refs_1_
  6.6 1.0 %collective-permute-start.4 = (bf16[1040,256]{1,0:T(8,128)(2,1)S(1)}, bf16[1040,256]{1,0:T(8,128)(2,1)S(1)}, u32[]{:S(2)}, u32[]{:S(2)}) collective-permute-start(bf16[1040,256]{1,0:T(8,128)(2,1)S(1)} %cut.3.refs_1_), channel_id=1, source_target_pairs={{0,9},{6,15},{1,8},{7,14},{16,25},{22,31},{17,24},{23,30},{8,2},{1... | collective-permute-start | bytes 1597448 | tf_op jit(solution)/shard_map/ppermute | solution.py:347
  7.6 4.5 %collective-permute-done.mine = bf16[528,256]{1,0:T(8,128)(2,1)S(1)} collective-permute-done((bf16[528,256]{1,0:T(8,128)(2,1)S(1)}, bf16[528,256]{1,0:T(8,128)(2,1)S(1)}, u32[]{:S(2)}, u32[]{:S(2)}) %collective-permute-start) | collective-permute-done | bytes 270368 | tf_op jit(solution)/shard_map/ppermute | solution.py:347
  12.2 1.5 %collective-permute-done.1.other = bf16[528,256]{1,0:T(8,128)(2,1)S(1)} collective-permute-done((bf16[528,256]{1,0:T(8,128)(2,1)S(1)}, bf16[528,256]{1,0:T(8,128)(2,1)S(1)}, u32[]{:S(2)}, u32[]{:S(2)}) %collective-permute-start.1) | collective-permute-done | bytes 270368 | tf_op jit(solution)/shard_map/ppermute | solution.py:347
  13.8 2.2 %collective-permute-done.4.refs_1_.refs_0_ = bf16[1040,256]{1,0:T(8,128)(2,1)S(1)} collective-permute-done((bf16[1040,256]{1,0:T(8,128)(2,1)S(1)}, bf16[1040,256]{1,0:T(8,128)(2,1)S(1)}, u32[]{:S(2)}, u32[]{:S(2)}) %collective-permute-start.4) | collective-permute-done | bytes 532512 | tf_op jit(solution)/shard_map/ppermute | solution.py:347
  16.0 0.7 collective-permute-start.5
  16.6 3.5 %collective-permute-start.6 = (bf16[1040,256]{1,0:T(8,128)(2,1)S(1)}, bf16[1040,256]{1,0:T(8,128)(2,1)S(1)}, u32[]{:S(2)}, u32[]{:S(2)}) collective-permute-start(bf16[1040,256]{1,0:T(8,128)(2,1)S(1)} %collective-permute-done.4.refs_1_.refs_0_), channel_id=1, source_target_pairs={{0,9},{6,15},{1,8},{7,14},{16,25},{22,31},{17,24},{23,30},{10,0},{... | collective-permute-start | bytes 1597448 | tf_op jit(solution)/shard_map/ppermute | solution.py:347
  20.1 0.8 copy-done.3
  20.9 0.5 collective-permute-start.13
  21.5 7.6 %collective-permute-done.5.refs_1_ = bf16[1040,256]{1,0:T(8,128)(2,1)} collective-permute-done((bf16[1040,256]{1,0:T(8,128)(2,1)S(1)}, bf16[1040,256]{1,0:T(8,128)(2,1)}, u32[]{:S(2)}, u32[]{:S(2)}) %collective-permute-start.5) | collective-permute-done | bytes 532512 | tf_op jit(solution)/shard_map/ppermute | solution.py:347
  29.0 1.9 %collective-permute-done.6.refs_0_.refs_1_ = bf16[1040,256]{1,0:T(8,128)(2,1)S(1)} collective-permute-done((bf16[1040,256]{1,0:T(8,128)(2,1)S(1)}, bf16[1040,256]{1,0:T(8,128)(2,1)S(1)}, u32[]{:S(2)}, u32[]{:S(2)}) %collective-permute-start.6) | collective-permute-done | bytes 532512 | tf_op jit(solution)/shard_map/ppermute | solution.py:347
  30.9 2.4 %collective-permute-start.7 = (bf16[1040,256]{1,0:T(8,128)(2,1)}, bf16[1040,256]{1,0:T(8,128)(2,1)S(1)}, u32[]{:S(2)}, u32[]{:S(2)}) collective-permute-start(bf16[1040,256]{1,0:T(8,128)(2,1)} %collective-permute-done.5.refs_1_), channel_id=1, source_target_pairs={{0,9},{6,15},{1,8},{7,14},{16,25},{22,31},{17,24},{23,30},{10,0},{... | collective-permute-start | bytes 1597448 | tf_op jit(solution)/shard_map/ppermute | solution.py:347
  33.3 1.0 %copy-done.4 = bf16[1040,256]{1,0:T(8,128)(2,1)S(1)} copy-done((bf16[1040,256]{1,0:T(8,128)(2,1)S(1)}, bf16[1040,256]{1,0:T(8,128)(2,1)}, u32[]{:S(2)}) %copy-start.4) | copy-done | bytes 532504
  34.4 0.8 pick.7
  35.3 0.7 dynamic-slice_bitcast_fusion
  36.3 1.0 %copy-done.5 = bf16[1040,256]{1,0:T(8,128)(2,1)S(1)} copy-done((bf16[1040,256]{1,0:T(8,128)(2,1)S(1)}, bf16[1040,256]{1,0:T(8,128)(2,1)}, u32[]{:S(2)}) %copy-start.5) | copy-done | bytes 532504
  37.3 3.4 %residual.4.refs_0_ = bf16[2048,256]{1,0:T(8,128)(2,1)S(1)} custom-call(s32[10]{0:T(128)S(1)} %pad_add_fusion.1.place, bf16[1040,256]{1,0:T(8,128)(2,1)S(1)} %copy-done.5, bf16[1040,256]{1,0:T(8,128)(2,1)} %collective-permute-done.5.refs_1_), custom_call_target="tpu_custom_call" | custom-call | flops 1000 | bytes 1000 | tf_op jit(solution)/shard_map/residual/pallas_call | solution.py:195
  40.7 1.0 %copy-done.1 = bf16[2048,256]{1,0:T(8,128)(2,1)} copy-done((bf16[2048,256]{1,0:T(8,128)(2,1)}, bf16[2048,256]{1,0:T(8,128)(2,1)S(1)}, u32[]{:S(2)}) %copy-start.1) | copy-done | bytes 1048600
  41.7 5.9 %collective-permute-done.8.refs_0_ = bf16[1040,256]{1,0:T(8,128)(2,1)} collective-permute-done((bf16[1040,256]{1,0:T(8,128)(2,1)}, bf16[1040,256]{1,0:T(8,128)(2,1)}, u32[]{:S(2)}, u32[]{:S(2)}) %collective-permute-start.8) | collective-permute-done | bytes 532512 | tf_op jit(solution)/shard_map/ppermute | solution.py:347
  47.5 1.9 %pick.9 = bf16[1040,256]{1,0:T(8,128)(2,1)} custom-call(s32[1]{0:T(128)S(6)} %sub.21.place, bf16[1040,256]{1,0:T(8,128)(2,1)} %collective-permute-done.8.refs_0_, bf16[1040,256]{1,0:T(8,128)(2,1)S(1)} %collective-permute-done.6.refs_0_.refs_1_), custom_call_target="tpu_custom_call" | custom-call | flops 1000 | bytes 1000 | tf_op jit(solution)/shard_map/pick/pallas_call | solution.py:89
  49.5 3.5 %collective-permute-start.10 = (bf16[1040,256]{1,0:T(8,128)(2,1)}, bf16[1040,256]{1,0:T(8,128)(2,1)}, u32[]{:S(2)}, u32[]{:S(2)}) collective-permute-start(bf16[1040,256]{1,0:T(8,128)(2,1)} %pick.9), channel_id=1, source_target_pairs={{0,9},{6,15},{1,8},{7,14},{16,25},{22,31},{17,24},{23,30},{8,2},{1... | collective-permute-start | bytes 1597448 | tf_op jit(solution)/shard_map/ppermute | solution.py:347
  53.0 1.9 %pick.8 = bf16[1040,256]{1,0:T(8,128)(2,1)} custom-call(s32[1]{0:T(128)} %bitcast.3.place, bf16[1040,256]{1,0:T(8,128)(2,1)S(1)} %collective-permute-done.7.refs_0_.refs_1_, bf16[1040,256]{1,0:T(8,128)(2,1)} %collective-permute-done.5.refs_1_), custom_call_target="tpu_custom_call" | custom-call | flops 1000 | bytes 1000 | tf_op jit(solution)/shard_map/pick/pallas_call | solution.py:89
  55.0 0.9 halves.1
  56.0 0.8 copy-done.6
  56.8 0.5 collective-permute-start.16
  57.3 0.2 collective-permute-start.14
  57.7 2.9 %residual.5.refs_1_ = bf16[2048,256]{1,0:T(8,128)(2,1)S(1)} custom-call(s32[10]{0:T(128)S(1)} %pad_add_fusion.1.place, bf16[1040,256]{1,0:T(8,128)(2,1)S(1)} %pick.10.refs_0_, bf16[1040,256]{1,0:T(8,128)(2,1)S(1)} %pick.11.refs_1_), custom_call_target="tpu_custom_call" | custom-call | flops 1000 | bytes 1000 | tf_op jit(solution)/shard_map/residual/pallas_call | solution.py:195
  60.6 1.2 %pick.12.refs_0_ = bf16[1040,256]{1,0:T(8,128)(2,1)S(1)} custom-call(s32[1]{0:T(128)} %bitcast.2.place, bf16[1040,256]{1,0:T(8,128)(2,1)} %collective-permute-done.10.refs_0_, bf16[1040,256]{1,0:T(8,128)(2,1)S(1)} %cut.3.refs_1_), custom_call_target="tpu_custom_call" | custom-call | flops 1000 | bytes 1000 | tf_op jit(solution)/shard_map/pick/pallas_call | solution.py:89
  61.7 3.2 %collective-permute-done.9.refs_0_.refs_1_ = bf16[1040,256]{1,0:T(8,128)(2,1)} collective-permute-done((bf16[1040,256]{1,0:T(8,128)(2,1)}, bf16[1040,256]{1,0:T(8,128)(2,1)}, u32[]{:S(2)}, u32[]{:S(2)}) %collective-permute-start.9) | collective-permute-done | bytes 532512 | tf_op jit(solution)/shard_map/ppermute | solution.py:347
  64.9 1.1 %pick.13 = bf16[1040,256]{1,0:T(8,128)(2,1)S(1)} custom-call(s32[1]{0:T(128)S(6)} %sub.21.place, bf16[1040,256]{1,0:T(8,128)(2,1)} %collective-permute-done.9.refs_0_.refs_1_, bf16[1040,256]{1,0:T(8,128)(2,1)S(1)} %collective-permute-done.7.refs_0_.refs_1_), custom_call_target="tpu_custom_call" | custom-call | flops 1000 | bytes 1000 | tf_op jit(solution)/shard_map/pick/pallas_call | solution.py:89
  66.0 4.1 %collective-permute-start.11 = (bf16[1040,256]{1,0:T(8,128)(2,1)S(1)}, bf16[1040,256]{1,0:T(8,128)(2,1)S(1)}, u32[]{:S(2)}, u32[]{:S(2)}) collective-permute-start(bf16[1040,256]{1,0:T(8,128)(2,1)S(1)} %pick.13), channel_id=1, source_target_pairs={{0,9},{6,15},{1,8},{7,14},{16,25},{22,31},{17,24},{23,30},{8,2},{1... | collective-permute-start | bytes 1597448 | tf_op jit(solution)/shard_map/ppermute | solution.py:347
  70.3 1.1 %collective-permute-done.16.refs_2_.refs_6_ = bf16[2,2,128,512]{3,2,1,0:T(8,128)(2,1)} collective-permute-done((bf16[2,2,128,512]{3,2,1,0:T(8,128)(2,1)}, bf16[2,2,128,512]{3,2,1,0:T(8,128)(2,1)}, u32[]{:S(2)}, u32[]{:S(2)}) %collective-permute-start.16) | collective-permute-done | bytes 524320 | tf_op jit(solution)/shard_map/ppermute | solution.py:347
  71.4 1.8 %residual.6.refs_2_ = f32[2048,256]{1,0:T(8,128)S(1)} custom-call(s32[10]{0:T(128)S(1)} %pad_add_fusion.1.place, bf16[1040,256]{1,0:T(8,128)(2,1)S(1)} %pick.12.refs_0_), custom_call_target="tpu_custom_call" | custom-call | flops 1000 | bytes 1000 | tf_op jit(solution)/shard_map/residual/pallas_call | solution.py:195
  73.2 3.5 %residual.7.refs_2_ = bf16[2048,256]{1,0:T(8,128)(2,1)S(1)} custom-call(s32[10]{0:T(128)S(1)} %pad_add_fusion.1.place, bf16[1040,256]{1,0:T(8,128)(2,1)} %collective-permute-done.8.refs_0_, bf16[1040,256]{1,0:T(8,128)(2,1)} %collective-permute-done.9.refs_0_.refs_1_), custom_call_target="tpu_custom_call" | custom-call | flops 1000 | bytes 1000 | tf_op jit(solution)/shard_map/residual/pallas_call | solution.py:195
  76.8 5.3 %correlate.1.factors = f32[3,2,128,512]{3,2,1,0:T(8,128)S(1)} custom-call(bf16[2048,256]{1,0:T(8,128)(2,1)S(1)} %copy-done.2, bf16[2048,256]{1,0:T(8,128)(2,1)S(1)} %residual.5.refs_1_, bf16[2048,256]{1,0:T(8,128)(2,1)S(1)} %residual.7.refs_2_, bf16[2,512,512]{2,1,0:T(8,128)(2,1)S(1)} %copy-done, ...), custom_call_target="tpu_custom_call" | custom-call | flops 1000 | bytes 1000 | tf_op jit(solution)/shard_map/correlate/pallas_call | solution.py:237
  82.1 2.5 %fold.1.refs_3_ = f32[1,512]{1,0:T(1,128)S(1)} custom-call(s32[10]{0:T(128)S(1)} %pad_add_fusion.1.place, f32[3,2,128,512]{3,2,1,0:T(8,128)S(1)} %correlate.1.factors, bf16[2,2,128,512]{3,2,1,0:T(8,128)(2,1)S(1)} %copy-done.7, bf16[2,2,128,512]{3,2,1,0:T(8,128)(2,1)S(1)} %collective-permute-done.15.refs_1_.refs_5_, ...), custom_call_target="tpu_custom_call" | custom-call | flops 1000 | bytes 1000 | tf_op jit(solution)/shard_map/fold/pallas_call | solution.py:281
  84.6 4.9 %last.1 = f32[1,512]{1,0:T(1,128)S(1)} custom-call(s32[10]{0:T(128)S(1)} %pad_add_fusion.1.place, bf16[1040,256]{1,0:T(8,128)(2,1)S(1)} %collective-permute-done.11.refs_0_, bf16[1040,256]{1,0:T(8,128)(2,1)S(1)} %join.1.refs_1_, f32[2048,256]{1,0:T(8,128)S(1)} %residual.6.refs_2_, f32[1,512]{1,0:T(1,128)S(1)} %fold.1.refs_3_, ...), custom_call_target="tpu_custom_call" | custom-call | flops 1000 | bytes 1000 | tf_op jit(solution)/shard_map/last/pallas_call | solution.py:316
  89.6 0.6 collective-permute-start.18
  90.1 0.5 collective-permute-start.19
  90.7 0.9 collective-permute-start.20
  91.6 2.2 %collective-permute-done.19 = f32[512]{0:T(512)S(1)} collective-permute-done((f32[512]{0:T(512)S(1)}, f32[512]{0:T(512)S(1)}, u32[]{:S(2)}, u32[]{:S(2)}) %collective-permute-start.19) | collective-permute-done | bytes 2080 | tf_op jit(solution)/shard_map/ppermute | solution.py:347
  93.7 0.6 add_add_fusion
  (43 shorter events, 0.9 us)
Async XLA Ops:
  0.0 20.9 %copy-start = (bf16[2,512,512]{2,1,0:T(8,128)(2,1)S(1)}, bf16[2,512,512]{2,1,0:T(8,128)(2,1)}, u32[]{:S(2)}) copy-start(bf16[2,512,512]{2,1,0:T(8,128)(2,1)} %refs_8_.1) | copy-start | bytes 3145732
  0.0 5.4 %collective-permute-start.2 = (bf16[512,512]{1,0:T(8,128)(2,1)}, bf16[512,512]{1,0:T(8,128)(2,1)S(1)}, u32[]{:S(2)}, u32[]{:S(2)}) collective-permute-start(bf16[512,512]{1,0:T(8,128)(2,1)} %bitcast.14), channel_id=1, source_target_pairs={{0,8},{2,10},{4,12},{6,14},{1,9},{3,11},{5,13},{7,15},{8,0},{10,2}... | collective-permute-start | bytes 1572872 | tf_op jit(solution)/shard_map/ppermute | solution.py:347
  1.2 4.2 %collective-permute-start.3 = (bf16[16,512]{1,0:T(8,128)(2,1)S(1)}, bf16[16,512]{1,0:T(8,128)(2,1)S(1)}, u32[]{:S(2)}, u32[]{:S(2)}) collective-permute-start(bf16[16,512]{1,0:T(8,128)(2,1)S(1)} %fusion.2.refs_1_.refs_2_), channel_id=1, source_target_pairs={{0,8},{2,10},{4,12},{6,14},{1,9},{3,11},{5,13},{7,15},{8,0},{10,2}... | collective-permute-start | bytes 49160 | tf_op jit(solution)/shard_map/ppermute | solution.py:347
  1.4 1.0 %copy-start.8 = (bf16[1,512,512]{2,1,0:T(8,128)(2,1)S(1)}, bf16[1,512,512]{2,1,0:T(8,128)(2,1)}, u32[]{:S(2)}) copy-start(bf16[1,512,512]{2,1,0:T(8,128)(2,1)} %param.6) | copy-start | bytes 1572868
  2.5 9.7 %collective-permute-start = (bf16[528,256]{1,0:T(8,128)(2,1)S(1)}, bf16[528,256]{1,0:T(8,128)(2,1)S(1)}, u32[]{:S(2)}, u32[]{:S(2)}) collective-permute-start(bf16[528,256]{1,0:T(8,128)(2,1)S(1)} %cut.2), channel_id=1, source_target_pairs={{0,16},{2,18},{4,20},{6,22},{1,17},{3,19},{5,21},{7,23},{8,24},{10... | collective-permute-start | bytes 811016 | tf_op jit(solution)/shard_map/ppermute | solution.py:347
  5.5 1.0 %copy-start.9 = (bf16[1,512,512]{2,1,0:T(8,128)(2,1)S(1)}, bf16[1,512,512]{2,1,0:T(8,128)(2,1)}, u32[]{:S(2)}) copy-start(bf16[1,512,512]{2,1,0:T(8,128)(2,1)} %param.6) | copy-start | bytes 1572868
  6.6 9.3 %collective-permute-start.4 = (bf16[1040,256]{1,0:T(8,128)(2,1)S(1)}, bf16[1040,256]{1,0:T(8,128)(2,1)S(1)}, u32[]{:S(2)}, u32[]{:S(2)}) collective-permute-start(bf16[1040,256]{1,0:T(8,128)(2,1)S(1)} %cut.3.refs_1_), channel_id=1, source_target_pairs={{0,9},{6,15},{1,8},{7,14},{16,25},{22,31},{17,24},{23,30},{8,2},{1... | collective-permute-start | bytes 1597448 | tf_op jit(solution)/shard_map/ppermute | solution.py:347
  12.2 1.5 %collective-permute-start.1 = (bf16[528,256]{1,0:T(8,128)(2,1)S(1)}, bf16[528,256]{1,0:T(8,128)(2,1)S(1)}, u32[]{:S(2)}, u32[]{:S(2)}) collective-permute-start(bf16[528,256]{1,0:T(8,128)(2,1)S(1)} %collective-permute-done.mine), channel_id=1, source_target_pairs={{0,8},{2,10},{4,12},{6,14},{1,9},{3,11},{5,13},{7,15},{8,0},{10,2}... | collective-permute-start | bytes 811016 | tf_op jit(solution)/shard_map/ppermute | solution.py:347
  16.0 13.1 %collective-permute-start.5 = (bf16[1040,256]{1,0:T(8,128)(2,1)S(1)}, bf16[1040,256]{1,0:T(8,128)(2,1)}, u32[]{:S(2)}, u32[]{:S(2)}) collective-permute-start(bf16[1040,256]{1,0:T(8,128)(2,1)S(1)} %join.1.refs_1_), channel_id=1, source_target_pairs={{0,9},{6,15},{1,8},{7,14},{16,25},{22,31},{17,24},{23,30},{8,2},{1... | collective-permute-start | bytes 1597448 | tf_op jit(solution)/shard_map/ppermute | solution.py:347
  16.6 14.3 %collective-permute-start.6 = (bf16[1040,256]{1,0:T(8,128)(2,1)S(1)}, bf16[1040,256]{1,0:T(8,128)(2,1)S(1)}, u32[]{:S(2)}, u32[]{:S(2)}) collective-permute-start(bf16[1040,256]{1,0:T(8,128)(2,1)S(1)} %collective-permute-done.4.refs_1_.refs_0_), channel_id=1, source_target_pairs={{0,9},{6,15},{1,8},{7,14},{16,25},{22,31},{17,24},{23,30},{10,0},{... | collective-permute-start | bytes 1597448 | tf_op jit(solution)/shard_map/ppermute | solution.py:347
  20.1 0.8 copy-start.3
  20.9 36.4 %collective-permute-start.13 = (bf16[2,512,512]{2,1,0:T(8,128)(2,1)S(1)}, bf16[2,512,512]{2,1,0:T(8,128)(2,1)}, u32[]{:S(2)}, u32[]{:S(2)}) collective-permute-start(bf16[2,512,512]{2,1,0:T(8,128)(2,1)S(1)} %copy-done), channel_id=1, source_target_pairs={{0,16},{2,18},{4,20},{6,22},{1,17},{3,19},{5,21},{7,23},{8,24},{10... | collective-permute-start | bytes 3145736 | tf_op jit(solution)/shard_map/ppermute | solution.py:347
  30.9 22.0 %collective-permute-start.7 = (bf16[1040,256]{1,0:T(8,128)(2,1)}, bf16[1040,256]{1,0:T(8,128)(2,1)S(1)}, u32[]{:S(2)}, u32[]{:S(2)}) collective-permute-start(bf16[1040,256]{1,0:T(8,128)(2,1)} %collective-permute-done.5.refs_1_), channel_id=1, source_target_pairs={{0,9},{6,15},{1,8},{7,14},{16,25},{22,31},{17,24},{23,30},{10,0},{... | collective-permute-start | bytes 1597448 | tf_op jit(solution)/shard_map/ppermute | solution.py:347
  33.3 1.0 %copy-start.4 = (bf16[1040,256]{1,0:T(8,128)(2,1)S(1)}, bf16[1040,256]{1,0:T(8,128)(2,1)}, u32[]{:S(2)}) copy-start(bf16[1040,256]{1,0:T(8,128)(2,1)} %copy-done.3) | copy-start | bytes 1597444
  35.2 12.3 %collective-permute-start.8 = (bf16[1040,256]{1,0:T(8,128)(2,1)}, bf16[1040,256]{1,0:T(8,128)(2,1)}, u32[]{:S(2)}, u32[]{:S(2)}) collective-permute-start(bf16[1040,256]{1,0:T(8,128)(2,1)} %pick.7), channel_id=1, source_target_pairs={{0,9},{6,15},{1,8},{7,14},{16,25},{22,31},{17,24},{23,30},{8,2},{1... | collective-permute-start | bytes 1597448 | tf_op jit(solution)/shard_map/ppermute | solution.py:347
  36.3 1.0 %copy-start.5 = (bf16[1040,256]{1,0:T(8,128)(2,1)S(1)}, bf16[1040,256]{1,0:T(8,128)(2,1)}, u32[]{:S(2)}) copy-start(bf16[1040,256]{1,0:T(8,128)(2,1)} %copy-done.3) | copy-start | bytes 1597444
  40.7 1.0 %copy-start.1 = (bf16[2048,256]{1,0:T(8,128)(2,1)}, bf16[2048,256]{1,0:T(8,128)(2,1)S(1)}, u32[]{:S(2)}) copy-start(bf16[2048,256]{1,0:T(8,128)(2,1)S(1)} %residual.4.refs_0_) | copy-start | bytes 3145732
  41.7 13.4 %copy-start.10 = (bf16[2,512,512]{2,1,0:T(8,128)(2,1)S(1)}, bf16[2,512,512]{2,1,0:T(8,128)(2,1)}, u32[]{:S(2)}) copy-start(bf16[2,512,512]{2,1,0:T(8,128)(2,1)} %param.10) | copy-start | bytes 3145732
  49.5 11.1 %collective-permute-start.10 = (bf16[1040,256]{1,0:T(8,128)(2,1)}, bf16[1040,256]{1,0:T(8,128)(2,1)}, u32[]{:S(2)}, u32[]{:S(2)}) collective-permute-start(bf16[1040,256]{1,0:T(8,128)(2,1)} %pick.9), channel_id=1, source_target_pairs={{0,9},{6,15},{1,8},{7,14},{16,25},{22,31},{17,24},{23,30},{8,2},{1... | collective-permute-start | bytes 1597448 | tf_op jit(solution)/shard_map/ppermute | solution.py:347
  54.9 10.1 %collective-permute-start.9 = (bf16[1040,256]{1,0:T(8,128)(2,1)}, bf16[1040,256]{1,0:T(8,128)(2,1)}, u32[]{:S(2)}, u32[]{:S(2)}) collective-permute-start(bf16[1040,256]{1,0:T(8,128)(2,1)} %pick.8), channel_id=1, source_target_pairs={{0,9},{6,15},{1,8},{7,14},{16,25},{22,31},{17,24},{23,30},{8,2},{1... | collective-permute-start | bytes 1597448 | tf_op jit(solution)/shard_map/ppermute | solution.py:347
  55.0 21.8 %collective-permute-start.12 = (bf16[2,512,512]{2,1,0:T(8,128)(2,1)S(1)}, bf16[2,512,512]{2,1,0:T(8,128)(2,1)}, u32[]{:S(2)}, u32[]{:S(2)}) collective-permute-start(bf16[2,512,512]{2,1,0:T(8,128)(2,1)S(1)} %copy-done), channel_id=1, source_target_pairs={{0,8},{2,10},{4,12},{6,14},{1,9},{3,11},{5,13},{7,15},{8,0},{10,2}... | collective-permute-start | bytes 3145736 | tf_op jit(solution)/shard_map/ppermute | solution.py:347
  56.0 0.8 copy-start.6
  56.8 14.6 %collective-permute-start.16 = (bf16[2,2,128,512]{3,2,1,0:T(8,128)(2,1)}, bf16[2,2,128,512]{3,2,1,0:T(8,128)(2,1)}, u32[]{:S(2)}, u32[]{:S(2)}) collective-permute-start(bf16[2,2,128,512]{3,2,1,0:T(8,128)(2,1)} %get-tuple-element.35), channel_id=1, source_target_pairs={{0,16},{2,18},{4,20},{6,22},{1,17},{3,19},{5,21},{7,23},{8,24},{10... | collective-permute-start | bytes 1572872 | tf_op jit(solution)/shard_map/ppermute | solution.py:347
  57.3 19.4 %collective-permute-start.14 = (bf16[2,512,512]{2,1,0:T(8,128)(2,1)}, bf16[2,512,512]{2,1,0:T(8,128)(2,1)}, u32[]{:S(2)}, u32[]{:S(2)}) collective-permute-start(bf16[2,512,512]{2,1,0:T(8,128)(2,1)} %collective-permute-done.13.refs_5_.refs_10_), channel_id=1, source_target_pairs={{0,8},{2,10},{4,12},{6,14},{1,9},{3,11},{5,13},{7,15},{8,0},{10,2}... | collective-permute-start | bytes 3145736 | tf_op jit(solution)/shard_map/ppermute | solution.py:347
  60.5 9.6 %copy-start.7 = (bf16[2,2,128,512]{3,2,1,0:T(8,128)(2,1)S(1)}, bf16[2,2,128,512]{3,2,1,0:T(8,128)(2,1)}, u32[]{:S(2)}) copy-start(bf16[2,2,128,512]{3,2,1,0:T(8,128)(2,1)} %copy-done.6) | copy-start | bytes 1572868
  66.0 18.6 %collective-permute-start.11 = (bf16[1040,256]{1,0:T(8,128)(2,1)S(1)}, bf16[1040,256]{1,0:T(8,128)(2,1)S(1)}, u32[]{:S(2)}, u32[]{:S(2)}) collective-permute-start(bf16[1040,256]{1,0:T(8,128)(2,1)S(1)} %pick.13), channel_id=1, source_target_pairs={{0,9},{6,15},{1,8},{7,14},{16,25},{22,31},{17,24},{23,30},{8,2},{1... | collective-permute-start | bytes 1597448 | tf_op jit(solution)/shard_map/ppermute | solution.py:347
  70.2 6.6 %copy-start.2 = (bf16[2048,256]{1,0:T(8,128)(2,1)S(1)}, bf16[2048,256]{1,0:T(8,128)(2,1)}, u32[]{:S(2)}) copy-start(bf16[2048,256]{1,0:T(8,128)(2,1)} %copy-done.1) | copy-start | bytes 3145732
  70.2 11.9 %collective-permute-start.15 = (bf16[2,2,128,512]{3,2,1,0:T(8,128)(2,1)S(1)}, bf16[2,2,128,512]{3,2,1,0:T(8,128)(2,1)S(1)}, u32[]{:S(2)}, u32[]{:S(2)}) collective-permute-start(bf16[2,2,128,512]{3,2,1,0:T(8,128)(2,1)S(1)} %copy-done.7), channel_id=1, source_target_pairs={{0,8},{2,10},{4,12},{6,14},{1,9},{3,11},{5,13},{7,15},{8,0},{10,2}... | collective-permute-start | bytes 1572872 | tf_op jit(solution)/shard_map/ppermute | solution.py:347
  71.4 10.7 %collective-permute-start.17 = (bf16[2,2,128,512]{3,2,1,0:T(8,128)(2,1)}, bf16[2,2,128,512]{3,2,1,0:T(8,128)(2,1)S(1)}, u32[]{:S(2)}, u32[]{:S(2)}) collective-permute-start(bf16[2,2,128,512]{3,2,1,0:T(8,128)(2,1)} %collective-permute-done.16.refs_2_.refs_6_), channel_id=1, source_target_pairs={{0,8},{2,10},{4,12},{6,14},{1,9},{3,11},{5,13},{7,15},{8,0},{10,2}... | collective-permute-start | bytes 1572872 | tf_op jit(solution)/shard_map/ppermute | solution.py:347
  89.6 2.0 %collective-permute-start.18 = (f32[512]{0:T(512)S(1)}, f32[512]{0:T(512)S(1)}, u32[]{:S(2)}, u32[]{:S(2)}) collective-permute-start(f32[512]{0:T(512)S(1)} %bitcast.18), channel_id=1, source_target_pairs={{0,8},{2,10},{4,12},{6,14},{1,9},{3,11},{5,13},{7,15},{8,0},{10,2}... | collective-permute-start | bytes 6152 | tf_op jit(solution)/shard_map/ppermute | solution.py:347
  90.1 3.6 %collective-permute-start.19 = (f32[512]{0:T(512)S(1)}, f32[512]{0:T(512)S(1)}, u32[]{:S(2)}, u32[]{:S(2)}) collective-permute-start(f32[512]{0:T(512)S(1)} %bitcast.19), channel_id=1, source_target_pairs={{0,16},{2,18},{4,20},{6,22},{1,17},{3,19},{5,21},{7,23},{8,24},{10... | collective-permute-start | bytes 6152 | tf_op jit(solution)/shard_map/ppermute | solution.py:347
  90.7 3.1 %collective-permute-start.20 = (f32[512]{0:T(512)S(1)}, f32[512]{0:T(512)S(1)}, u32[]{:S(2)}, u32[]{:S(2)}) collective-permute-start(f32[512]{0:T(512)S(1)} %bitcast.20), channel_id=1, source_target_pairs={{0,24},{2,26},{4,28},{6,30},{1,25},{3,27},{5,29},{7,31},{8,16},{10... | collective-permute-start | bytes 6152 | tf_op jit(solution)/shard_map/ppermute | solution.py:347

commit v3 on v2

--- a/solution.py
+++ b/solution.py
@@ -59,11 +59,15 @@
 
 
 def cut_kernel(n, place, *refs):
-    values, ids, out_ref = refs[:n], refs[n : 2 * n], refs[2 * n]
-    rows = values[0].shape[0]
-    for k, ref in enumerate(values):
-        receivers(ref, place[0] == 0, rows, out_ref, k * rows)
+    values, ids, (out_ref, mine, sem) = refs[:n], refs[n : 2 * n], refs[2 * n :]
+    copy = pltpu.make_async_copy(values[0], mine, sem)
+    copy.start()
+    rows = mine.shape[0]
     out_ref[n * rows :, :] = id_block(ids, range(2))
+    for k in range(1, n):
+        receivers(values[k], place[0] == 0, rows, out_ref, k * rows)
+    copy.wait()
+    receivers(mine, place[0] == 0, rows, out_ref, 0)
 
 
 def cut(half, values, ids):
@@ -73,29 +77,16 @@
         functools.partial(cut_kernel, n),
         name="cut",
         out_shape=jax.ShapeDtypeStruct((n * rows + PAD, width // 2), jnp.bfloat16),
-        in_specs=[SMEM_SPEC] + [VMEM_SPEC] * (2 * n),
-        out_specs=VMEM_SPEC,
+        in_specs=[SMEM_SPEC, pl.BlockSpec(memory_space=pltpu.HBM)]
+        + [VMEM_SPEC] * (2 * n - 1),
+        out_specs=VMEM_SPEC,
+        scratch_shapes=[
+            pltpu.VMEM(values[0].shape, jnp.bfloat16),
+            pltpu.SemaphoreType.DMA,
+        ],
         compiler_params=params(),
         cost_estimate=light(),
     )(half, *values, *ids)
-
-
-def pick_kernel(n, place, *refs):
-    fetch(place[0], refs[:n], refs[n], refs[n + 1])
-
-
-def pick(which, candidates):
-    first = candidates[0]
-    return pl.pallas_call(
-        functools.partial(pick_kernel, len(candidates)),
-        name="pick",
-        out_shape=jax.ShapeDtypeStruct(first.shape, first.dtype),
-        in_specs=[SMEM_SPEC] + [VMEM_SPEC] * len(candidates),
-        out_specs=VMEM_SPEC,
-        scratch_shapes=[pltpu.SemaphoreType.DMA],
-        compiler_params=params(),
-        cost_estimate=light(),
-    )(which, *candidates)
 
 
 def join_kernel(mine, other, out_ref):
@@ -191,16 +182,40 @@
         ).astype(out_ref.dtype)
 
 
-def residual(place, pieces, sources, dtype=jnp.bfloat16):
+def residual(place, pieces, sources):
     return pl.pallas_call(
         functools.partial(residual_kernel, len(pieces)),
         name="residual",
-        out_shape=jax.ShapeDtypeStruct((sources, pieces[0].shape[1]), dtype),
+        out_shape=jax.ShapeDtypeStruct((sources, pieces[0].shape[1]), jnp.bfloat16),
         in_specs=[SMEM_SPEC] + [VMEM_SPEC] * len(pieces),
         out_specs=VMEM_SPEC,
         compiler_params=params(),
         cost_estimate=light(),
     )(place, *pieces)
+
+
+def begin_kernel(n, place, *refs):
+    cand, (out_ref, piece, sem) = refs[:n], refs[n:]
+    fetch(place[9], cand, piece, sem)
+    rows = out_ref.shape[0] // 4
+    for group in range(4):
+        out_ref[group * rows : (group + 1) * rows, :] = assemble(
+            place[0], (piece,), group
+        )
+
+
+def begin(place, cand, sources):
+    shape = cand[0].shape
+    return pl.pallas_call(
+        functools.partial(begin_kernel, len(cand)),
+        name="begin",
+        out_shape=jax.ShapeDtypeStruct((sources, shape[1]), jnp.float32),
+        in_specs=[SMEM_SPEC] + [VMEM_SPEC] * len(cand),
+        out_specs=VMEM_SPEC,
+        scratch_shapes=[pltpu.VMEM(shape, jnp.bfloat16), pltpu.SemaphoreType.DMA],
+        compiler_params=params(),
+        cost_estimate=light(),
+    )(place, *cand)
 
 
 def correlate(res, fields):
@@ -261,28 +276,29 @@
     return wait
 
 
-def fold_kernel(place, factors, *refs):
-    greens, (out_ref, green, sems) = refs[:4], refs[4:]
-    slots = factors.shape[0]
+def fold_kernel(n, place, *refs):
+    factors, greens, (out_ref, green, sems) = refs[:n], refs[n : n + 4], refs[n + 4 :]
+    slots = [(ref, k) for ref in factors for k in range(ref.shape[0])]
     waits = [
-        fetch_green(place, k, greens, green.at[k], sems.at[k]) for k in range(slots)
+        fetch_green(place, j, greens, green.at[j], sems.at[j])
+        for j in range(len(slots))
     ]
     total = None
-    for k in range(slots):
-        waits[k]()
+    for j, (ref, k) in enumerate(slots):
+        waits[j]()
         for p in range(2):
-            term = green[k, p].astype(jnp.float32) * factors[k, p]
+            term = green[j, p].astype(jnp.float32) * ref[k, p]
             total = term if total is None else total + term
     out_ref[...] = jnp.sum(total, axis=0, keepdims=True)
 
 
 def fold(place, factors, greens):
-    slots = factors.shape[0]
-    return pl.pallas_call(
-        fold_kernel,
+    slots = sum(f.shape[0] for f in factors)
+    return pl.pallas_call(
+        functools.partial(fold_kernel, len(factors)),
         name="fold",
-        out_shape=jax.ShapeDtypeStruct((1, factors.shape[3]), jnp.float32),
-        in_specs=[SMEM_SPEC] + [VMEM_SPEC] * (1 + len(greens)),
+        out_shape=jax.ShapeDtypeStruct((1, factors[0].shape[3]), jnp.float32),
+        in_specs=[SMEM_SPEC] + [VMEM_SPEC] * (len(factors) + len(greens)),
         out_specs=VMEM_SPEC,
         scratch_shapes=[
             pltpu.VMEM((slots, 2) + greens[0].shape[2:], jnp.bfloat16),
@@ -290,7 +306,7 @@
         ],
         compiler_params=params(),
         cost_estimate=light(),
-    )(place, factors, *greens)
+    )(place, *factors, *greens)
 
 
 def last_kernel(n_b, place, *refs):
@@ -366,10 +382,11 @@
 
     moves = []
     for steps in (
+        [(0, 0, 1, None), (1, 0, 1, 1), (0, 1, 0, 0), (1, 1, 0, 2)],
         [(0, 0, 1, None), (1, 0, 0, 1), (0, 1, 0, 0), (1, 1, 1, 2)],
-        [(0, 0, 1, None), (1, 1, 0, 0), (0, 1, 0, 2)],
-        [(0, 0, 1, None), (1, 0, 0, 1), (0, 1, 0, 0), (1, 1, 1, None)],
-        [(0, 0, 1, None), (1, 0, 0, 1), (0, 1, 1, None)],
+        [(0, 0, 1, None), (1, 0, 1, 1), (0, 1, 0, 2), (1, 1, 0, 0)],
+        [(0, 0, 1, None), (1, 1, 1, 2)],
+        [(1, 0, 1, 1), (0, 1, 1, 0)],
     ):
         pairs = []
         for here_c, here_z, there_c, there_z in steps:
@@ -386,14 +403,13 @@
     brought = np.array(
         [
             [[(1, 0), (2, 0), (3, 0), (0, 0)], [(0, 1), (1, 1), (2, 1), (3, 1)]],
-            [[(0, 0), (3, 0), (0, 1), (1, 1)], [(2, 0), (1, 0), (2, 1), (3, 1)]],
+            [[(2, 0), (0, 1), (3, 1), (1, 0)], [(0, 0), (3, 0), (1, 1), (2, 1)]],
         ],
         np.int32,
     )
     mirrored = brought[::-1].copy()
     mirrored[..., 0] = len(lines) - 1 - mirrored[..., 0]
     table = jnp.asarray(np.concatenate([brought, mirrored]))
-    outer = (z == 0) | (z == len(lines) - 1)
 
     mine_now = lax.dynamic_index_in_dim(
         lax.dynamic_index_in_dim(table, z, 0, keepdims=False), c, 0, keepdims=False
@@ -401,45 +417,41 @@
     groups = jnp.bitwise_xor(mine_now[:, 0], slab)
     on_line = jnp.bitwise_xor(mine_now[:, 1], y)
     where_green = jnp.stack([groups, on_line], axis=1).reshape(-1)
-    stay_2 = jnp.where((~outer) & (c == 1), 1, 0)
-    stay_4 = jnp.where(outer & (c == 0), 1, 0)
     place = jnp.concatenate(
-        [jnp.stack([slab]), where_green, jnp.stack([stay_4])]
+        [jnp.stack([slab]), where_green, jnp.stack([1 - c])]
     ).astype(jnp.int32)
-    stay_2, stay_4 = (jnp.stack([k]).astype(jnp.int32) for k in (stay_2, stay_4))
-    core = jnp.stack([c]).astype(jnp.int32)
     sources = 4 * sources_here
+
+    def touch(array):
+        return array[:8, :128]
 
     r1_a = send(own, moves[0])
     r2_a = send(r1_a, moves[1])
     r1_b = send(after(crossed, r1_a), moves[0])
-    r3_a = send(pick(core, (r2_a, r1_a)), moves[2])
-    r2_b = send(after(r1_b, r2_a), moves[1])
+    r3_a = send(r2_a, moves[2])
+    r2_b = send(after(r1_b, touch(r2_a)), moves[1])
     res_1 = residual(place, (r1_a, after(r1_b, r2_a)), sources)
-    r4_a = send(pick(1 - stay_4, (after(r3_a, res_1), r2_a)), moves[3])
-    to_r3_b = pick(core, (after(r2_b, r3_a), r1_b))
-    r3_b = send(to_r3_b, moves[2])
-    second_a, second_b = pick(stay_2, (r2_a, own)), pick(stay_2, (r2_b, crossed))
-    res_2 = residual(place, (second_a, after(second_b, to_r3_b)), sources)
-    fourth_a = pick(stay_4, (after(r4_a, res_2), own))
-    to_r4_b = pick(1 - stay_4, (after(r3_b, fourth_a), r2_b))
-    r4_b = send(to_r4_b, moves[3])
-
-    field_core = send(after(source_fields, own), to_core)
+    r4_a = send(after(r3_a, res_1), moves[3])
+    r3_b = send(after(r2_b, touch(r3_a)), moves[2])
+    res_2 = residual(place, (r2_a, after(r2_b, r3_a)), sources)
+    begun = begin(place, (r4_a, own), sources)
+    r4_b = send(after(r3_b, res_2), moves[4])
+
+    field_core = send(after(source_fields, r1_a), to_core)
     field_x = send(after(source_fields, crossed_here), to_x)
-    field_far = send(after(field_x, to_r3_b), to_core)
+    field_far = send(after(field_x, res_1), to_core)
     fields = (source_fields, field_core, field_x, field_far)
 
     blocks = green_fields.reshape(2, 2, 2, -1, green_fields.shape[2])
     near, away_green = halves(place_x, after(blocks, r1_a))
-    far = send(after(away_green, r2_a), to_x)
-    far_core = send(after(far, to_r4_b), to_core)
+    far = send(after(away_green, r2_b), to_x)
+
+    res_3 = residual(place, (r3_a, r3_b), sources)
+    early = correlated((res_1, res_2), fields)
+    middle = correlated((after(res_3, early),), fields)
+    far_core = send(after(far, middle, begun), to_core)
     greens = (near, send(near, to_core), far, far_core)
-
-    res_3 = residual(place, (r3_a, after(r3_b, to_r4_b)), sources)
-    factors = correlated((res_1, res_2, res_3), fields)
-    begun = residual(place, (fourth_a,), sources, jnp.float32)
-    folded = fold(place, factors, greens)
+    folded = fold(place, (early, middle), greens)
     partial = last(place, (r4_b, crossed), begun, folded, greens, fields)[0]
     here = partial + send(partial, to_core)
     there = send(partial, to_x) + send(partial, to_both)

time: 95.4 us -> 74.4 us (0.78)
  Pallas kernels: 32.5 us -> 21.2 us
  local copies, waits for them, and re-layouts: 7.64 us -> 2.95 us
  starting transfers between devices: 22.3 us -> 17.7 us
    pallas_call x8 -> x2, Pallas kernels: 9.49 us -> 3.82 us  [the longest x1 1.96 us: fold(): pl.pallas_call(functools.partial(fold_kernel, len(factors)), name='fold',...]
    unnamed x22 -> x8, local copies, waits for them, and re-layouts: 6.77 us -> 2.09 us
    ppermute x21, starting transfers between devices: 22.3 us -> 17.7 us  [send(): return lax.ppermute(array, AXES, pairs)]
    pallas_call x4 -> x3, Pallas kernels: 11.6 us -> 9.77 us  [residual(): pl.pallas_call(functools.partial(residual_kernel, len(pieces)), name='res...]
    pallas_call x1 -> x2, Pallas kernels: 5.33 us -> 3.68 us  [correlated(): pl.pallas_call(functools.partial(correlate_kernel, len(res)), name='corre...]
    pallas_call x1, Pallas kernels: 4.94 us -> 3.46 us  [last(): pl.pallas_call(functools.partial(last_kernel, len(cand_b)), name='last',...]
  transfers between devices with their start and end apart: 21 -> 21, of which waited for: 9 -> 12; matrix products, arithmetic and copies ran while one was open for 2% -> 2% of each run, Pallas kernels for 29% -> 24%
where the time goes in v3:
time: 74.4 us; the launch traced here: 74 us
  waiting for transfers between devices  30.7 us (41%)
  Pallas kernels  21.2 us (28%)
  starting transfers between devices  17.7 us (24%)
  local copies, waits for them, and re-layouts  2.95 us (4%)
  other arithmetic  1.41 us (2%)
    ppermute x21, waiting for transfers between devices, send(): return lax.ppermute(array, AXES, pairs)  30.7 us
    ppermute x21, starting transfers between devices, send(): return lax.ppermute(array, AXES, pairs)  17.7 us
    pallas_call x3, Pallas kernels, residual(): pl.pallas_call(functools.partial(residual_kernel, len(pieces)), name='res...  9.77 us
    pallas_call x2, Pallas kernels, correlated(): pl.pallas_call(functools.partial(correlate_kernel, len(res)), name='corre...  3.68 us
    pallas_call x1, Pallas kernels, last(): pl.pallas_call(functools.partial(last_kernel, len(cand_b)), name='last',...  3.46 us
    unnamed x8, local copies, waits for them, and re-layouts  2.09 us
    pallas_call x1, Pallas kernels, fold(): pl.pallas_call(functools.partial(fold_kernel, len(factors)), name='fold',...  1.96 us
    pallas_call x1, Pallas kernels, begin(): pl.pallas_call(functools.partial(begin_kernel, len(cand)), name='begin',...  1.86 us
  transfers between devices with their start and end apart: 21, of which 12 were waited for; matrix products, arithmetic and copies ran while one was open for 2% of the time, Pallas kernels for 24%

profile of v3, /device:TPU:0, one launch (start us, length us, event | category | flops | bytes accessed | tf_op | source)
XLA Modules:
  0.0 74.0 jit_solution(2566088897897586212)
XLA Ops:
  0.0 0.5 collective-permute-start.2
  0.5 0.7 fusion.4
  1.2 1.0 %copy-done.1 = bf16[1,512,512]{2,1,0:T(8,128)(2,1)S(1)} copy-done((bf16[1,512,512]{2,1,0:T(8,128)(2,1)S(1)}, bf16[1,512,512]{2,1,0:T(8,128)(2,1)}, u32[]{:S(2)}) %copy-start.1) | copy-done | bytes 524312
  2.2 0.1 cut.2
  2.4 2.6 %collective-permute-start = (bf16[528,256]{1,0:T(8,128)(2,1)S(1)}, bf16[528,256]{1,0:T(8,128)(2,1)S(1)}, u32[]{:S(2)}, u32[]{:S(2)}) collective-permute-start(bf16[528,256]{1,0:T(8,128)(2,1)S(1)} %cut.2), channel_id=1, source_target_pairs={{0,16},{2,18},{4,20},{6,22},{1,17},{3,19},{5,21},{7,23},{8,24},{10... | collective-permute-start | bytes 811016 | tf_op jit(solution)/shard_map/ppermute | solution.py:363
  5.0 0.2 collective-permute-start.3
  5.2 1.0 %collective-permute-done.3.refs_3_ = bf16[16,512]{1,0:T(8,128)(2,1)S(1)} collective-permute-done((bf16[16,512]{1,0:T(8,128)(2,1)S(1)}, bf16[16,512]{1,0:T(8,128)(2,1)S(1)}, u32[]{:S(2)}, u32[]{:S(2)}) %collective-permute-start.3) | collective-permute-done | bytes 16416 | tf_op jit(solution)/shard_map/ppermute | solution.py:363
  6.2 1.0 %copy-done.2 = bf16[1,512,512]{2,1,0:T(8,128)(2,1)S(1)} copy-done((bf16[1,512,512]{2,1,0:T(8,128)(2,1)S(1)}, bf16[1,512,512]{2,1,0:T(8,128)(2,1)}, u32[]{:S(2)}) %copy-start.2) | copy-done | bytes 524312
  7.2 0.2 cut.3.refs_1_
  7.4 1.4 %collective-permute-start.4 = (bf16[1040,256]{1,0:T(8,128)(2,1)S(1)}, bf16[1040,256]{1,0:T(8,128)(2,1)}, u32[]{:S(2)}, u32[]{:S(2)}) collective-permute-start(bf16[1040,256]{1,0:T(8,128)(2,1)S(1)} %cut.3.refs_1_), channel_id=1, source_target_pairs={{0,9},{6,15},{1,8},{7,14},{16,25},{22,31},{17,24},{23,30},{8,10},{... | collective-permute-start | bytes 1597448 | tf_op jit(solution)/shard_map/ppermute | solution.py:363
  8.8 3.3 %collective-permute-done.mine = bf16[528,256]{1,0:T(8,128)(2,1)S(1)} collective-permute-done((bf16[528,256]{1,0:T(8,128)(2,1)S(1)}, bf16[528,256]{1,0:T(8,128)(2,1)S(1)}, u32[]{:S(2)}, u32[]{:S(2)}) %collective-permute-start) | collective-permute-done | bytes 270368 | tf_op jit(solution)/shard_map/ppermute | solution.py:363
  12.1 1.8 %collective-permute-start.13 = (bf16[2,512,512]{2,1,0:T(8,128)(2,1)S(1)}, bf16[2,512,512]{2,1,0:T(8,128)(2,1)S(1)}, u32[]{:S(2)}, u32[]{:S(2)}) collective-permute-start(bf16[2,512,512]{2,1,0:T(8,128)(2,1)S(1)} %copy-done), channel_id=1, source_target_pairs={{0,16},{2,18},{4,20},{6,22},{1,17},{3,19},{5,21},{7,23},{8,24},{10... | collective-permute-start | bytes 3145736 | tf_op jit(solution)/shard_map/ppermute | solution.py:363
  13.8 1.5 %collective-permute-done.1.other = bf16[528,256]{1,0:T(8,128)(2,1)S(1)} collective-permute-done((bf16[528,256]{1,0:T(8,128)(2,1)S(1)}, bf16[528,256]{1,0:T(8,128)(2,1)S(1)}, u32[]{:S(2)}, u32[]{:S(2)}) %collective-permute-start.1) | collective-permute-done | bytes 270368 | tf_op jit(solution)/shard_map/ppermute | solution.py:363
  15.4 1.4 %collective-permute-done.4.refs_0_ = bf16[1040,256]{1,0:T(8,128)(2,1)} collective-permute-done((bf16[1040,256]{1,0:T(8,128)(2,1)S(1)}, bf16[1040,256]{1,0:T(8,128)(2,1)}, u32[]{:S(2)}, u32[]{:S(2)}) %collective-permute-start.4) | collective-permute-done | bytes 532512 | tf_op jit(solution)/shard_map/ppermute | solution.py:363
  16.9 1.0 %collective-permute-start.5 = (bf16[1040,256]{1,0:T(8,128)(2,1)S(1)}, bf16[1040,256]{1,0:T(8,128)(2,1)}, u32[]{:S(2)}, u32[]{:S(2)}) collective-permute-start(bf16[1040,256]{1,0:T(8,128)(2,1)S(1)} %join.1.refs_1_), channel_id=1, source_target_pairs={{0,9},{6,15},{1,8},{7,14},{16,25},{22,31},{17,24},{23,30},{8,10},{... | collective-permute-start | bytes 1597448 | tf_op jit(solution)/shard_map/ppermute | solution.py:363
  17.9 0.7 collective-permute-start.8
  18.6 0.7 dynamic-slice_bitcast_fusion
  19.3 0.1 copy.8
  19.4 0.1 reshape.20
  19.5 6.8 %collective-permute-done.5.refs_1_ = bf16[1040,256]{1,0:T(8,128)(2,1)} collective-permute-done((bf16[1040,256]{1,0:T(8,128)(2,1)S(1)}, bf16[1040,256]{1,0:T(8,128)(2,1)}, u32[]{:S(2)}, u32[]{:S(2)}) %collective-permute-start.5) | collective-permute-done | bytes 532512 | tf_op jit(solution)/shard_map/ppermute | solution.py:363
  26.3 0.7 collective-permute-start.6
  27.0 5.0 %collective-permute-done.8.refs_0_ = bf16[1040,256]{1,0:T(8,128)(2,1)} collective-permute-done((bf16[1040,256]{1,0:T(8,128)(2,1)}, bf16[1040,256]{1,0:T(8,128)(2,1)}, u32[]{:S(2)}, u32[]{:S(2)}) %collective-permute-start.8) | collective-permute-done | bytes 532512 | tf_op jit(solution)/shard_map/ppermute | solution.py:363
  32.0 0.7 collective-permute-start.9
  32.7 0.1 pad_add_fusion.1.place
  32.8 3.5 %residual.4.refs_0_ = bf16[2048,256]{1,0:T(8,128)(2,1)S(1)} custom-call(s32[10]{0:T(128)S(1)} %pad_add_fusion.1.place, bf16[1040,256]{1,0:T(8,128)(2,1)} %collective-permute-done.4.refs_0_, bf16[1040,256]{1,0:T(8,128)(2,1)} %collective-permute-done.5.refs_1_), custom_call_target="tpu_custom_call" | custom-call | flops 1000 | bytes 1000 | tf_op jit(solution)/shard_map/residual/pallas_call | solution.py:186
  36.3 0.8 %collective-permute-done.13.refs_4_.refs_3_.refs_10_ = bf16[2,512,512]{2,1,0:T(8,128)(2,1)S(1)} collective-permute-done((bf16[2,512,512]{2,1,0:T(8,128)(2,1)S(1)}, bf16[2,512,512]{2,1,0:T(8,128)(2,1)S(1)}, u32[]{:S(2)}, u32[]{:S(2)}) %collective-permute-start.13) | collective-permute-done | bytes 1048608 | tf_op jit(solution)/shard_map/ppermute | solution.py:363
  37.1 2.8 %collective-permute-done.6.refs_1_ = bf16[1040,256]{1,0:T(8,128)(2,1)S(1)} collective-permute-done((bf16[1040,256]{1,0:T(8,128)(2,1)}, bf16[1040,256]{1,0:T(8,128)(2,1)S(1)}, u32[]{:S(2)}, u32[]{:S(2)}) %collective-permute-start.6) | collective-permute-done | bytes 532512 | tf_op jit(solution)/shard_map/ppermute | solution.py:363
  39.9 3.4 %collective-permute-done.9.refs_0_ = bf16[1040,256]{1,0:T(8,128)(2,1)S(1)} collective-permute-done((bf16[1040,256]{1,0:T(8,128)(2,1)}, bf16[1040,256]{1,0:T(8,128)(2,1)S(1)}, u32[]{:S(2)}, u32[]{:S(2)}) %collective-permute-start.9) | collective-permute-done | bytes 532512 | tf_op jit(solution)/shard_map/ppermute | solution.py:363
  43.3 2.7 %collective-permute-start.11 = (bf16[1040,256]{1,0:T(8,128)(2,1)S(1)}, bf16[1040,256]{1,0:T(8,128)(2,1)S(1)}, u32[]{:S(2)}, u32[]{:S(2)}) collective-permute-start(bf16[1040,256]{1,0:T(8,128)(2,1)S(1)} %collective-permute-done.9.refs_0_), channel_id=1, source_target_pairs={{0,9},{6,15},{1,8},{7,14},{16,25},{22,31},{17,24},{23,30},{10,12},... | collective-permute-start | bytes 1597448 | tf_op jit(solution)/shard_map/ppermute | solution.py:363
  45.9 0.1 halves.1
  46.0 0.6 collective-permute-start.16
  46.6 3.4 %residual.3.refs_1_ = bf16[2048,256]{1,0:T(8,128)(2,1)S(1)} custom-call(s32[10]{0:T(128)S(1)} %pad_add_fusion.1.place, bf16[1040,256]{1,0:T(8,128)(2,1)} %collective-permute-done.8.refs_0_, bf16[1040,256]{1,0:T(8,128)(2,1)S(1)} %collective-permute-done.6.refs_1_), custom_call_target="tpu_custom_call" | custom-call | flops 1000 | bytes 1000 | tf_op jit(solution)/shard_map/residual/pallas_call | solution.py:186
  50.0 0.7 collective-permute-start.10
  50.7 2.2 %collective-permute-start.15 = (bf16[2,2,128,512]{3,2,1,0:T(8,128)(2,1)S(1)}, bf16[2,2,128,512]{3,2,1,0:T(8,128)(2,1)S(1)}, u32[]{:S(2)}, u32[]{:S(2)}) collective-permute-start(bf16[2,2,128,512]{3,2,1,0:T(8,128)(2,1)S(1)} %get-tuple-element.29.refs_2_.refs_4_), channel_id=1, source_target_pairs={{0,8},{2,10},{4,12},{6,14},{1,9},{3,11},{5,13},{7,15},{8,0},{10,2}... | collective-permute-start | bytes 1572872 | tf_op jit(solution)/shard_map/ppermute | solution.py:363
  52.9 2.4 %correlate.2.refs_0_ = f32[2,2,128,512]{3,2,1,0:T(8,128)S(1)} custom-call(bf16[2048,256]{1,0:T(8,128)(2,1)S(1)} %residual.4.refs_0_, bf16[2048,256]{1,0:T(8,128)(2,1)S(1)} %residual.3.refs_1_, bf16[2,512,512]{2,1,0:T(8,128)(2,1)S(1)} %copy-done, bf16[2,512,512]{2,1,0:T(8,128)(2,1)S(1)} %collective-permute-done.12.refs_3_.refs_2_.refs_9_, ...), custom_call_target="tpu_custom_call" | custom-call | flops 1000 | bytes 1000 | tf_op jit(solution)/shard_map/correlate/pallas_call | solution.py:252
  55.3 2.9 %residual.5.refs_0_ = bf16[2048,256]{1,0:T(8,128)(2,1)S(1)} custom-call(s32[10]{0:T(128)S(1)} %pad_add_fusion.1.place, bf16[1040,256]{1,0:T(8,128)(2,1)S(1)} %collective-permute-done.9.refs_0_, bf16[1040,256]{1,0:T(8,128)(2,1)S(1)} %collective-permute-done.7.refs_1_), custom_call_target="tpu_custom_call" | custom-call | flops 1000 | bytes 1000 | tf_op jit(solution)/shard_map/residual/pallas_call | solution.py:186
  58.1 1.3 %correlate.3.refs_1_ = f32[1,2,128,512]{3,2,1,0:T(8,128)S(1)} custom-call(bf16[2048,256]{1,0:T(8,128)(2,1)S(1)} %residual.5.refs_0_, bf16[2,512,512]{2,1,0:T(8,128)(2,1)S(1)} %copy-done, bf16[2,512,512]{2,1,0:T(8,128)(2,1)S(1)} %collective-permute-done.12.refs_3_.refs_2_.refs_9_, bf16[2,512,512]{2,1,0:T(8,128)(2,1)S(1)} %collective-permute-done.13.refs_4_.refs_3_.refs_10_, ...), custom_call_target="tpu_custom_call" | custom-call | flops 1000 | bytes 1000 | tf_op jit(solution)/shard_map/correlate/pallas_call | solution.py:252
  59.4 1.9 %begin.1.refs_2_ = f32[2048,256]{1,0:T(8,128)S(1)} custom-call(s32[10]{0:T(128)S(1)} %pad_add_fusion.1.place, bf16[1040,256]{1,0:T(8,128)(2,1)S(1)} %collective-permute-done.11.refs_0_, bf16[1040,256]{1,0:T(8,128)(2,1)S(1)} %cut.3.refs_1_), custom_call_target="tpu_custom_call" | custom-call | flops 1000 | bytes 1000 | tf_op jit(solution)/shard_map/begin/pallas_call | solution.py:209
  61.3 0.1 collective-permute-start.17
  61.4 1.9 %collective-permute-done.17.refs_5_.refs_7_ = bf16[2,2,128,512]{3,2,1,0:T(8,128)(2,1)S(1)} collective-permute-done((bf16[2,2,128,512]{3,2,1,0:T(8,128)(2,1)S(1)}, bf16[2,2,128,512]{3,2,1,0:T(8,128)(2,1)S(1)}, u32[]{:S(2)}, u32[]{:S(2)}) %collective-permute-start.17) | collective-permute-done | bytes 524320 | tf_op jit(solution)/shard_map/ppermute | solution.py:363
  63.3 2.0 %fold.1.refs_3_ = f32[1,512]{1,0:T(1,128)S(1)} custom-call(s32[10]{0:T(128)S(1)} %pad_add_fusion.1.place, f32[2,2,128,512]{3,2,1,0:T(8,128)S(1)} %correlate.2.refs_0_, f32[1,2,128,512]{3,2,1,0:T(8,128)S(1)} %correlate.3.refs_1_, bf16[2,2,128,512]{3,2,1,0:T(8,128)(2,1)S(1)} %get-tuple-element.29.refs_2_.refs_4_, ...), custom_call_target="tpu_custom_call" | custom-call | flops 1000 | bytes 1000 | tf_op jit(solution)/shard_map/fold/pallas_call | solution.py:297
  65.3 3.5 %last.1 = f32[1,512]{1,0:T(1,128)S(1)} custom-call(s32[10]{0:T(128)S(1)} %pad_add_fusion.1.place, bf16[1040,256]{1,0:T(8,128)(2,1)S(1)} %collective-permute-done.10.refs_0_, bf16[1040,256]{1,0:T(8,128)(2,1)S(1)} %join.1.refs_1_, f32[2048,256]{1,0:T(8,128)S(1)} %begin.1.refs_2_, f32[1,512]{1,0:T(1,128)S(1)} %fold.1.refs_3_, ...), custom_call_target="tpu_custom_call" | custom-call | flops 1000 | bytes 1000 | tf_op jit(solution)/shard_map/last/pallas_call | solution.py:332
  68.7 0.2 collective-permute-start.18
  69.0 1.5 %collective-permute-start.19 = (f32[512]{0:T(512)S(1)}, f32[512]{0:T(512)S(1)}, u32[]{:S(2)}, u32[]{:S(2)}) collective-permute-start(f32[512]{0:T(512)S(1)} %bitcast.17), channel_id=1, source_target_pairs={{0,16},{2,18},{4,20},{6,22},{1,17},{3,19},{5,21},{7,23},{8,24},{10... | collective-permute-start | bytes 6152 | tf_op jit(solution)/shard_map/ppermute | solution.py:363
  70.5 0.2 collective-permute-start.20
  70.7 1.9 %collective-permute-done.19 = f32[512]{0:T(512)S(1)} collective-permute-done((f32[512]{0:T(512)S(1)}, f32[512]{0:T(512)S(1)}, u32[]{:S(2)}, u32[]{:S(2)}) %collective-permute-start.19) | collective-permute-done | bytes 2080 | tf_op jit(solution)/shard_map/ppermute | solution.py:363
  72.6 0.9 %collective-permute-done.20 = f32[512]{0:T(512)S(1)} collective-permute-done((f32[512]{0:T(512)S(1)}, f32[512]{0:T(512)S(1)}, u32[]{:S(2)}, u32[]{:S(2)}) %collective-permute-start.20) | collective-permute-done | bytes 2080 | tf_op jit(solution)/shard_map/ppermute | solution.py:363
  73.5 0.6 add_add_fusion
  (23 shorter events, 0.1 us)
Async XLA Ops:
  0.0 12.1 %copy-start = (bf16[2,512,512]{2,1,0:T(8,128)(2,1)S(1)}, bf16[2,512,512]{2,1,0:T(8,128)(2,1)}, u32[]{:S(2)}) copy-start(bf16[2,512,512]{2,1,0:T(8,128)(2,1)} %refs_8_.1) | copy-start | bytes 3145732
  0.0 6.2 %collective-permute-start.2 = (bf16[512,512]{1,0:T(8,128)(2,1)}, bf16[512,512]{1,0:T(8,128)(2,1)S(1)}, u32[]{:S(2)}, u32[]{:S(2)}) collective-permute-start(bf16[512,512]{1,0:T(8,128)(2,1)} %bitcast.12), channel_id=1, source_target_pairs={{0,8},{2,10},{4,12},{6,14},{1,9},{3,11},{5,13},{7,15},{8,0},{10,2}... | collective-permute-start | bytes 1572872 | tf_op jit(solution)/shard_map/ppermute | solution.py:363
  1.2 1.0 %copy-start.1 = (bf16[1,512,512]{2,1,0:T(8,128)(2,1)S(1)}, bf16[1,512,512]{2,1,0:T(8,128)(2,1)}, u32[]{:S(2)}) copy-start(bf16[1,512,512]{2,1,0:T(8,128)(2,1)} %param.6) | copy-start | bytes 1572868
  2.4 9.7 %collective-permute-start = (bf16[528,256]{1,0:T(8,128)(2,1)S(1)}, bf16[528,256]{1,0:T(8,128)(2,1)S(1)}, u32[]{:S(2)}, u32[]{:S(2)}) collective-permute-start(bf16[528,256]{1,0:T(8,128)(2,1)S(1)} %cut.2), channel_id=1, source_target_pairs={{0,16},{2,18},{4,20},{6,22},{1,17},{3,19},{5,21},{7,23},{8,24},{10... | collective-permute-start | bytes 811016 | tf_op jit(solution)/shard_map/ppermute | solution.py:363
  5.0 1.2 %collective-permute-start.3 = (bf16[16,512]{1,0:T(8,128)(2,1)S(1)}, bf16[16,512]{1,0:T(8,128)(2,1)S(1)}, u32[]{:S(2)}, u32[]{:S(2)}) collective-permute-start(bf16[16,512]{1,0:T(8,128)(2,1)S(1)} %fusion.2.refs_1_.refs_2_), channel_id=1, source_target_pairs={{0,8},{2,10},{4,12},{6,14},{1,9},{3,11},{5,13},{7,15},{8,0},{10,2}... | collective-permute-start | bytes 49160 | tf_op jit(solution)/shard_map/ppermute | solution.py:363
  6.2 1.0 %copy-start.2 = (bf16[1,512,512]{2,1,0:T(8,128)(2,1)S(1)}, bf16[1,512,512]{2,1,0:T(8,128)(2,1)}, u32[]{:S(2)}) copy-start(bf16[1,512,512]{2,1,0:T(8,128)(2,1)} %param.6) | copy-start | bytes 1572868
  7.4 9.4 %collective-permute-start.4 = (bf16[1040,256]{1,0:T(8,128)(2,1)S(1)}, bf16[1040,256]{1,0:T(8,128)(2,1)}, u32[]{:S(2)}, u32[]{:S(2)}) collective-permute-start(bf16[1040,256]{1,0:T(8,128)(2,1)S(1)} %cut.3.refs_1_), channel_id=1, source_target_pairs={{0,9},{6,15},{1,8},{7,14},{16,25},{22,31},{17,24},{23,30},{8,10},{... | collective-permute-start | bytes 1597448 | tf_op jit(solution)/shard_map/ppermute | solution.py:363
  12.1 25.0 %collective-permute-start.13 = (bf16[2,512,512]{2,1,0:T(8,128)(2,1)S(1)}, bf16[2,512,512]{2,1,0:T(8,128)(2,1)S(1)}, u32[]{:S(2)}, u32[]{:S(2)}) collective-permute-start(bf16[2,512,512]{2,1,0:T(8,128)(2,1)S(1)} %copy-done), channel_id=1, source_target_pairs={{0,16},{2,18},{4,20},{6,22},{1,17},{3,19},{5,21},{7,23},{8,24},{10... | collective-permute-start | bytes 3145736 | tf_op jit(solution)/shard_map/ppermute | solution.py:363
  13.8 1.5 %collective-permute-start.1 = (bf16[528,256]{1,0:T(8,128)(2,1)S(1)}, bf16[528,256]{1,0:T(8,128)(2,1)S(1)}, u32[]{:S(2)}, u32[]{:S(2)}) collective-permute-start(bf16[528,256]{1,0:T(8,128)(2,1)S(1)} %collective-permute-done.mine), channel_id=1, source_target_pairs={{0,8},{2,10},{4,12},{6,14},{1,9},{3,11},{5,13},{7,15},{8,0},{10,2}... | collective-permute-start | bytes 811016 | tf_op jit(solution)/shard_map/ppermute | solution.py:363
  16.9 9.4 %collective-permute-start.5 = (bf16[1040,256]{1,0:T(8,128)(2,1)S(1)}, bf16[1040,256]{1,0:T(8,128)(2,1)}, u32[]{:S(2)}, u32[]{:S(2)}) collective-permute-start(bf16[1040,256]{1,0:T(8,128)(2,1)S(1)} %join.1.refs_1_), channel_id=1, source_target_pairs={{0,9},{6,15},{1,8},{7,14},{16,25},{22,31},{17,24},{23,30},{8,10},{... | collective-permute-start | bytes 1597448 | tf_op jit(solution)/shard_map/ppermute | solution.py:363
  17.9 14.1 %collective-permute-start.8 = (bf16[1040,256]{1,0:T(8,128)(2,1)}, bf16[1040,256]{1,0:T(8,128)(2,1)}, u32[]{:S(2)}, u32[]{:S(2)}) collective-permute-start(bf16[1040,256]{1,0:T(8,128)(2,1)} %collective-permute-done.4.refs_0_), channel_id=1, source_target_pairs={{0,9},{6,15},{1,8},{7,14},{16,25},{22,31},{17,24},{23,30},{8,2},{1... | collective-permute-start | bytes 1597448 | tf_op jit(solution)/shard_map/ppermute | solution.py:363
  19.5 26.4 %copy-start.3 = (bf16[2,512,512]{2,1,0:T(8,128)(2,1)S(1)}, bf16[2,512,512]{2,1,0:T(8,128)(2,1)}, u32[]{:S(2)}) copy-start(bf16[2,512,512]{2,1,0:T(8,128)(2,1)} %param.10) | copy-start | bytes 3145732
  26.3 13.6 %collective-permute-start.6 = (bf16[1040,256]{1,0:T(8,128)(2,1)}, bf16[1040,256]{1,0:T(8,128)(2,1)S(1)}, u32[]{:S(2)}, u32[]{:S(2)}) collective-permute-start(bf16[1040,256]{1,0:T(8,128)(2,1)} %collective-permute-done.5.refs_1_), channel_id=1, source_target_pairs={{0,9},{6,15},{1,8},{7,14},{16,25},{22,31},{17,24},{23,30},{8,2},{1... | collective-permute-start | bytes 1597448 | tf_op jit(solution)/shard_map/ppermute | solution.py:363
  32.0 11.3 %collective-permute-start.9 = (bf16[1040,256]{1,0:T(8,128)(2,1)}, bf16[1040,256]{1,0:T(8,128)(2,1)S(1)}, u32[]{:S(2)}, u32[]{:S(2)}) collective-permute-start(bf16[1040,256]{1,0:T(8,128)(2,1)} %collective-permute-done.8.refs_0_), channel_id=1, source_target_pairs={{0,9},{6,15},{1,8},{7,14},{16,25},{22,31},{17,24},{23,30},{8,10},{... | collective-permute-start | bytes 1597448 | tf_op jit(solution)/shard_map/ppermute | solution.py:363
  32.8 18.0 %collective-permute-start.12 = (bf16[2,512,512]{2,1,0:T(8,128)(2,1)S(1)}, bf16[2,512,512]{2,1,0:T(8,128)(2,1)S(1)}, u32[]{:S(2)}, u32[]{:S(2)}) collective-permute-start(bf16[2,512,512]{2,1,0:T(8,128)(2,1)S(1)} %copy-done), channel_id=1, source_target_pairs={{0,8},{2,10},{4,12},{6,14},{1,9},{3,11},{5,13},{7,15},{8,0},{10,2}... | collective-permute-start | bytes 3145736 | tf_op jit(solution)/shard_map/ppermute | solution.py:363
  37.1 15.8 %collective-permute-start.14 = (bf16[2,512,512]{2,1,0:T(8,128)(2,1)S(1)}, bf16[2,512,512]{2,1,0:T(8,128)(2,1)S(1)}, u32[]{:S(2)}, u32[]{:S(2)}) collective-permute-start(bf16[2,512,512]{2,1,0:T(8,128)(2,1)S(1)} %collective-permute-done.13.refs_4_.refs_3_.refs_10_), channel_id=1, source_target_pairs={{0,8},{2,10},{4,12},{6,14},{1,9},{3,11},{5,13},{7,15},{8,0},{10,2}... | collective-permute-start | bytes 3145736 | tf_op jit(solution)/shard_map/ppermute | solution.py:363
  39.9 10.1 %collective-permute-start.7 = (bf16[1040,256]{1,0:T(8,128)(2,1)S(1)}, bf16[1040,256]{1,0:T(8,128)(2,1)S(1)}, u32[]{:S(2)}, u32[]{:S(2)}) collective-permute-start(bf16[1040,256]{1,0:T(8,128)(2,1)S(1)} %collective-permute-done.6.refs_1_), channel_id=1, source_target_pairs={{0,9},{6,15},{1,8},{7,14},{16,25},{22,31},{17,24},{23,30},{8,10},{... | collective-permute-start | bytes 1597448 | tf_op jit(solution)/shard_map/ppermute | solution.py:363
  43.3 16.2 %collective-permute-start.11 = (bf16[1040,256]{1,0:T(8,128)(2,1)S(1)}, bf16[1040,256]{1,0:T(8,128)(2,1)S(1)}, u32[]{:S(2)}, u32[]{:S(2)}) collective-permute-start(bf16[1040,256]{1,0:T(8,128)(2,1)S(1)} %collective-permute-done.9.refs_0_), channel_id=1, source_target_pairs={{0,9},{6,15},{1,8},{7,14},{16,25},{22,31},{17,24},{23,30},{10,12},... | collective-permute-start | bytes 1597448 | tf_op jit(solution)/shard_map/ppermute | solution.py:363
  46.0 15.3 %collective-permute-start.16 = (bf16[2,2,128,512]{3,2,1,0:T(8,128)(2,1)S(1)}, bf16[2,2,128,512]{3,2,1,0:T(8,128)(2,1)S(1)}, u32[]{:S(2)}, u32[]{:S(2)}) collective-permute-start(bf16[2,2,128,512]{3,2,1,0:T(8,128)(2,1)S(1)} %get-tuple-element.31), channel_id=1, source_target_pairs={{0,16},{2,18},{4,20},{6,22},{1,17},{3,19},{5,21},{7,23},{8,24},{10... | collective-permute-start | bytes 1572872 | tf_op jit(solution)/shard_map/ppermute | solution.py:363
  50.0 15.3 %collective-permute-start.10 = (bf16[1040,256]{1,0:T(8,128)(2,1)S(1)}, bf16[1040,256]{1,0:T(8,128)(2,1)S(1)}, u32[]{:S(2)}, u32[]{:S(2)}) collective-permute-start(bf16[1040,256]{1,0:T(8,128)(2,1)S(1)} %collective-permute-done.7.refs_1_), channel_id=1, source_target_pairs={{8,10},{14,12},{9,11},{15,13},{24,26},{30,28},{25,27},{31,29},{2,8... | collective-permute-start | bytes 1597448 | tf_op jit(solution)/shard_map/ppermute | solution.py:363
  50.7 10.7 %collective-permute-start.15 = (bf16[2,2,128,512]{3,2,1,0:T(8,128)(2,1)S(1)}, bf16[2,2,128,512]{3,2,1,0:T(8,128)(2,1)S(1)}, u32[]{:S(2)}, u32[]{:S(2)}) collective-permute-start(bf16[2,2,128,512]{3,2,1,0:T(8,128)(2,1)S(1)} %get-tuple-element.29.refs_2_.refs_4_), channel_id=1, source_target_pairs={{0,8},{2,10},{4,12},{6,14},{1,9},{3,11},{5,13},{7,15},{8,0},{10,2}... | collective-permute-start | bytes 1572872 | tf_op jit(solution)/shard_map/ppermute | solution.py:363
  61.3 2.0 %collective-permute-start.17 = (bf16[2,2,128,512]{3,2,1,0:T(8,128)(2,1)S(1)}, bf16[2,2,128,512]{3,2,1,0:T(8,128)(2,1)S(1)}, u32[]{:S(2)}, u32[]{:S(2)}) collective-permute-start(bf16[2,2,128,512]{3,2,1,0:T(8,128)(2,1)S(1)} %collective-permute-done.16.refs_4_.refs_6_), channel_id=1, source_target_pairs={{0,8},{2,10},{4,12},{6,14},{1,9},{3,11},{5,13},{7,15},{8,0},{10,2}... | collective-permute-start | bytes 1572872 | tf_op jit(solution)/shard_map/ppermute | solution.py:363
  68.7 1.9 %collective-permute-start.18 = (f32[512]{0:T(512)S(1)}, f32[512]{0:T(512)S(1)}, u32[]{:S(2)}, u32[]{:S(2)}) collective-permute-start(f32[512]{0:T(512)S(1)} %bitcast.16), channel_id=1, source_target_pairs={{0,8},{2,10},{4,12},{6,14},{1,9},{3,11},{5,13},{7,15},{8,0},{10,2}... | collective-permute-start | bytes 6152 | tf_op jit(solution)/shard_map/ppermute | solution.py:363
  69.0 3.6 %collective-permute-start.19 = (f32[512]{0:T(512)S(1)}, f32[512]{0:T(512)S(1)}, u32[]{:S(2)}, u32[]{:S(2)}) collective-permute-start(f32[512]{0:T(512)S(1)} %bitcast.17), channel_id=1, source_target_pairs={{0,16},{2,18},{4,20},{6,22},{1,17},{3,19},{5,21},{7,23},{8,24},{10... | collective-permute-start | bytes 6152 | tf_op jit(solution)/shard_map/ppermute | solution.py:363
  70.5 3.0 %collective-permute-start.20 = (f32[512]{0:T(512)S(1)}, f32[512]{0:T(512)S(1)}, u32[]{:S(2)}, u32[]{:S(2)}) collective-permute-start(f32[512]{0:T(512)S(1)} %bitcast.18), channel_id=1, source_target_pairs={{0,24},{2,26},{4,28},{6,30},{1,25},{3,27},{5,29},{7,31},{8,16},{10... | collective-permute-start | bytes 6152 | tf_op jit(solution)/shard_map/ppermute | solution.py:363

commit v4 on v3

--- a/solution.py
+++ b/solution.py
@@ -18,35 +18,22 @@
     return pltpu.CompilerParams(vmem_limit_bytes=VMEM_LIMIT)
 
 
-def light():
-    return pl.CostEstimate(flops=1000, bytes_accessed=1000, transcendentals=0)
+def light(name):
+    return pl.CostEstimate(
+        flops=COSTS.get(name, 1000), bytes_accessed=1000, transcendentals=0
+    )
 
 
 SMEM_SPEC = pl.BlockSpec(memory_space=pltpu.SMEM)
 VMEM_SPEC = pl.BlockSpec(memory_space=pltpu.VMEM)
 
 
+COSTS = {}
+ORDER = {'r1_b': ('r1_a',), 'r4_a': ('res_1',), 'r4_b': ('res_2',), 'res_1': ('r2_a',), 'res_2': ('r3_a',), 'field_core': ('r1_a',), 'field_x': ('crossed_here',), 'field_far': ('res_1',), 'halves': ('r1_a',), 'far': ('r3_a',), 'res_3': ('early',), 'far_core': ('res_3',), }
+
+
 def number(x, c, y, z, n_src):
     return (2 * x + c) * n_src + 2 * z + y
-
-
-def id_rows(trace_owner, trace_source, sources_here):
-    per = sources_here // TILE
-    ids = trace_source[0]
-    high = trace_owner[0, :, 0] * per + ids // TILE
-    rows = jnp.stack([high, ids % TILE])
-    return jnp.pad(rows, ((0, PAD - 2), (0, 0))).astype(jnp.bfloat16)
-
-
-def id_block(ids, kinds):
-    pieces = [
-        rows[kind : kind + 1, j * TILE : (j + 1) * TILE]
-        for kind in kinds
-        for rows in ids
-        for j in range(rows.shape[1] // TILE)
-    ]
-    pad = jnp.zeros((PAD - len(pieces), TILE), jnp.bfloat16)
-    return jnp.concatenate(pieces + [pad], axis=0)
 
 
 def receivers(values, first, rows, out_ref, spot):
@@ -58,35 +45,44 @@
         out_ref[pl.ds(spot, rows), lanes] = jnp.where(first, low, high)
 
 
-def cut_kernel(n, place, *refs):
-    values, ids, (out_ref, mine, sem) = refs[:n], refs[n : 2 * n], refs[2 * n :]
-    copy = pltpu.make_async_copy(values[0], mine, sem)
-    copy.start()
-    rows = mine.shape[0]
-    out_ref[n * rows :, :] = id_block(ids, range(2))
-    for k in range(1, n):
-        receivers(values[k], place[0] == 0, rows, out_ref, k * rows)
-    copy.wait()
-    receivers(mine, place[0] == 0, rows, out_ref, 0)
-
-
-def cut(half, values, ids):
-    rows, width = values[0].shape
-    n = len(values)
-    return pl.pallas_call(
-        functools.partial(cut_kernel, n),
+def id_rows(trace_owner, trace_source, sources_here):
+    ids = trace_source[0]
+    high = trace_owner[0, :, 0] * (sources_here // TILE) + ids // TILE
+    rows = jnp.stack([high, ids % TILE])
+    return jnp.pad(rows, ((0, PAD - 2), (0, 0))).astype(jnp.bfloat16)
+
+
+def cut_kernel(place, values, ids, near_ref, away_ref):
+    rows = values.shape[0]
+    first = place[0] == 0
+    receivers(values, first, rows, near_ref, 0)
+    receivers(values, jnp.logical_not(first), rows, away_ref, 0)
+    tiles = rows // TILE
+    block = jnp.concatenate(
+        [
+            ids[kind : kind + 1, j * TILE : (j + 1) * TILE]
+            for kind in range(2)
+            for j in range(tiles)
+        ]
+        + [jnp.zeros((PAD - 2 * tiles, TILE), jnp.bfloat16)],
+        axis=0,
+    )
+    near_ref[rows:, :] = block
+    away_ref[rows:, :] = block
+
+
+def cut(place, values, ids):
+    rows, width = values.shape
+    shape = jax.ShapeDtypeStruct((rows + PAD, width // 2), jnp.bfloat16)
+    return pl.pallas_call(
+        cut_kernel,
         name="cut",
-        out_shape=jax.ShapeDtypeStruct((n * rows + PAD, width // 2), jnp.bfloat16),
-        in_specs=[SMEM_SPEC, pl.BlockSpec(memory_space=pltpu.HBM)]
-        + [VMEM_SPEC] * (2 * n - 1),
-        out_specs=VMEM_SPEC,
-        scratch_shapes=[
-            pltpu.VMEM(values[0].shape, jnp.bfloat16),
-            pltpu.SemaphoreType.DMA,
-        ],
-        compiler_params=params(),
-        cost_estimate=light(),
-    )(half, *values, *ids)
+        out_shape=(shape, shape),
+        in_specs=[SMEM_SPEC] + [VMEM_SPEC] * 2,
+        out_specs=(VMEM_SPEC, VMEM_SPEC),
+        compiler_params=params(),
+        cost_estimate=light("cut"),
+    )(place, values, ids)
 
 
 def join_kernel(mine, other, out_ref):
@@ -109,7 +105,7 @@
         in_specs=[VMEM_SPEC] * 2,
         out_specs=VMEM_SPEC,
         compiler_params=params(),
-        cost_estimate=light(),
+        cost_estimate=light("join"),
     )(mine, other)
 
 
@@ -131,7 +127,7 @@
         in_specs=[SMEM_SPEC, VMEM_SPEC],
         out_specs=(VMEM_SPEC, VMEM_SPEC),
         compiler_params=params(),
-        cost_estimate=light(),
+        cost_estimate=light("halves"),
     )(place, blocks)
 
 
@@ -190,7 +186,7 @@
         in_specs=[SMEM_SPEC] + [VMEM_SPEC] * len(pieces),
         out_specs=VMEM_SPEC,
         compiler_params=params(),
-        cost_estimate=light(),
+        cost_estimate=light("residual"),
     )(place, *pieces)
 
 
@@ -214,7 +210,7 @@
         out_specs=VMEM_SPEC,
         scratch_shapes=[pltpu.VMEM(shape, jnp.bfloat16), pltpu.SemaphoreType.DMA],
         compiler_params=params(),
-        cost_estimate=light(),
+        cost_estimate=light("begin"),
     )(place, *cand)
 
 
@@ -256,7 +252,7 @@
         in_specs=[VMEM_SPEC] * (len(res) + len(fields)),
         out_specs=VMEM_SPEC,
         compiler_params=params(),
-        cost_estimate=light(),
+        cost_estimate=light("correlate"),
     )(*res, *fields)
 
 
@@ -305,7 +301,7 @@
             pltpu.SemaphoreType.DMA((slots, 2)),
         ],
         compiler_params=params(),
-        cost_estimate=light(),
+        cost_estimate=light("fold"),
     )(place, *factors, *greens)
 
 
@@ -343,7 +339,7 @@
             pltpu.SemaphoreType.DMA((2,)),
         ],
         compiler_params=params(),
-        cost_estimate=light(),
+        cost_estimate=light("last"),
     )(place, *cand_b, begun, folded, *greens, *fields)
 
 
@@ -372,12 +368,12 @@
     def after(array, *earlier):
         return lax.optimization_barrier((array, *earlier))[0]
 
-    other = send(values, to_core)
-    mine_ids = id_rows(trace_owner, trace_source, sources_here)
-    other_ids = send(mine_ids, to_core)
     place_x = jnp.stack([x]).astype(jnp.int32)
-    crossed_here = send(cut(1 - place_x, (values,), (mine_ids,)), to_x)
-    own = cut(place_x, (values, other), (mine_ids, other_ids))
+    ids = id_rows(trace_owner, trace_source, sources_here)
+    kept, away = cut(place_x, values, ids)
+    kept_core = send(kept, to_core)
+    own = join(kept, kept_core)
+    crossed_here = after(send(away, to_x), own)
     crossed = join(crossed_here, send(crossed_here, to_core))
 
     moves = []
@@ -422,37 +418,62 @@
     ).astype(jnp.int32)
     sources = 4 * sources_here
 
-    def touch(array):
-        return array[:8, :128]
-
-    r1_a = send(own, moves[0])
-    r2_a = send(r1_a, moves[1])
-    r1_b = send(after(crossed, r1_a), moves[0])
-    r3_a = send(r2_a, moves[2])
-    r2_b = send(after(r1_b, touch(r2_a)), moves[1])
-    res_1 = residual(place, (r1_a, after(r1_b, r2_a)), sources)
-    r4_a = send(after(r3_a, res_1), moves[3])
-    r3_b = send(after(r2_b, touch(r3_a)), moves[2])
-    res_2 = residual(place, (r2_a, after(r2_b, r3_a)), sources)
-    begun = begin(place, (r4_a, own), sources)
-    r4_b = send(after(r3_b, res_2), moves[4])
-
-    field_core = send(after(source_fields, r1_a), to_core)
-    field_x = send(after(source_fields, crossed_here), to_x)
-    field_far = send(after(field_x, res_1), to_core)
-    fields = (source_fields, field_core, field_x, field_far)
-
     blocks = green_fields.reshape(2, 2, 2, -1, green_fields.shape[2])
-    near, away_green = halves(place_x, after(blocks, r1_a))
-    far = send(after(away_green, r2_b), to_x)
-
-    res_3 = residual(place, (r3_a, r3_b), sources)
-    early = correlated((res_1, res_2), fields)
-    middle = correlated((after(res_3, early),), fields)
-    far_core = send(after(far, middle, begun), to_core)
-    greens = (near, send(near, to_core), far, far_core)
-    folded = fold(place, (early, middle), greens)
-    partial = last(place, (r4_b, crossed), begun, folded, greens, fields)[0]
+    made = {"own": own, "crossed": crossed, "crossed_here": crossed_here}
+    steps = {}
+
+    def get(name):
+        if name not in made:
+            made[name] = None
+            made[name] = steps[name]()
+        return made[name]
+
+    def behind(name, array):
+        return after(array, *[get(k) for k in ORDER.get(name, ())])
+
+    steps["r1_a"] = lambda: send(own, moves[0])
+    steps["r2_a"] = lambda: send(behind("r2_a", get("r1_a")), moves[1])
+    steps["r3_a"] = lambda: send(behind("r3_a", get("r2_a")), moves[2])
+    steps["r4_a"] = lambda: send(behind("r4_a", get("r3_a")), moves[3])
+    steps["r1_b"] = lambda: send(behind("r1_b", crossed), moves[0])
+    steps["r2_b"] = lambda: send(behind("r2_b", get("r1_b")), moves[1])
+    steps["r3_b"] = lambda: send(behind("r3_b", get("r2_b")), moves[2])
+    steps["r4_b"] = lambda: send(behind("r4_b", get("r3_b")), moves[4])
+    steps["res_1"] = lambda: residual(
+        place, (get("r1_a"), behind("res_1", get("r1_b"))), sources
+    )
+    steps["res_2"] = lambda: residual(
+        place, (get("r2_a"), behind("res_2", get("r2_b"))), sources
+    )
+    steps["res_3"] = lambda: residual(
+        place, (get("r3_a"), behind("res_3", get("r3_b"))), sources
+    )
+    steps["begun"] = lambda: begin(place, (behind("begun", get("r4_a")), own), sources)
+    steps["field_core"] = lambda: send(behind("field_core", source_fields), to_core)
+    steps["field_x"] = lambda: send(behind("field_x", source_fields), to_x)
+    steps["field_far"] = lambda: send(behind("field_far", get("field_x")), to_core)
+    steps["halves"] = lambda: halves(place_x, behind("halves", blocks))
+    steps["near"] = lambda: get("halves")[0]
+    steps["away"] = lambda: get("halves")[1]
+    steps["near_core"] = lambda: send(behind("near_core", get("near")), to_core)
+    steps["far"] = lambda: send(behind("far", get("away")), to_x)
+    steps["far_core"] = lambda: send(behind("far_core", get("far")), to_core)
+    steps["fields"] = lambda: (
+        source_fields, get("field_core"), get("field_x"), get("field_far")
+    )
+    steps["early"] = lambda: correlated(
+        (get("res_1"), behind("early", get("res_2"))), get("fields")
+    )
+    steps["middle"] = lambda: correlated(
+        (behind("middle", get("res_3")),), get("fields")
+    )
+    greens = [get(k) for k in ("near", "near_core", "far", "far_core")]
+    folded = fold(
+        place, (get("early"), behind("fold", get("middle"))), greens
+    )
+    partial = last(
+        place, (get("r4_b"), crossed), get("begun"), folded, greens, get("fields")
+    )[0]
     here = partial + send(partial, to_core)
     there = send(partial, to_x) + send(partial, to_both)
     return here + there

time: 74.4 us -> 70.8 us (0.952)
  waiting for transfers between devices: 30.7 us -> 26.3 us
  starting transfers between devices: 17.7 us -> 19.6 us
  local copies, waits for them, and re-layouts: 2.95 us -> 1.9 us
    ppermute x21 -> x20, waiting for transfers between devices: 30.7 us -> 26.3 us  [send(): return lax.ppermute(array, AXES, pairs)]
    ppermute x21 -> x20, starting transfers between devices: 17.7 us -> 19.6 us  [send(): return lax.ppermute(array, AXES, pairs)]
    unnamed x8 -> x6, local copies, waits for them, and re-layouts: 2.09 us -> 1.04 us
  transfers between devices with their start and end apart: 21 -> 20, of which waited for: 12 -> 9; matrix products, arithmetic and copies ran while one was open for 2% -> 1% of each run, Pallas kernels for 24% -> 25%
where the time goes in v4:
time: 70.8 us; the launch traced here: 70.6 us
  waiting for transfers between devices  26.3 us (37%)
  Pallas kernels  21 us (30%)
  starting transfers between devices  19.6 us (28%)
  local copies, waits for them, and re-layouts  1.9 us (3%)
  other arithmetic  1.5 us (2%)
    ppermute x20, waiting for transfers between devices, send(): return lax.ppermute(array, AXES, pairs)  26.3 us
    ppermute x20, starting transfers between devices, send(): return lax.ppermute(array, AXES, pairs)  19.6 us
    pallas_call x3, Pallas kernels, residual(): pl.pallas_call(functools.partial(residual_kernel, len(pieces)), name='res...  9.78 us
    pallas_call x2, Pallas kernels, correlated(): pl.pallas_call(functools.partial(correlate_kernel, len(res)), name='corre...  3.67 us
    pallas_call x1, Pallas kernels, last(): pl.pallas_call(functools.partial(last_kernel, len(cand_b)), name='last',...  3.47 us
    pallas_call x1, Pallas kernels, fold(): pl.pallas_call(functools.partial(fold_kernel, len(factors)), name='fold',...  1.95 us
    pallas_call x1, Pallas kernels, begin(): pl.pallas_call(functools.partial(begin_kernel, len(cand)), name='begin',...  1.86 us
  transfers between devices with their start and end apart: 20, of which 9 were waited for; matrix products, arithmetic and copies ran while one was open for 1% of the time, Pallas kernels for 25%

profile of v4, /device:TPU:0, one launch (start us, length us, event | category | flops | bytes accessed | tf_op | source)
XLA Modules:
  0.0 70.6 jit_solution(5478643120163950851)
XLA Ops:
  0.0 0.8 %fusion.4 = (bf16[1,512]{1,0:T(2,128)(2,1)S(1)}, bf16[1,512]{1,0:T(2,128)(2,1)S(1)}) fusion(s32[1,512,1]{1,2,0:T(1,128)} %param.7, s32[1,512]{1,0:T(1,128)} %param.8), kind=kLoop, calls=%fused_computation.11 | loop fusion | flops 11776 | bytes 6144 | tf_op jit(solution)/shard_map/convert.2
  0.8 0.0 copy-start.2
  0.8 1.0 %copy-done.2 = bf16[1,512,512]{2,1,0:T(8,128)(2,1)S(1)} copy-done((bf16[1,512,512]{2,1,0:T(8,128)(2,1)S(1)}, bf16[1,512,512]{2,1,0:T(8,128)(2,1)}, u32[]{:S(2)}) %copy-start.2) | copy-done | bytes 524312
  1.9 0.1 cut.1
  2.0 0.5 collective-permute-start.1
  2.5 2.6 %collective-permute-start = (bf16[528,256]{1,0:T(8,128)(2,1)S(1)}, bf16[528,256]{1,0:T(8,128)(2,1)S(1)}, u32[]{:S(2)}, u32[]{:S(2)}) collective-permute-start(bf16[528,256]{1,0:T(8,128)(2,1)S(1)} %get-tuple-element.22), channel_id=1, source_target_pairs={{0,16},{2,18},{4,20},{6,22},{1,17},{3,19},{5,21},{7,23},{8,24},{10... | collective-permute-start | bytes 811016 | tf_op jit(solution)/shard_map/ppermute | solution.py:359
  5.1 0.0 collective-permute-done.1.other
  5.2 1.4 %collective-permute-start.3 = (bf16[1040,256]{1,0:T(8,128)(2,1)S(1)}, bf16[1040,256]{1,0:T(8,128)(2,1)}, u32[]{:S(2)}, u32[]{:S(2)}) collective-permute-start(bf16[1040,256]{1,0:T(8,128)(2,1)S(1)} %join.2.refs_1_), channel_id=1, source_target_pairs={{0,9},{6,15},{1,8},{7,14},{16,25},{22,31},{17,24},{23,30},{8,10},{... | collective-permute-start | bytes 1597448 | tf_op jit(solution)/shard_map/ppermute | solution.py:359
  6.5 5.7 %collective-permute-done.mine = bf16[528,256]{1,0:T(8,128)(2,1)S(1)} collective-permute-done((bf16[528,256]{1,0:T(8,128)(2,1)S(1)}, bf16[528,256]{1,0:T(8,128)(2,1)S(1)}, u32[]{:S(2)}, u32[]{:S(2)}) %collective-permute-start) | collective-permute-done | bytes 270368 | tf_op jit(solution)/shard_map/ppermute | solution.py:359
  12.2 1.8 %collective-permute-start.12 = (bf16[2,512,512]{2,1,0:T(8,128)(2,1)}, bf16[2,512,512]{2,1,0:T(8,128)(2,1)S(1)}, u32[]{:S(2)}, u32[]{:S(2)}) collective-permute-start(bf16[2,512,512]{2,1,0:T(8,128)(2,1)} %refs_8_.1), channel_id=1, source_target_pairs={{0,16},{2,18},{4,20},{6,22},{1,17},{3,19},{5,21},{7,23},{8,24},{10... | collective-permute-start | bytes 3145736 | tf_op jit(solution)/shard_map/ppermute | solution.py:359
  13.9 0.0 collective-permute-start.2
  13.9 1.5 %collective-permute-done.2.other = bf16[528,256]{1,0:T(8,128)(2,1)S(1)} collective-permute-done((bf16[528,256]{1,0:T(8,128)(2,1)S(1)}, bf16[528,256]{1,0:T(8,128)(2,1)S(1)}, u32[]{:S(2)}, u32[]{:S(2)}) %collective-permute-start.2) | collective-permute-done | bytes 270368 | tf_op jit(solution)/shard_map/ppermute | solution.py:359
  15.5 0.0 collective-permute-done.3.refs_0_
  15.5 1.3 %collective-permute-start.4 = (bf16[1040,256]{1,0:T(8,128)(2,1)S(1)}, bf16[1040,256]{1,0:T(8,128)(2,1)}, u32[]{:S(2)}, u32[]{:S(2)}) collective-permute-start(bf16[1040,256]{1,0:T(8,128)(2,1)S(1)} %join.3.refs_1_), channel_id=1, source_target_pairs={{0,9},{6,15},{1,8},{7,14},{16,25},{22,31},{17,24},{23,30},{8,10},{... | collective-permute-start | bytes 1597448 | tf_op jit(solution)/shard_map/ppermute | solution.py:359
  16.9 1.3 %collective-permute-start.7 = (bf16[1040,256]{1,0:T(8,128)(2,1)}, bf16[1040,256]{1,0:T(8,128)(2,1)}, u32[]{:S(2)}, u32[]{:S(2)}) collective-permute-start(bf16[1040,256]{1,0:T(8,128)(2,1)} %collective-permute-done.3.refs_0_), channel_id=1, source_target_pairs={{0,9},{6,15},{1,8},{7,14},{16,25},{22,31},{17,24},{23,30},{8,2},{1... | collective-permute-start | bytes 1597448 | tf_op jit(solution)/shard_map/ppermute | solution.py:359
  18.2 0.7 dynamic-slice_bitcast_fusion
  18.9 0.1 copy.8
  19.0 0.1 reshape.20
  19.0 5.9 %collective-permute-done.4.refs_1_ = bf16[1040,256]{1,0:T(8,128)(2,1)} collective-permute-done((bf16[1040,256]{1,0:T(8,128)(2,1)S(1)}, bf16[1040,256]{1,0:T(8,128)(2,1)}, u32[]{:S(2)}, u32[]{:S(2)}) %collective-permute-start.4) | collective-permute-done | bytes 532512 | tf_op jit(solution)/shard_map/ppermute | solution.py:359
  25.0 1.0 %collective-permute-start.5 = (bf16[1040,256]{1,0:T(8,128)(2,1)}, bf16[1040,256]{1,0:T(8,128)(2,1)S(1)}, u32[]{:S(2)}, u32[]{:S(2)}) collective-permute-start(bf16[1040,256]{1,0:T(8,128)(2,1)} %collective-permute-done.4.refs_1_), channel_id=1, source_target_pairs={{0,9},{6,15},{1,8},{7,14},{16,25},{22,31},{17,24},{23,30},{8,2},{1... | collective-permute-start | bytes 1597448 | tf_op jit(solution)/shard_map/ppermute | solution.py:359
  26.0 4.7 %collective-permute-done.7.refs_0_ = bf16[1040,256]{1,0:T(8,128)(2,1)} collective-permute-done((bf16[1040,256]{1,0:T(8,128)(2,1)}, bf16[1040,256]{1,0:T(8,128)(2,1)}, u32[]{:S(2)}, u32[]{:S(2)}) %collective-permute-start.7) | collective-permute-done | bytes 532512 | tf_op jit(solution)/shard_map/ppermute | solution.py:359
  30.7 1.0 %collective-permute-start.8 = (bf16[1040,256]{1,0:T(8,128)(2,1)}, bf16[1040,256]{1,0:T(8,128)(2,1)S(1)}, u32[]{:S(2)}, u32[]{:S(2)}) collective-permute-start(bf16[1040,256]{1,0:T(8,128)(2,1)} %collective-permute-done.7.refs_0_), channel_id=1, source_target_pairs={{0,9},{6,15},{1,8},{7,14},{16,25},{22,31},{17,24},{23,30},{8,10},{... | collective-permute-start | bytes 1597448 | tf_op jit(solution)/shard_map/ppermute | solution.py:359
  31.7 0.1 pad_add_fusion.1.place
  31.7 0.0 collective-permute-start.11
  31.8 3.5 %residual.4.refs_0_ = bf16[2048,256]{1,0:T(8,128)(2,1)S(1)} custom-call(s32[10]{0:T(128)S(1)} %pad_add_fusion.1.place, bf16[1040,256]{1,0:T(8,128)(2,1)} %collective-permute-done.3.refs_0_, bf16[1040,256]{1,0:T(8,128)(2,1)} %collective-permute-done.4.refs_1_), custom_call_target="tpu_custom_call" | custom-call | flops 1000 | bytes 1000 | tf_op jit(solution)/shard_map/residual/pallas_call | solution.py:182
  35.3 2.1 %collective-permute-done.12.refs_4_.refs_3_.refs_10_ = bf16[2,512,512]{2,1,0:T(8,128)(2,1)S(1)} collective-permute-done((bf16[2,512,512]{2,1,0:T(8,128)(2,1)}, bf16[2,512,512]{2,1,0:T(8,128)(2,1)S(1)}, u32[]{:S(2)}, u32[]{:S(2)}) %collective-permute-start.12) | collective-permute-done | bytes 1048608 | tf_op jit(solution)/shard_map/ppermute | solution.py:359
  37.4 1.2 %collective-permute-done.5.refs_1_ = bf16[1040,256]{1,0:T(8,128)(2,1)S(1)} collective-permute-done((bf16[1040,256]{1,0:T(8,128)(2,1)}, bf16[1040,256]{1,0:T(8,128)(2,1)S(1)}, u32[]{:S(2)}, u32[]{:S(2)}) %collective-permute-start.5) | collective-permute-done | bytes 532512 | tf_op jit(solution)/shard_map/ppermute | solution.py:359
  38.6 0.5 collective-permute-start.6
  39.1 0.1 halves.1
  39.2 2.8 %collective-permute-done.8.refs_0_ = bf16[1040,256]{1,0:T(8,128)(2,1)S(1)} collective-permute-done((bf16[1040,256]{1,0:T(8,128)(2,1)}, bf16[1040,256]{1,0:T(8,128)(2,1)S(1)}, u32[]{:S(2)}, u32[]{:S(2)}) %collective-permute-start.8) | collective-permute-done | bytes 532512 | tf_op jit(solution)/shard_map/ppermute | solution.py:359
  42.0 0.5 collective-permute-start.15
  42.4 2.7 %collective-permute-start.10 = (bf16[1040,256]{1,0:T(8,128)(2,1)S(1)}, bf16[1040,256]{1,0:T(8,128)(2,1)S(1)}, u32[]{:S(2)}, u32[]{:S(2)}) collective-permute-start(bf16[1040,256]{1,0:T(8,128)(2,1)S(1)} %collective-permute-done.8.refs_0_), channel_id=1, source_target_pairs={{0,9},{6,15},{1,8},{7,14},{16,25},{22,31},{17,24},{23,30},{10,12},... | collective-permute-start | bytes 1597448 | tf_op jit(solution)/shard_map/ppermute | solution.py:359
  45.2 3.4 %residual.3.refs_1_ = bf16[2048,256]{1,0:T(8,128)(2,1)S(1)} custom-call(s32[10]{0:T(128)S(1)} %pad_add_fusion.1.place, bf16[1040,256]{1,0:T(8,128)(2,1)} %collective-permute-done.7.refs_0_, bf16[1040,256]{1,0:T(8,128)(2,1)S(1)} %collective-permute-done.5.refs_1_), custom_call_target="tpu_custom_call" | custom-call | flops 1000 | bytes 1000 | tf_op jit(solution)/shard_map/residual/pallas_call | solution.py:182
  48.6 0.7 collective-permute-start.9
  49.3 2.2 %collective-permute-start.14 = (bf16[2,2,128,512]{3,2,1,0:T(8,128)(2,1)S(1)}, bf16[2,2,128,512]{3,2,1,0:T(8,128)(2,1)S(1)}, u32[]{:S(2)}, u32[]{:S(2)}) collective-permute-start(bf16[2,2,128,512]{3,2,1,0:T(8,128)(2,1)S(1)} %get-tuple-element.35.refs_2_.refs_4_), channel_id=1, source_target_pairs={{0,8},{2,10},{4,12},{6,14},{1,9},{3,11},{5,13},{7,15},{8,0},{10,2}... | collective-permute-start | bytes 1572872 | tf_op jit(solution)/shard_map/ppermute | solution.py:359
  51.5 2.4 %correlate.2.refs_0_ = f32[2,2,128,512]{3,2,1,0:T(8,128)S(1)} custom-call(bf16[2048,256]{1,0:T(8,128)(2,1)S(1)} %residual.4.refs_0_, bf16[2048,256]{1,0:T(8,128)(2,1)S(1)} %residual.3.refs_1_, bf16[2,512,512]{2,1,0:T(8,128)(2,1)S(1)} %copy-done, bf16[2,512,512]{2,1,0:T(8,128)(2,1)S(1)} %collective-permute-done.11.refs_3_.refs_2_.refs_9_, ...), custom_call_target="tpu_custom_call" | custom-call | flops 1000 | bytes 1000 | tf_op jit(solution)/shard_map/correlate/pallas_call | solution.py:248
  53.8 2.9 %residual.5.refs_0_ = bf16[2048,256]{1,0:T(8,128)(2,1)S(1)} custom-call(s32[10]{0:T(128)S(1)} %pad_add_fusion.1.place, bf16[1040,256]{1,0:T(8,128)(2,1)S(1)} %collective-permute-done.8.refs_0_, bf16[1040,256]{1,0:T(8,128)(2,1)S(1)} %collective-permute-done.6.refs_1_), custom_call_target="tpu_custom_call" | custom-call | flops 1000 | bytes 1000 | tf_op jit(solution)/shard_map/residual/pallas_call | solution.py:182
  56.7 0.1 collective-permute-start.16
  56.8 1.9 %begin.1.refs_2_ = f32[2048,256]{1,0:T(8,128)S(1)} custom-call(s32[10]{0:T(128)S(1)} %pad_add_fusion.1.place, bf16[1040,256]{1,0:T(8,128)(2,1)S(1)} %collective-permute-done.10.refs_0_, bf16[1040,256]{1,0:T(8,128)(2,1)S(1)} %join.2.refs_1_), custom_call_target="tpu_custom_call" | custom-call | flops 1000 | bytes 1000 | tf_op jit(solution)/shard_map/begin/pallas_call | solution.py:205
  58.7 1.3 %correlate.3.refs_1_ = f32[1,2,128,512]{3,2,1,0:T(8,128)S(1)} custom-call(bf16[2048,256]{1,0:T(8,128)(2,1)S(1)} %residual.5.refs_0_, bf16[2,512,512]{2,1,0:T(8,128)(2,1)S(1)} %copy-done, bf16[2,512,512]{2,1,0:T(8,128)(2,1)S(1)} %collective-permute-done.11.refs_3_.refs_2_.refs_9_, bf16[2,512,512]{2,1,0:T(8,128)(2,1)S(1)} %collective-permute-done.12.refs_4_.refs_3_.refs_10_, ...), custom_call_target="tpu_custom_call" | custom-call | flops 1000 | bytes 1000 | tf_op jit(solution)/shard_map/correlate/pallas_call | solution.py:248
  60.0 2.0 %fold.1.refs_3_ = f32[1,512]{1,0:T(1,128)S(1)} custom-call(s32[10]{0:T(128)S(1)} %pad_add_fusion.1.place, f32[2,2,128,512]{3,2,1,0:T(8,128)S(1)} %correlate.2.refs_0_, f32[1,2,128,512]{3,2,1,0:T(8,128)S(1)} %correlate.3.refs_1_, bf16[2,2,128,512]{3,2,1,0:T(8,128)(2,1)S(1)} %get-tuple-element.35.refs_2_.refs_4_, ...), custom_call_target="tpu_custom_call" | custom-call | flops 1000 | bytes 1000 | tf_op jit(solution)/shard_map/fold/pallas_call | solution.py:293
  62.0 3.5 %last.1 = f32[1,512]{1,0:T(1,128)S(1)} custom-call(s32[10]{0:T(128)S(1)} %pad_add_fusion.1.place, bf16[1040,256]{1,0:T(8,128)(2,1)S(1)} %collective-permute-done.9.refs_0_, bf16[1040,256]{1,0:T(8,128)(2,1)S(1)} %join.3.refs_1_, f32[2048,256]{1,0:T(8,128)S(1)} %begin.1.refs_2_, f32[1,512]{1,0:T(1,128)S(1)} %fold.1.refs_3_, ...), custom_call_target="tpu_custom_call" | custom-call | flops 1000 | bytes 1000 | tf_op jit(solution)/shard_map/last/pallas_call | solution.py:328
  65.4 1.6 %collective-permute-start.18 = (f32[512]{0:T(512)S(1)}, f32[512]{0:T(512)S(1)}, u32[]{:S(2)}, u32[]{:S(2)}) collective-permute-start(f32[512]{0:T(512)S(1)} %bitcast.14), channel_id=1, source_target_pairs={{0,16},{2,18},{4,20},{6,22},{1,17},{3,19},{5,21},{7,23},{8,24},{10... | collective-permute-start | bytes 6152 | tf_op jit(solution)/shard_map/ppermute | solution.py:359
  67.0 0.3 collective-permute-start.19
  67.3 0.3 collective-permute-start.17
  67.6 1.4 %collective-permute-done.18 = f32[512]{0:T(512)S(1)} collective-permute-done((f32[512]{0:T(512)S(1)}, f32[512]{0:T(512)S(1)}, u32[]{:S(2)}, u32[]{:S(2)}) %collective-permute-start.18) | collective-permute-done | bytes 2080 | tf_op jit(solution)/shard_map/ppermute | solution.py:359
  69.1 0.9 %collective-permute-done.19 = f32[512]{0:T(512)S(1)} collective-permute-done((f32[512]{0:T(512)S(1)}, f32[512]{0:T(512)S(1)}, u32[]{:S(2)}, u32[]{:S(2)}) %collective-permute-start.19) | collective-permute-done | bytes 2080 | tf_op jit(solution)/shard_map/ppermute | solution.py:359
  70.0 0.6 add_add_fusion
  (19 shorter events, 0.1 us)
Async XLA Ops:
  0.0 31.7 %copy-start = (bf16[2,512,512]{2,1,0:T(8,128)(2,1)S(1)}, bf16[2,512,512]{2,1,0:T(8,128)(2,1)}, u32[]{:S(2)}) copy-start(bf16[2,512,512]{2,1,0:T(8,128)(2,1)} %refs_8_.1) | copy-start | bytes 3145732
  0.8 1.0 %copy-start.2 = (bf16[1,512,512]{2,1,0:T(8,128)(2,1)S(1)}, bf16[1,512,512]{2,1,0:T(8,128)(2,1)}, u32[]{:S(2)}) copy-start(bf16[1,512,512]{2,1,0:T(8,128)(2,1)} %param.6) | copy-start | bytes 1572868
  2.0 3.1 %collective-permute-start.1 = (bf16[528,256]{1,0:T(8,128)(2,1)S(1)}, bf16[528,256]{1,0:T(8,128)(2,1)S(1)}, u32[]{:S(2)}, u32[]{:S(2)}) collective-permute-start(bf16[528,256]{1,0:T(8,128)(2,1)S(1)} %get-tuple-element.23.mine), channel_id=1, source_target_pairs={{0,8},{2,10},{4,12},{6,14},{1,9},{3,11},{5,13},{7,15},{8,0},{10,2}... | collective-permute-start | bytes 811016 | tf_op jit(solution)/shard_map/ppermute | solution.py:359
  2.5 9.6 %collective-permute-start = (bf16[528,256]{1,0:T(8,128)(2,1)S(1)}, bf16[528,256]{1,0:T(8,128)(2,1)S(1)}, u32[]{:S(2)}, u32[]{:S(2)}) collective-permute-start(bf16[528,256]{1,0:T(8,128)(2,1)S(1)} %get-tuple-element.22), channel_id=1, source_target_pairs={{0,16},{2,18},{4,20},{6,22},{1,17},{3,19},{5,21},{7,23},{8,24},{10... | collective-permute-start | bytes 811016 | tf_op jit(solution)/shard_map/ppermute | solution.py:359
  5.2 10.4 %collective-permute-start.3 = (bf16[1040,256]{1,0:T(8,128)(2,1)S(1)}, bf16[1040,256]{1,0:T(8,128)(2,1)}, u32[]{:S(2)}, u32[]{:S(2)}) collective-permute-start(bf16[1040,256]{1,0:T(8,128)(2,1)S(1)} %join.2.refs_1_), channel_id=1, source_target_pairs={{0,9},{6,15},{1,8},{7,14},{16,25},{22,31},{17,24},{23,30},{8,10},{... | collective-permute-start | bytes 1597448 | tf_op jit(solution)/shard_map/ppermute | solution.py:359
  12.2 25.2 %collective-permute-start.12 = (bf16[2,512,512]{2,1,0:T(8,128)(2,1)}, bf16[2,512,512]{2,1,0:T(8,128)(2,1)S(1)}, u32[]{:S(2)}, u32[]{:S(2)}) collective-permute-start(bf16[2,512,512]{2,1,0:T(8,128)(2,1)} %refs_8_.1), channel_id=1, source_target_pairs={{0,16},{2,18},{4,20},{6,22},{1,17},{3,19},{5,21},{7,23},{8,24},{10... | collective-permute-start | bytes 3145736 | tf_op jit(solution)/shard_map/ppermute | solution.py:359
  13.9 1.5 %collective-permute-start.2 = (bf16[528,256]{1,0:T(8,128)(2,1)S(1)}, bf16[528,256]{1,0:T(8,128)(2,1)S(1)}, u32[]{:S(2)}, u32[]{:S(2)}) collective-permute-start(bf16[528,256]{1,0:T(8,128)(2,1)S(1)} %collective-permute-done.mine), channel_id=1, source_target_pairs={{0,8},{2,10},{4,12},{6,14},{1,9},{3,11},{5,13},{7,15},{8,0},{10,2}... | collective-permute-start | bytes 811016 | tf_op jit(solution)/shard_map/ppermute | solution.py:359
  15.5 9.4 %collective-permute-start.4 = (bf16[1040,256]{1,0:T(8,128)(2,1)S(1)}, bf16[1040,256]{1,0:T(8,128)(2,1)}, u32[]{:S(2)}, u32[]{:S(2)}) collective-permute-start(bf16[1040,256]{1,0:T(8,128)(2,1)S(1)} %join.3.refs_1_), channel_id=1, source_target_pairs={{0,9},{6,15},{1,8},{7,14},{16,25},{22,31},{17,24},{23,30},{8,10},{... | collective-permute-start | bytes 1597448 | tf_op jit(solution)/shard_map/ppermute | solution.py:359
  16.9 13.8 %collective-permute-start.7 = (bf16[1040,256]{1,0:T(8,128)(2,1)}, bf16[1040,256]{1,0:T(8,128)(2,1)}, u32[]{:S(2)}, u32[]{:S(2)}) collective-permute-start(bf16[1040,256]{1,0:T(8,128)(2,1)} %collective-permute-done.3.refs_0_), channel_id=1, source_target_pairs={{0,9},{6,15},{1,8},{7,14},{16,25},{22,31},{17,24},{23,30},{8,2},{1... | collective-permute-start | bytes 1597448 | tf_op jit(solution)/shard_map/ppermute | solution.py:359
  19.0 20.1 %copy-start.1 = (bf16[2,512,512]{2,1,0:T(8,128)(2,1)S(1)}, bf16[2,512,512]{2,1,0:T(8,128)(2,1)}, u32[]{:S(2)}) copy-start(bf16[2,512,512]{2,1,0:T(8,128)(2,1)} %param.10) | copy-start | bytes 3145732
  25.0 13.6 %collective-permute-start.5 = (bf16[1040,256]{1,0:T(8,128)(2,1)}, bf16[1040,256]{1,0:T(8,128)(2,1)S(1)}, u32[]{:S(2)}, u32[]{:S(2)}) collective-permute-start(bf16[1040,256]{1,0:T(8,128)(2,1)} %collective-permute-done.4.refs_1_), channel_id=1, source_target_pairs={{0,9},{6,15},{1,8},{7,14},{16,25},{22,31},{17,24},{23,30},{8,2},{1... | collective-permute-start | bytes 1597448 | tf_op jit(solution)/shard_map/ppermute | solution.py:359
  30.7 11.3 %collective-permute-start.8 = (bf16[1040,256]{1,0:T(8,128)(2,1)}, bf16[1040,256]{1,0:T(8,128)(2,1)S(1)}, u32[]{:S(2)}, u32[]{:S(2)}) collective-permute-start(bf16[1040,256]{1,0:T(8,128)(2,1)} %collective-permute-done.7.refs_0_), channel_id=1, source_target_pairs={{0,9},{6,15},{1,8},{7,14},{16,25},{22,31},{17,24},{23,30},{8,10},{... | collective-permute-start | bytes 1597448 | tf_op jit(solution)/shard_map/ppermute | solution.py:359
  31.7 17.5 %collective-permute-start.11 = (bf16[2,512,512]{2,1,0:T(8,128)(2,1)S(1)}, bf16[2,512,512]{2,1,0:T(8,128)(2,1)S(1)}, u32[]{:S(2)}, u32[]{:S(2)}) collective-permute-start(bf16[2,512,512]{2,1,0:T(8,128)(2,1)S(1)} %copy-done), channel_id=1, source_target_pairs={{0,8},{2,10},{4,12},{6,14},{1,9},{3,11},{5,13},{7,15},{8,0},{10,2}... | collective-permute-start | bytes 3145736 | tf_op jit(solution)/shard_map/ppermute | solution.py:359
  37.4 14.0 %collective-permute-start.13 = (bf16[2,512,512]{2,1,0:T(8,128)(2,1)S(1)}, bf16[2,512,512]{2,1,0:T(8,128)(2,1)S(1)}, u32[]{:S(2)}, u32[]{:S(2)}) collective-permute-start(bf16[2,512,512]{2,1,0:T(8,128)(2,1)S(1)} %collective-permute-done.12.refs_4_.refs_3_.refs_10_), channel_id=1, source_target_pairs={{0,8},{2,10},{4,12},{6,14},{1,9},{3,11},{5,13},{7,15},{8,0},{10,2}... | collective-permute-start | bytes 3145736 | tf_op jit(solution)/shard_map/ppermute | solution.py:359
  38.6 9.9 %collective-permute-start.6 = (bf16[1040,256]{1,0:T(8,128)(2,1)S(1)}, bf16[1040,256]{1,0:T(8,128)(2,1)S(1)}, u32[]{:S(2)}, u32[]{:S(2)}) collective-permute-start(bf16[1040,256]{1,0:T(8,128)(2,1)S(1)} %collective-permute-done.5.refs_1_), channel_id=1, source_target_pairs={{0,9},{6,15},{1,8},{7,14},{16,25},{22,31},{17,24},{23,30},{8,10},{... | collective-permute-start | bytes 1597448 | tf_op jit(solution)/shard_map/ppermute | solution.py:359
  42.0 14.7 %collective-permute-start.15 = (bf16[2,2,128,512]{3,2,1,0:T(8,128)(2,1)S(1)}, bf16[2,2,128,512]{3,2,1,0:T(8,128)(2,1)S(1)}, u32[]{:S(2)}, u32[]{:S(2)}) collective-permute-start(bf16[2,2,128,512]{3,2,1,0:T(8,128)(2,1)S(1)} %get-tuple-element.37), channel_id=1, source_target_pairs={{0,16},{2,18},{4,20},{6,22},{1,17},{3,19},{5,21},{7,23},{8,24},{10... | collective-permute-start | bytes 1572872 | tf_op jit(solution)/shard_map/ppermute | solution.py:359
  42.4 14.4 %collective-permute-start.10 = (bf16[1040,256]{1,0:T(8,128)(2,1)S(1)}, bf16[1040,256]{1,0:T(8,128)(2,1)S(1)}, u32[]{:S(2)}, u32[]{:S(2)}) collective-permute-start(bf16[1040,256]{1,0:T(8,128)(2,1)S(1)} %collective-permute-done.8.refs_0_), channel_id=1, source_target_pairs={{0,9},{6,15},{1,8},{7,14},{16,25},{22,31},{17,24},{23,30},{10,12},... | collective-permute-start | bytes 1597448 | tf_op jit(solution)/shard_map/ppermute | solution.py:359
  48.6 13.4 %collective-permute-start.9 = (bf16[1040,256]{1,0:T(8,128)(2,1)S(1)}, bf16[1040,256]{1,0:T(8,128)(2,1)S(1)}, u32[]{:S(2)}, u32[]{:S(2)}) collective-permute-start(bf16[1040,256]{1,0:T(8,128)(2,1)S(1)} %collective-permute-done.6.refs_1_), channel_id=1, source_target_pairs={{8,10},{14,12},{9,11},{15,13},{24,26},{30,28},{25,27},{31,29},{2,8... | collective-permute-start | bytes 1597448 | tf_op jit(solution)/shard_map/ppermute | solution.py:359
  49.3 10.7 %collective-permute-start.14 = (bf16[2,2,128,512]{3,2,1,0:T(8,128)(2,1)S(1)}, bf16[2,2,128,512]{3,2,1,0:T(8,128)(2,1)S(1)}, u32[]{:S(2)}, u32[]{:S(2)}) collective-permute-start(bf16[2,2,128,512]{3,2,1,0:T(8,128)(2,1)S(1)} %get-tuple-element.35.refs_2_.refs_4_), channel_id=1, source_target_pairs={{0,8},{2,10},{4,12},{6,14},{1,9},{3,11},{5,13},{7,15},{8,0},{10,2}... | collective-permute-start | bytes 1572872 | tf_op jit(solution)/shard_map/ppermute | solution.py:359
  56.7 3.3 %collective-permute-start.16 = (bf16[2,2,128,512]{3,2,1,0:T(8,128)(2,1)S(1)}, bf16[2,2,128,512]{3,2,1,0:T(8,128)(2,1)S(1)}, u32[]{:S(2)}, u32[]{:S(2)}) collective-permute-start(bf16[2,2,128,512]{3,2,1,0:T(8,128)(2,1)S(1)} %collective-permute-done.15.refs_4_.refs_6_), channel_id=1, source_target_pairs={{0,8},{2,10},{4,12},{6,14},{1,9},{3,11},{5,13},{7,15},{8,0},{10,2}... | collective-permute-start | bytes 1572872 | tf_op jit(solution)/shard_map/ppermute | solution.py:359
  65.4 3.7 %collective-permute-start.18 = (f32[512]{0:T(512)S(1)}, f32[512]{0:T(512)S(1)}, u32[]{:S(2)}, u32[]{:S(2)}) collective-permute-start(f32[512]{0:T(512)S(1)} %bitcast.14), channel_id=1, source_target_pairs={{0,16},{2,18},{4,20},{6,22},{1,17},{3,19},{5,21},{7,23},{8,24},{10... | collective-permute-start | bytes 6152 | tf_op jit(solution)/shard_map/ppermute | solution.py:359
  67.0 3.0 %collective-permute-start.19 = (f32[512]{0:T(512)S(1)}, f32[512]{0:T(512)S(1)}, u32[]{:S(2)}, u32[]{:S(2)}) collective-permute-start(f32[512]{0:T(512)S(1)} %bitcast.15), channel_id=1, source_target_pairs={{0,24},{2,26},{4,28},{6,30},{1,25},{3,27},{5,29},{7,31},{8,16},{10... | collective-permute-start | bytes 6152 | tf_op jit(solution)/shard_map/ppermute | solution.py:359
  67.3 2.7 %collective-permute-start.17 = (f32[512]{0:T(512)S(1)}, f32[512]{0:T(512)S(1)}, u32[]{:S(2)}, u32[]{:S(2)}) collective-permute-start(f32[512]{0:T(512)S(1)} %bitcast.16), channel_id=1, source_target_pairs={{0,8},{2,10},{4,12},{6,14},{1,9},{3,11},{5,13},{7,15},{8,0},{10,2}... | collective-permute-start | bytes 6152 | tf_op jit(solution)/shard_map/ppermute | solution.py:359

commit v5 on v4

--- a/solution.py
+++ b/solution.py
@@ -18,18 +18,28 @@
     return pltpu.CompilerParams(vmem_limit_bytes=VMEM_LIMIT)
 
 
-def light(name):
-    return pl.CostEstimate(
-        flops=COSTS.get(name, 1000), bytes_accessed=1000, transcendentals=0
-    )
+def light():
+    return pl.CostEstimate(flops=1000, bytes_accessed=1000, transcendentals=0)
 
 
 SMEM_SPEC = pl.BlockSpec(memory_space=pltpu.SMEM)
 VMEM_SPEC = pl.BlockSpec(memory_space=pltpu.VMEM)
 
 
-COSTS = {}
-ORDER = {'r1_b': ('r1_a',), 'r4_a': ('res_1',), 'r4_b': ('res_2',), 'res_1': ('r2_a',), 'res_2': ('r3_a',), 'field_core': ('r1_a',), 'field_x': ('crossed_here',), 'field_far': ('res_1',), 'halves': ('r1_a',), 'far': ('r3_a',), 'res_3': ('early',), 'far_core': ('res_3',), }
+ORDER = {
+    "r4_a": ("res_1",),
+    "r4_b": ("res_2",),
+    "res_1": ("r2_a",),
+    "res_2": ("r3_a",),
+    "field_core": ("r1_a",),
+    "field_x": ("own",),
+    "field_far": ("res_1",),
+    "halves": ("r1_a",),
+    "far": ("r3_a", "near_core",),
+    "res_3": ("early",),
+    "far_core": ("res_3",),
+    "near_core": ("r2_a",),
+}
 
 
 def number(x, c, y, z, n_src):
@@ -81,7 +91,7 @@
         in_specs=[SMEM_SPEC] + [VMEM_SPEC] * 2,
         out_specs=(VMEM_SPEC, VMEM_SPEC),
         compiler_params=params(),
-        cost_estimate=light("cut"),
+        cost_estimate=light(),
     )(place, values, ids)
 
 
@@ -105,7 +115,7 @@
         in_specs=[VMEM_SPEC] * 2,
         out_specs=VMEM_SPEC,
         compiler_params=params(),
-        cost_estimate=light("join"),
+        cost_estimate=light(),
     )(mine, other)
 
 
@@ -127,27 +137,21 @@
         in_specs=[SMEM_SPEC, VMEM_SPEC],
         out_specs=(VMEM_SPEC, VMEM_SPEC),
         compiler_params=params(),
-        cost_estimate=light("halves"),
+        cost_estimate=light(),
     )(place, blocks)
 
 
-def fetch(which, candidates, target, sem):
-    for k, ref in enumerate(candidates):
-
-        @pl.when(which == k)
-        def _(ref=ref):
-            copy = pltpu.make_async_copy(ref, target, sem)
-            copy.start()
-            copy.wait()
-
-
-def assemble(slab, pieces, group, start=None):
+def choose(which, candidates, target):
+    first, second = candidates
+    target[...] = jnp.where(which == 0, first[...], second[...])
+
+
+def assemble(slab, pieces, group, per, start=None):
     traces = pieces[0].shape[0] - PAD
     tiles = traces // TILE
     iota = lax.broadcasted_iota(jnp.int32, (TILE, TILE), 0).astype(jnp.bfloat16)
     out = []
     owner = slab ^ group
-    per = 2
     for h in range(per):
         name = (owner * per + h).astype(jnp.float32).astype(jnp.bfloat16)
         total = None if start is None else start[h * TILE : (h + 1) * TILE, :]
@@ -174,7 +178,7 @@
     rows = out_ref.shape[0] // 4
     for group in range(4):
         out_ref[group * rows : (group + 1) * rows, :] = assemble(
-            place[0], refs[:n], group
+            place[0], refs[:n], group, rows // TILE
         ).astype(out_ref.dtype)
 
 
@@ -186,17 +190,17 @@
         in_specs=[SMEM_SPEC] + [VMEM_SPEC] * len(pieces),
         out_specs=VMEM_SPEC,
         compiler_params=params(),
-        cost_estimate=light("residual"),
+        cost_estimate=light(),
     )(place, *pieces)
 
 
 def begin_kernel(n, place, *refs):
-    cand, (out_ref, piece, sem) = refs[:n], refs[n:]
-    fetch(place[9], cand, piece, sem)
+    cand, (out_ref, piece) = refs[:n], refs[n:]
+    choose(place[9], cand, piece)
     rows = out_ref.shape[0] // 4
     for group in range(4):
         out_ref[group * rows : (group + 1) * rows, :] = assemble(
-            place[0], (piece,), group
+            place[0], (piece,), group, rows // TILE
         )
 
 
@@ -208,9 +212,9 @@
         out_shape=jax.ShapeDtypeStruct((sources, shape[1]), jnp.float32),
         in_specs=[SMEM_SPEC] + [VMEM_SPEC] * len(cand),
         out_specs=VMEM_SPEC,
-        scratch_shapes=[pltpu.VMEM(shape, jnp.bfloat16), pltpu.SemaphoreType.DMA],
-        compiler_params=params(),
-        cost_estimate=light("begin"),
+        scratch_shapes=[pltpu.VMEM(shape, jnp.bfloat16)],
+        compiler_params=params(),
+        cost_estimate=light(),
     )(place, *cand)
 
 
@@ -252,7 +256,7 @@
         in_specs=[VMEM_SPEC] * (len(res) + len(fields)),
         out_specs=VMEM_SPEC,
         compiler_params=params(),
-        cost_estimate=light("correlate"),
+        cost_estimate=light(),
     )(*res, *fields)
 
 
@@ -301,20 +305,24 @@
             pltpu.SemaphoreType.DMA((slots, 2)),
         ],
         compiler_params=params(),
-        cost_estimate=light("fold"),
+        cost_estimate=light(),
     )(place, *factors, *greens)
 
 
 def last_kernel(n_b, place, *refs):
     cand_b, (begun, folded) = refs[:n_b], refs[n_b : n_b + 2]
     greens, fields = refs[n_b + 2 : n_b + 6], refs[n_b + 6 : n_b + 10]
-    out_ref, piece, green, sem, sems = refs[n_b + 10 :]
+    out_ref, piece, green, sems = refs[n_b + 10 :]
     wait = fetch_green(place, 3, greens, green, sems)
-    fetch(place[9], cand_b, piece, sem)
+    choose(place[9], cand_b, piece)
     rows = begun.shape[0] // 4
     parts = [
         assemble(
-            place[0], (piece,), g, begun[g * rows : (g + 1) * rows, :]
+            place[0],
+            (piece,),
+            g,
+            rows // TILE,
+            begun[g * rows : (g + 1) * rows, :],
         ).astype(jnp.bfloat16)
         for g in range(4)
     ]
@@ -335,11 +343,10 @@
         scratch_shapes=[
             pltpu.VMEM(cand_b[0].shape, jnp.bfloat16),
             pltpu.VMEM((2,) + greens[0].shape[2:], jnp.bfloat16),
-            pltpu.SemaphoreType.DMA,
             pltpu.SemaphoreType.DMA((2,)),
         ],
         compiler_params=params(),
-        cost_estimate=light("last"),
+        cost_estimate=light(),
     )(place, *cand_b, begun, folded, *greens, *fields)
 
 

time: 70.8 us -> 69.7 us (0.984)
  waiting for transfers between devices: 26.3 us -> 21.6 us
  starting transfers between devices: 19.6 us -> 22.1 us
  local copies, waits for them, and re-layouts: 1.9 us -> 3.12 us
    ppermute x20, waiting for transfers between devices: 26.3 us -> 21.6 us  [send(): return lax.ppermute(array, AXES, pairs)]
    ppermute x20, starting transfers between devices: 19.6 us -> 22.1 us  [send(): return lax.ppermute(array, AXES, pairs)]
    unnamed x6, local copies, waits for them, and re-layouts: 1.04 us -> 2.26 us
  transfers between devices with their start and end apart: 20 -> 20, of which waited for: 9 -> 8; matrix products, arithmetic and copies ran while one was open for 1% -> 1% of each run, Pallas kernels for 25% -> 25%
where the time goes in v5:
time: 69.7 us; the launch traced here: 69.4 us
  starting transfers between devices  22.1 us (32%)
  waiting for transfers between devices  21.6 us (31%)
  Pallas kernels  20.9 us (30%)
  local copies, waits for them, and re-layouts  3.12 us (4%)
  other arithmetic  1.5 us (2%)
    ppermute x20, starting transfers between devices, send(): return lax.ppermute(array, AXES, pairs)  22.1 us
    ppermute x20, waiting for transfers between devices, send(): return lax.ppermute(array, AXES, pairs)  21.6 us
    pallas_call x3, Pallas kernels, residual(): pl.pallas_call(functools.partial(residual_kernel, len(pieces)), name='res...  9.78 us
    pallas_call x2, Pallas kernels, correlated(): pl.pallas_call(functools.partial(correlate_kernel, len(res)), name='corre...  3.68 us
    pallas_call x1, Pallas kernels, last(): pl.pallas_call(functools.partial(last_kernel, len(cand_b)), name='last',...  3.44 us
    unnamed x6, local copies, waits for them, and re-layouts  2.26 us
    pallas_call x1, Pallas kernels, fold(): pl.pallas_call(functools.partial(fold_kernel, len(factors)), name='fold',...  1.96 us
    pallas_call x1, Pallas kernels, begin(): pl.pallas_call(functools.partial(begin_kernel, len(cand)), name='begin',...  1.79 us
  transfers between devices with their start and end apart: 20, of which 8 were waited for; matrix products, arithmetic and copies ran while one was open for 1% of the time, Pallas kernels for 25%

profile of v5, /device:TPU:0, one launch (start us, length us, event | category | flops | bytes accessed | tf_op | source)
XLA Modules:
  0.0 69.4 jit_solution(16712425925304565326)
XLA Ops:
  0.0 0.8 %fusion.4 = (bf16[1,512]{1,0:T(2,128)(2,1)S(1)}, bf16[1,512]{1,0:T(2,128)(2,1)S(1)}) fusion(s32[1,512,1]{1,2,0:T(1,128)} %param.7, s32[1,512]{1,0:T(1,128)} %param.8), kind=kLoop, calls=%fused_computation.11 | loop fusion | flops 11776 | bytes 6144 | tf_op jit(solution)/shard_map/convert.2
  0.8 0.0 copy-start.2
  0.8 1.0 %copy-done.2 = bf16[1,512,512]{2,1,0:T(8,128)(2,1)S(1)} copy-done((bf16[1,512,512]{2,1,0:T(8,128)(2,1)S(1)}, bf16[1,512,512]{2,1,0:T(8,128)(2,1)}, u32[]{:S(2)}) %copy-start.2) | copy-done | bytes 524312
  1.9 0.1 cut.1
  2.0 0.5 collective-permute-start.1
  2.5 2.6 %collective-permute-start = (bf16[528,256]{1,0:T(8,128)(2,1)S(1)}, bf16[528,256]{1,0:T(8,128)(2,1)S(1)}, u32[]{:S(2)}, u32[]{:S(2)}) collective-permute-start(bf16[528,256]{1,0:T(8,128)(2,1)S(1)} %get-tuple-element.22), channel_id=1, source_target_pairs={{0,16},{2,18},{4,20},{6,22},{1,17},{3,19},{5,21},{7,23},{8,24},{10... | collective-permute-start | bytes 811016 | tf_op jit(solution)/shard_map/ppermute | solution.py:366
  5.2 1.4 %collective-permute-start.6 = (bf16[1040,256]{1,0:T(8,128)(2,1)S(1)}, bf16[1040,256]{1,0:T(8,128)(2,1)}, u32[]{:S(2)}, u32[]{:S(2)}) collective-permute-start(bf16[1040,256]{1,0:T(8,128)(2,1)S(1)} %join.2.refs_1_), channel_id=1, source_target_pairs={{0,9},{6,15},{1,8},{7,14},{16,25},{22,31},{17,24},{23,30},{8,10},{... | collective-permute-start | bytes 1597448 | tf_op jit(solution)/shard_map/ppermute | solution.py:366
  6.5 1.4 %collective-permute-start.12 = (bf16[2,512,512]{2,1,0:T(8,128)(2,1)}, bf16[2,512,512]{2,1,0:T(8,128)(2,1)S(1)}, u32[]{:S(2)}, u32[]{:S(2)}) collective-permute-start(bf16[2,512,512]{2,1,0:T(8,128)(2,1)} %refs_8_.1), channel_id=1, source_target_pairs={{0,16},{2,18},{4,20},{6,22},{1,17},{3,19},{5,21},{7,23},{8,24},{10... | collective-permute-start | bytes 3145736 | tf_op jit(solution)/shard_map/ppermute | solution.py:366
  7.9 4.5 %collective-permute-done.mine = bf16[528,256]{1,0:T(8,128)(2,1)S(1)} collective-permute-done((bf16[528,256]{1,0:T(8,128)(2,1)S(1)}, bf16[528,256]{1,0:T(8,128)(2,1)S(1)}, u32[]{:S(2)}, u32[]{:S(2)}) %collective-permute-start) | collective-permute-done | bytes 270368 | tf_op jit(solution)/shard_map/ppermute | solution.py:366
  12.4 1.5 %collective-permute-done.2.other = bf16[528,256]{1,0:T(8,128)(2,1)S(1)} collective-permute-done((bf16[528,256]{1,0:T(8,128)(2,1)S(1)}, bf16[528,256]{1,0:T(8,128)(2,1)S(1)}, u32[]{:S(2)}, u32[]{:S(2)}) %collective-permute-start.2) | collective-permute-done | bytes 270368 | tf_op jit(solution)/shard_map/ppermute | solution.py:366
  14.0 1.8 %collective-permute-start.3 = (bf16[1040,256]{1,0:T(8,128)(2,1)S(1)}, bf16[1040,256]{1,0:T(8,128)(2,1)}, u32[]{:S(2)}, u32[]{:S(2)}) collective-permute-start(bf16[1040,256]{1,0:T(8,128)(2,1)S(1)} %join.3.refs_1_), channel_id=1, source_target_pairs={{0,9},{6,15},{1,8},{7,14},{16,25},{22,31},{17,24},{23,30},{8,10},{... | collective-permute-start | bytes 1597448 | tf_op jit(solution)/shard_map/ppermute | solution.py:366
  15.8 1.3 %collective-permute-start.7 = (bf16[1040,256]{1,0:T(8,128)(2,1)}, bf16[1040,256]{1,0:T(8,128)(2,1)}, u32[]{:S(2)}, u32[]{:S(2)}) collective-permute-start(bf16[1040,256]{1,0:T(8,128)(2,1)} %collective-permute-done.6.refs_0_), channel_id=1, source_target_pairs={{0,9},{6,15},{1,8},{7,14},{16,25},{22,31},{17,24},{23,30},{8,2},{1... | collective-permute-start | bytes 1597448 | tf_op jit(solution)/shard_map/ppermute | solution.py:366
  17.1 0.7 dynamic-slice_bitcast_fusion
  17.8 0.1 copy.8
  17.9 0.1 reshape.20
  18.0 5.5 %collective-permute-done.3.refs_1_ = bf16[1040,256]{1,0:T(8,128)(2,1)} collective-permute-done((bf16[1040,256]{1,0:T(8,128)(2,1)S(1)}, bf16[1040,256]{1,0:T(8,128)(2,1)}, u32[]{:S(2)}, u32[]{:S(2)}) %collective-permute-start.3) | collective-permute-done | bytes 532512 | tf_op jit(solution)/shard_map/ppermute | solution.py:366
  23.5 1.4 %collective-permute-start.4 = (bf16[1040,256]{1,0:T(8,128)(2,1)}, bf16[1040,256]{1,0:T(8,128)(2,1)S(1)}, u32[]{:S(2)}, u32[]{:S(2)}) collective-permute-start(bf16[1040,256]{1,0:T(8,128)(2,1)} %collective-permute-done.3.refs_1_), channel_id=1, source_target_pairs={{0,9},{6,15},{1,8},{7,14},{16,25},{22,31},{17,24},{23,30},{8,2},{1... | collective-permute-start | bytes 1597448 | tf_op jit(solution)/shard_map/ppermute | solution.py:366
  24.9 4.3 %collective-permute-done.7.refs_0_ = bf16[1040,256]{1,0:T(8,128)(2,1)} collective-permute-done((bf16[1040,256]{1,0:T(8,128)(2,1)}, bf16[1040,256]{1,0:T(8,128)(2,1)}, u32[]{:S(2)}, u32[]{:S(2)}) %collective-permute-start.7) | collective-permute-done | bytes 532512 | tf_op jit(solution)/shard_map/ppermute | solution.py:366
  29.2 1.4 %collective-permute-start.8 = (bf16[1040,256]{1,0:T(8,128)(2,1)}, bf16[1040,256]{1,0:T(8,128)(2,1)S(1)}, u32[]{:S(2)}, u32[]{:S(2)}) collective-permute-start(bf16[1040,256]{1,0:T(8,128)(2,1)} %collective-permute-done.7.refs_0_), channel_id=1, source_target_pairs={{0,9},{6,15},{1,8},{7,14},{16,25},{22,31},{17,24},{23,30},{8,10},{... | collective-permute-start | bytes 1597448 | tf_op jit(solution)/shard_map/ppermute | solution.py:366
  30.6 0.1 pad_add_fusion.1.place
  30.7 0.0 collective-permute-start.11
  30.7 0.0 copy-start.1
  30.7 1.2 %copy-done.1 = bf16[2,512,512]{2,1,0:T(8,128)(2,1)S(1)} copy-done((bf16[2,512,512]{2,1,0:T(8,128)(2,1)S(1)}, bf16[2,512,512]{2,1,0:T(8,128)(2,1)}, u32[]{:S(2)}) %copy-start.1) | copy-done | bytes 1048600
  31.9 0.1 halves.1
  32.0 3.5 %residual.4.refs_0_ = bf16[2048,256]{1,0:T(8,128)(2,1)S(1)} custom-call(s32[10]{0:T(128)S(1)} %pad_add_fusion.1.place, bf16[1040,256]{1,0:T(8,128)(2,1)} %collective-permute-done.6.refs_0_, bf16[1040,256]{1,0:T(8,128)(2,1)} %collective-permute-done.3.refs_1_), custom_call_target="tpu_custom_call" | custom-call | flops 1000 | bytes 1000 | tf_op jit(solution)/shard_map/residual/pallas_call | solution.py:186
  35.6 0.6 collective-permute-start.14
  36.1 0.1 collective-permute-start.13
  36.2 0.9 %collective-permute-done.4.refs_1_ = bf16[1040,256]{1,0:T(8,128)(2,1)S(1)} collective-permute-done((bf16[1040,256]{1,0:T(8,128)(2,1)}, bf16[1040,256]{1,0:T(8,128)(2,1)S(1)}, u32[]{:S(2)}, u32[]{:S(2)}) %collective-permute-start.4) | collective-permute-done | bytes 532512 | tf_op jit(solution)/shard_map/ppermute | solution.py:366
  37.1 0.0 collective-permute-start.5
  37.1 0.5 collective-permute-done.14.refs_3_.refs_5_
  37.7 2.8 %collective-permute-done.8.refs_0_ = bf16[1040,256]{1,0:T(8,128)(2,1)S(1)} collective-permute-done((bf16[1040,256]{1,0:T(8,128)(2,1)}, bf16[1040,256]{1,0:T(8,128)(2,1)S(1)}, u32[]{:S(2)}, u32[]{:S(2)}) %collective-permute-start.8) | collective-permute-done | bytes 532512 | tf_op jit(solution)/shard_map/ppermute | solution.py:366
  40.5 1.9 %collective-permute-start.15 = (bf16[2,2,128,512]{3,2,1,0:T(8,128)(2,1)S(1)}, bf16[2,2,128,512]{3,2,1,0:T(8,128)(2,1)S(1)}, u32[]{:S(2)}, u32[]{:S(2)}) collective-permute-start(bf16[2,2,128,512]{3,2,1,0:T(8,128)(2,1)S(1)} %get-tuple-element.37), channel_id=1, source_target_pairs={{0,16},{2,18},{4,20},{6,22},{1,17},{3,19},{5,21},{7,23},{8,24},{10... | collective-permute-start | bytes 1572872 | tf_op jit(solution)/shard_map/ppermute | solution.py:366
  42.4 2.6 %collective-permute-start.10 = (bf16[1040,256]{1,0:T(8,128)(2,1)S(1)}, bf16[1040,256]{1,0:T(8,128)(2,1)S(1)}, u32[]{:S(2)}, u32[]{:S(2)}) collective-permute-start(bf16[1040,256]{1,0:T(8,128)(2,1)S(1)} %collective-permute-done.8.refs_0_), channel_id=1, source_target_pairs={{0,9},{6,15},{1,8},{7,14},{16,25},{22,31},{17,24},{23,30},{10,12},... | collective-permute-start | bytes 1597448 | tf_op jit(solution)/shard_map/ppermute | solution.py:366
  45.1 3.4 %residual.3.refs_1_ = bf16[2048,256]{1,0:T(8,128)(2,1)S(1)} custom-call(s32[10]{0:T(128)S(1)} %pad_add_fusion.1.place, bf16[1040,256]{1,0:T(8,128)(2,1)} %collective-permute-done.7.refs_0_, bf16[1040,256]{1,0:T(8,128)(2,1)S(1)} %collective-permute-done.4.refs_1_), custom_call_target="tpu_custom_call" | custom-call | flops 1000 | bytes 1000 | tf_op jit(solution)/shard_map/residual/pallas_call | solution.py:186
  48.4 0.0 collective-permute-done.5.refs_1_
  48.5 0.7 %collective-permute-start.9 = (bf16[1040,256]{1,0:T(8,128)(2,1)S(1)}, bf16[1040,256]{1,0:T(8,128)(2,1)S(1)}, u32[]{:S(2)}, u32[]{:S(2)}) collective-permute-start(bf16[1040,256]{1,0:T(8,128)(2,1)S(1)} %collective-permute-done.5.refs_1_), channel_id=1, source_target_pairs={{8,10},{14,12},{9,11},{15,13},{24,26},{30,28},{25,27},{31,29},{2,8... | collective-permute-start | bytes 1597448 | tf_op jit(solution)/shard_map/ppermute | solution.py:366
  49.2 2.4 %correlate.2.refs_0_ = f32[2,2,128,512]{3,2,1,0:T(8,128)S(1)} custom-call(bf16[2048,256]{1,0:T(8,128)(2,1)S(1)} %residual.4.refs_0_, bf16[2048,256]{1,0:T(8,128)(2,1)S(1)} %residual.3.refs_1_, bf16[2,512,512]{2,1,0:T(8,128)(2,1)S(1)} %copy-done, bf16[2,512,512]{2,1,0:T(8,128)(2,1)S(1)} %collective-permute-done.11.refs_3_.refs_2_.refs_9_, ...), custom_call_target="tpu_custom_call" | custom-call | flops 1000 | bytes 1000 | tf_op jit(solution)/shard_map/correlate/pallas_call | solution.py:252
  51.6 2.9 %residual.5.refs_0_ = bf16[2048,256]{1,0:T(8,128)(2,1)S(1)} custom-call(s32[10]{0:T(128)S(1)} %pad_add_fusion.1.place, bf16[1040,256]{1,0:T(8,128)(2,1)S(1)} %collective-permute-done.8.refs_0_, bf16[1040,256]{1,0:T(8,128)(2,1)S(1)} %collective-permute-done.5.refs_1_), custom_call_target="tpu_custom_call" | custom-call | flops 1000 | bytes 1000 | tf_op jit(solution)/shard_map/residual/pallas_call | solution.py:186
  54.5 2.2 %collective-permute-start.16 = (bf16[2,2,128,512]{3,2,1,0:T(8,128)(2,1)S(1)}, bf16[2,2,128,512]{3,2,1,0:T(8,128)(2,1)S(1)}, u32[]{:S(2)}, u32[]{:S(2)}) collective-permute-start(bf16[2,2,128,512]{3,2,1,0:T(8,128)(2,1)S(1)} %collective-permute-done.15.refs_4_.refs_6_), channel_id=1, source_target_pairs={{0,8},{2,10},{4,12},{6,14},{1,9},{3,11},{5,13},{7,15},{8,0},{10,2}... | collective-permute-start | bytes 1572872 | tf_op jit(solution)/shard_map/ppermute | solution.py:366
  56.6 1.3 %correlate.3.refs_1_ = f32[1,2,128,512]{3,2,1,0:T(8,128)S(1)} custom-call(bf16[2048,256]{1,0:T(8,128)(2,1)S(1)} %residual.5.refs_0_, bf16[2,512,512]{2,1,0:T(8,128)(2,1)S(1)} %copy-done, bf16[2,512,512]{2,1,0:T(8,128)(2,1)S(1)} %collective-permute-done.11.refs_3_.refs_2_.refs_9_, bf16[2,512,512]{2,1,0:T(8,128)(2,1)S(1)} %collective-permute-done.12.refs_4_.refs_3_.refs_10_, ...), custom_call_target="tpu_custom_call" | custom-call | flops 1000 | bytes 1000 | tf_op jit(solution)/shard_map/correlate/pallas_call | solution.py:252
  57.9 1.8 %begin.1.refs_2_ = f32[2048,256]{1,0:T(8,128)S(1)} custom-call(s32[10]{0:T(128)S(1)} %pad_add_fusion.1.place, bf16[1040,256]{1,0:T(8,128)(2,1)S(1)} %collective-permute-done.10.refs_0_, bf16[1040,256]{1,0:T(8,128)(2,1)S(1)} %join.2.refs_1_), custom_call_target="tpu_custom_call" | custom-call | flops 1000 | bytes 1000 | tf_op jit(solution)/shard_map/begin/pallas_call | solution.py:209
  59.7 2.0 %fold.1.refs_3_ = f32[1,512]{1,0:T(1,128)S(1)} custom-call(s32[10]{0:T(128)S(1)} %pad_add_fusion.1.place, f32[2,2,128,512]{3,2,1,0:T(8,128)S(1)} %correlate.2.refs_0_, f32[1,2,128,512]{3,2,1,0:T(8,128)S(1)} %correlate.3.refs_1_, bf16[2,2,128,512]{3,2,1,0:T(8,128)(2,1)S(1)} %get-tuple-element.35.refs_2_.refs_4_, ...), custom_call_target="tpu_custom_call" | custom-call | flops 1000 | bytes 1000 | tf_op jit(solution)/shard_map/fold/pallas_call | solution.py:297
  61.7 3.4 %last.1 = f32[1,512]{1,0:T(1,128)S(1)} custom-call(s32[10]{0:T(128)S(1)} %pad_add_fusion.1.place, bf16[1040,256]{1,0:T(8,128)(2,1)S(1)} %collective-permute-done.9.refs_0_, bf16[1040,256]{1,0:T(8,128)(2,1)S(1)} %join.3.refs_1_, f32[2048,256]{1,0:T(8,128)S(1)} %begin.1.refs_2_, f32[1,512]{1,0:T(1,128)S(1)} %fold.1.refs_3_, ...), custom_call_target="tpu_custom_call" | custom-call | flops 1000 | bytes 1000 | tf_op jit(solution)/shard_map/last/pallas_call | solution.py:336
  65.2 0.6 collective-permute-start.18
  65.8 0.8 %collective-permute-start.19 = (f32[512]{0:T(512)S(1)}, f32[512]{0:T(512)S(1)}, u32[]{:S(2)}, u32[]{:S(2)}) collective-permute-start(f32[512]{0:T(512)S(1)} %bitcast.15), channel_id=1, source_target_pairs={{0,24},{2,26},{4,28},{6,30},{1,25},{3,27},{5,29},{7,31},{8,16},{10... | collective-permute-start | bytes 6152 | tf_op jit(solution)/shard_map/ppermute | solution.py:366
  66.6 0.8 %collective-permute-start.17 = (f32[512]{0:T(512)S(1)}, f32[512]{0:T(512)S(1)}, u32[]{:S(2)}, u32[]{:S(2)}) collective-permute-start(f32[512]{0:T(512)S(1)} %bitcast.16), channel_id=1, source_target_pairs={{0,8},{2,10},{4,12},{6,14},{1,9},{3,11},{5,13},{7,15},{8,0},{10,2}... | collective-permute-start | bytes 6152 | tf_op jit(solution)/shard_map/ppermute | solution.py:366
  67.4 1.4 %collective-permute-done.18 = f32[512]{0:T(512)S(1)} collective-permute-done((f32[512]{0:T(512)S(1)}, f32[512]{0:T(512)S(1)}, u32[]{:S(2)}, u32[]{:S(2)}) %collective-permute-start.18) | collective-permute-done | bytes 2080 | tf_op jit(solution)/shard_map/ppermute | solution.py:366
  68.8 0.6 add_add_fusion
  (19 shorter events, 0.1 us)
Async XLA Ops:
  0.0 30.7 %copy-start = (bf16[2,512,512]{2,1,0:T(8,128)(2,1)S(1)}, bf16[2,512,512]{2,1,0:T(8,128)(2,1)}, u32[]{:S(2)}) copy-start(bf16[2,512,512]{2,1,0:T(8,128)(2,1)} %refs_8_.1) | copy-start | bytes 3145732
  0.8 1.0 %copy-start.2 = (bf16[1,512,512]{2,1,0:T(8,128)(2,1)S(1)}, bf16[1,512,512]{2,1,0:T(8,128)(2,1)}, u32[]{:S(2)}) copy-start(bf16[1,512,512]{2,1,0:T(8,128)(2,1)} %param.6) | copy-start | bytes 1572868
  2.0 3.1 %collective-permute-start.1 = (bf16[528,256]{1,0:T(8,128)(2,1)S(1)}, bf16[528,256]{1,0:T(8,128)(2,1)S(1)}, u32[]{:S(2)}, u32[]{:S(2)}) collective-permute-start(bf16[528,256]{1,0:T(8,128)(2,1)S(1)} %get-tuple-element.23.mine), channel_id=1, source_target_pairs={{0,8},{2,10},{4,12},{6,14},{1,9},{3,11},{5,13},{7,15},{8,0},{10,2}... | collective-permute-start | bytes 811016 | tf_op jit(solution)/shard_map/ppermute | solution.py:366
  2.5 9.9 %collective-permute-start = (bf16[528,256]{1,0:T(8,128)(2,1)S(1)}, bf16[528,256]{1,0:T(8,128)(2,1)S(1)}, u32[]{:S(2)}, u32[]{:S(2)}) collective-permute-start(bf16[528,256]{1,0:T(8,128)(2,1)S(1)} %get-tuple-element.22), channel_id=1, source_target_pairs={{0,16},{2,18},{4,20},{6,22},{1,17},{3,19},{5,21},{7,23},{8,24},{10... | collective-permute-start | bytes 811016 | tf_op jit(solution)/shard_map/ppermute | solution.py:366
  5.2 10.7 %collective-permute-start.6 = (bf16[1040,256]{1,0:T(8,128)(2,1)S(1)}, bf16[1040,256]{1,0:T(8,128)(2,1)}, u32[]{:S(2)}, u32[]{:S(2)}) collective-permute-start(bf16[1040,256]{1,0:T(8,128)(2,1)S(1)} %join.2.refs_1_), channel_id=1, source_target_pairs={{0,9},{6,15},{1,8},{7,14},{16,25},{22,31},{17,24},{23,30},{8,10},{... | collective-permute-start | bytes 1597448 | tf_op jit(solution)/shard_map/ppermute | solution.py:366
  6.5 29.1 %collective-permute-start.12 = (bf16[2,512,512]{2,1,0:T(8,128)(2,1)}, bf16[2,512,512]{2,1,0:T(8,128)(2,1)S(1)}, u32[]{:S(2)}, u32[]{:S(2)}) collective-permute-start(bf16[2,512,512]{2,1,0:T(8,128)(2,1)} %refs_8_.1), channel_id=1, source_target_pairs={{0,16},{2,18},{4,20},{6,22},{1,17},{3,19},{5,21},{7,23},{8,24},{10... | collective-permute-start | bytes 3145736 | tf_op jit(solution)/shard_map/ppermute | solution.py:366
  12.4 1.5 %collective-permute-start.2 = (bf16[528,256]{1,0:T(8,128)(2,1)S(1)}, bf16[528,256]{1,0:T(8,128)(2,1)S(1)}, u32[]{:S(2)}, u32[]{:S(2)}) collective-permute-start(bf16[528,256]{1,0:T(8,128)(2,1)S(1)} %collective-permute-done.mine), channel_id=1, source_target_pairs={{0,8},{2,10},{4,12},{6,14},{1,9},{3,11},{5,13},{7,15},{8,0},{10,2}... | collective-permute-start | bytes 811016 | tf_op jit(solution)/shard_map/ppermute | solution.py:366
  14.0 9.5 %collective-permute-start.3 = (bf16[1040,256]{1,0:T(8,128)(2,1)S(1)}, bf16[1040,256]{1,0:T(8,128)(2,1)}, u32[]{:S(2)}, u32[]{:S(2)}) collective-permute-start(bf16[1040,256]{1,0:T(8,128)(2,1)S(1)} %join.3.refs_1_), channel_id=1, source_target_pairs={{0,9},{6,15},{1,8},{7,14},{16,25},{22,31},{17,24},{23,30},{8,10},{... | collective-permute-start | bytes 1597448 | tf_op jit(solution)/shard_map/ppermute | solution.py:366
  15.8 13.4 %collective-permute-start.7 = (bf16[1040,256]{1,0:T(8,128)(2,1)}, bf16[1040,256]{1,0:T(8,128)(2,1)}, u32[]{:S(2)}, u32[]{:S(2)}) collective-permute-start(bf16[1040,256]{1,0:T(8,128)(2,1)} %collective-permute-done.6.refs_0_), channel_id=1, source_target_pairs={{0,9},{6,15},{1,8},{7,14},{16,25},{22,31},{17,24},{23,30},{8,2},{1... | collective-permute-start | bytes 1597448 | tf_op jit(solution)/shard_map/ppermute | solution.py:366
  23.5 13.6 %collective-permute-start.4 = (bf16[1040,256]{1,0:T(8,128)(2,1)}, bf16[1040,256]{1,0:T(8,128)(2,1)S(1)}, u32[]{:S(2)}, u32[]{:S(2)}) collective-permute-start(bf16[1040,256]{1,0:T(8,128)(2,1)} %collective-permute-done.3.refs_1_), channel_id=1, source_target_pairs={{0,9},{6,15},{1,8},{7,14},{16,25},{22,31},{17,24},{23,30},{8,2},{1... | collective-permute-start | bytes 1597448 | tf_op jit(solution)/shard_map/ppermute | solution.py:366
  29.2 11.3 %collective-permute-start.8 = (bf16[1040,256]{1,0:T(8,128)(2,1)}, bf16[1040,256]{1,0:T(8,128)(2,1)S(1)}, u32[]{:S(2)}, u32[]{:S(2)}) collective-permute-start(bf16[1040,256]{1,0:T(8,128)(2,1)} %collective-permute-done.7.refs_0_), channel_id=1, source_target_pairs={{0,9},{6,15},{1,8},{7,14},{16,25},{22,31},{17,24},{23,30},{8,10},{... | collective-permute-start | bytes 1597448 | tf_op jit(solution)/shard_map/ppermute | solution.py:366
  30.7 18.5 %collective-permute-start.11 = (bf16[2,512,512]{2,1,0:T(8,128)(2,1)S(1)}, bf16[2,512,512]{2,1,0:T(8,128)(2,1)S(1)}, u32[]{:S(2)}, u32[]{:S(2)}) collective-permute-start(bf16[2,512,512]{2,1,0:T(8,128)(2,1)S(1)} %copy-done), channel_id=1, source_target_pairs={{0,8},{2,10},{4,12},{6,14},{1,9},{3,11},{5,13},{7,15},{8,0},{10,2}... | collective-permute-start | bytes 3145736 | tf_op jit(solution)/shard_map/ppermute | solution.py:366
  30.7 1.2 %copy-start.1 = (bf16[2,512,512]{2,1,0:T(8,128)(2,1)S(1)}, bf16[2,512,512]{2,1,0:T(8,128)(2,1)}, u32[]{:S(2)}) copy-start(bf16[2,512,512]{2,1,0:T(8,128)(2,1)} %param.10) | copy-start | bytes 3145732
  35.6 2.1 %collective-permute-start.14 = (bf16[2,2,128,512]{3,2,1,0:T(8,128)(2,1)S(1)}, bf16[2,2,128,512]{3,2,1,0:T(8,128)(2,1)S(1)}, u32[]{:S(2)}, u32[]{:S(2)}) collective-permute-start(bf16[2,2,128,512]{3,2,1,0:T(8,128)(2,1)S(1)} %get-tuple-element.35.refs_2_.refs_4_), channel_id=1, source_target_pairs={{0,8},{2,10},{4,12},{6,14},{1,9},{3,11},{5,13},{7,15},{8,0},{10,2}... | collective-permute-start | bytes 1572872 | tf_op jit(solution)/shard_map/ppermute | solution.py:366
  36.1 13.0 %collective-permute-start.13 = (bf16[2,512,512]{2,1,0:T(8,128)(2,1)S(1)}, bf16[2,512,512]{2,1,0:T(8,128)(2,1)S(1)}, u32[]{:S(2)}, u32[]{:S(2)}) collective-permute-start(bf16[2,512,512]{2,1,0:T(8,128)(2,1)S(1)} %collective-permute-done.12.refs_4_.refs_3_.refs_10_), channel_id=1, source_target_pairs={{0,8},{2,10},{4,12},{6,14},{1,9},{3,11},{5,13},{7,15},{8,0},{10,2}... | collective-permute-start | bytes 3145736 | tf_op jit(solution)/shard_map/ppermute | solution.py:366
  37.1 11.3 %collective-permute-start.5 = (bf16[1040,256]{1,0:T(8,128)(2,1)S(1)}, bf16[1040,256]{1,0:T(8,128)(2,1)S(1)}, u32[]{:S(2)}, u32[]{:S(2)}) collective-permute-start(bf16[1040,256]{1,0:T(8,128)(2,1)S(1)} %collective-permute-done.4.refs_1_), channel_id=1, source_target_pairs={{0,9},{6,15},{1,8},{7,14},{16,25},{22,31},{17,24},{23,30},{8,10},{... | collective-permute-start | bytes 1597448 | tf_op jit(solution)/shard_map/ppermute | solution.py:366
  40.5 14.0 %collective-permute-start.15 = (bf16[2,2,128,512]{3,2,1,0:T(8,128)(2,1)S(1)}, bf16[2,2,128,512]{3,2,1,0:T(8,128)(2,1)S(1)}, u32[]{:S(2)}, u32[]{:S(2)}) collective-permute-start(bf16[2,2,128,512]{3,2,1,0:T(8,128)(2,1)S(1)} %get-tuple-element.37), channel_id=1, source_target_pairs={{0,16},{2,18},{4,20},{6,22},{1,17},{3,19},{5,21},{7,23},{8,24},{10... | collective-permute-start | bytes 1572872 | tf_op jit(solution)/shard_map/ppermute | solution.py:366
  42.4 15.5 %collective-permute-start.10 = (bf16[1040,256]{1,0:T(8,128)(2,1)S(1)}, bf16[1040,256]{1,0:T(8,128)(2,1)S(1)}, u32[]{:S(2)}, u32[]{:S(2)}) collective-permute-start(bf16[1040,256]{1,0:T(8,128)(2,1)S(1)} %collective-permute-done.8.refs_0_), channel_id=1, source_target_pairs={{0,9},{6,15},{1,8},{7,14},{16,25},{22,31},{17,24},{23,30},{10,12},... | collective-permute-start | bytes 1597448 | tf_op jit(solution)/shard_map/ppermute | solution.py:366
  48.5 13.3 %collective-permute-start.9 = (bf16[1040,256]{1,0:T(8,128)(2,1)S(1)}, bf16[1040,256]{1,0:T(8,128)(2,1)S(1)}, u32[]{:S(2)}, u32[]{:S(2)}) collective-permute-start(bf16[1040,256]{1,0:T(8,128)(2,1)S(1)} %collective-permute-done.5.refs_1_), channel_id=1, source_target_pairs={{8,10},{14,12},{9,11},{15,13},{24,26},{30,28},{25,27},{31,29},{2,8... | collective-permute-start | bytes 1597448 | tf_op jit(solution)/shard_map/ppermute | solution.py:366
  54.5 5.3 %collective-permute-start.16 = (bf16[2,2,128,512]{3,2,1,0:T(8,128)(2,1)S(1)}, bf16[2,2,128,512]{3,2,1,0:T(8,128)(2,1)S(1)}, u32[]{:S(2)}, u32[]{:S(2)}) collective-permute-start(bf16[2,2,128,512]{3,2,1,0:T(8,128)(2,1)S(1)} %collective-permute-done.15.refs_4_.refs_6_), channel_id=1, source_target_pairs={{0,8},{2,10},{4,12},{6,14},{1,9},{3,11},{5,13},{7,15},{8,0},{10,2}... | collective-permute-start | bytes 1572872 | tf_op jit(solution)/shard_map/ppermute | solution.py:366
  65.2 3.7 %collective-permute-start.18 = (f32[512]{0:T(512)S(1)}, f32[512]{0:T(512)S(1)}, u32[]{:S(2)}, u32[]{:S(2)}) collective-permute-start(f32[512]{0:T(512)S(1)} %bitcast.14), channel_id=1, source_target_pairs={{0,16},{2,18},{4,20},{6,22},{1,17},{3,19},{5,21},{7,23},{8,24},{10... | collective-permute-start | bytes 6152 | tf_op jit(solution)/shard_map/ppermute | solution.py:366
  65.8 3.0 %collective-permute-start.19 = (f32[512]{0:T(512)S(1)}, f32[512]{0:T(512)S(1)}, u32[]{:S(2)}, u32[]{:S(2)}) collective-permute-start(f32[512]{0:T(512)S(1)} %bitcast.15), channel_id=1, source_target_pairs={{0,24},{2,26},{4,28},{6,30},{1,25},{3,27},{5,29},{7,31},{8,16},{10... | collective-permute-start | bytes 6152 | tf_op jit(solution)/shard_map/ppermute | solution.py:366
  66.6 2.2 %collective-permute-start.17 = (f32[512]{0:T(512)S(1)}, f32[512]{0:T(512)S(1)}, u32[]{:S(2)}, u32[]{:S(2)}) collective-permute-start(f32[512]{0:T(512)S(1)} %bitcast.16), channel_id=1, source_target_pairs={{0,8},{2,10},{4,12},{6,14},{1,9},{3,11},{5,13},{7,15},{8,0},{10,2}... | collective-permute-start | bytes 6152 | tf_op jit(solution)/shard_map/ppermute | solution.py:366

commit v6 on v5

--- a/solution.py
+++ b/solution.py
@@ -370,7 +370,6 @@
     ]
     to_core = [((a, b, d, e), (a, 1 - b, d, e)) for a, b, d, e in everywhere]
     to_x = [((a, b, d, e), (1 - a, b, d, e)) for a, b, d, e in everywhere]
-    to_both = [((a, b, d, e), (1 - a, 1 - b, d, e)) for a, b, d, e in everywhere]
 
     def after(array, *earlier):
         return lax.optimization_barrier((array, *earlier))[0]
@@ -481,9 +480,8 @@
     partial = last(
         place, (get("r4_b"), crossed), get("begun"), folded, greens, get("fields")
     )[0]
-    here = partial + send(partial, to_core)
-    there = send(partial, to_x) + send(partial, to_both)
-    return here + there
+    chip = partial + send(partial, to_core)
+    return chip + send(chip, to_x)
 
 
 def gathered(trace_values, trace_owner, trace_source, source_fields, green_fields):

time: 69.7 us -> 70.9 us (1.017)
  waiting for transfers between devices: 21.6 us -> 24.3 us
  starting transfers between devices: 22.1 us -> 20.5 us
    ppermute x20 -> x19, waiting for transfers between devices: 21.6 us -> 24.3 us  [send(): return lax.ppermute(array, AXES, pairs)]
    ppermute x20 -> x19, starting transfers between devices: 22.1 us -> 20.5 us  [send(): return lax.ppermute(array, AXES, pairs)]
  transfers between devices with their start and end apart: 20 -> 19, of which waited for: 8 -> 9; matrix products, arithmetic and copies ran while one was open for 1% -> 1% of each run, Pallas kernels for 25% -> 25%
where the time goes in v6:
time: 70.9 us; the launch traced here: 70.6 us
  waiting for transfers between devices  24.3 us (34%)
  Pallas kernels  20.9 us (29%)
  starting transfers between devices  20.5 us (29%)
  local copies, waits for them, and re-layouts  3.12 us (4%)
  other arithmetic  1.5 us (2%)
    ppermute x19, waiting for transfers between devices, send(): return lax.ppermute(array, AXES, pairs)  24.3 us
    ppermute x19, starting transfers between devices, send(): return lax.ppermute(array, AXES, pairs)  20.5 us
    pallas_call x3, Pallas kernels, residual(): pl.pallas_call(functools.partial(residual_kernel, len(pieces)), name='res...  9.78 us
    pallas_call x2, Pallas kernels, correlated(): pl.pallas_call(functools.partial(correlate_kernel, len(res)), name='corre...  3.68 us
    pallas_call x1, Pallas kernels, last(): pl.pallas_call(functools.partial(last_kernel, len(cand_b)), name='last',...  3.44 us
    unnamed x6, local copies, waits for them, and re-layouts  2.26 us
    pallas_call x1, Pallas kernels, fold(): pl.pallas_call(functools.partial(fold_kernel, len(factors)), name='fold',...  1.96 us
    pallas_call x1, Pallas kernels, begin(): pl.pallas_call(functools.partial(begin_kernel, len(cand)), name='begin',...  1.79 us
  transfers between devices with their start and end apart: 19, of which 9 were waited for; matrix products, arithmetic and copies ran while one was open for 1% of the time, Pallas kernels for 25%

profile of v6, /device:TPU:0, one launch (start us, length us, event | category | flops | bytes accessed | tf_op | source)
XLA Modules:
  0.0 70.6 jit_solution(3672906808656886189)
XLA Ops:
  0.0 0.8 %fusion.4 = (bf16[1,512]{1,0:T(2,128)(2,1)S(1)}, bf16[1,512]{1,0:T(2,128)(2,1)S(1)}) fusion(s32[1,512,1]{1,2,0:T(1,128)} %param.7, s32[1,512]{1,0:T(1,128)} %param.8), kind=kLoop, calls=%fused_computation.11 | loop fusion | flops 11776 | bytes 6144 | tf_op jit(solution)/shard_map/convert.2
  0.8 0.0 copy-start.2
  0.8 1.0 %copy-done.2 = bf16[1,512,512]{2,1,0:T(8,128)(2,1)S(1)} copy-done((bf16[1,512,512]{2,1,0:T(8,128)(2,1)S(1)}, bf16[1,512,512]{2,1,0:T(8,128)(2,1)}, u32[]{:S(2)}) %copy-start.2) | copy-done | bytes 524312
  1.9 0.1 cut.1
  2.0 0.5 collective-permute-start.1
  2.5 2.6 %collective-permute-start = (bf16[528,256]{1,0:T(8,128)(2,1)S(1)}, bf16[528,256]{1,0:T(8,128)(2,1)S(1)}, u32[]{:S(2)}, u32[]{:S(2)}) collective-permute-start(bf16[528,256]{1,0:T(8,128)(2,1)S(1)} %get-tuple-element.22), channel_id=1, source_target_pairs={{0,16},{2,18},{4,20},{6,22},{1,17},{3,19},{5,21},{7,23},{8,24},{10... | collective-permute-start | bytes 811016 | tf_op jit(solution)/shard_map/ppermute | solution.py:366
  5.2 1.4 %collective-permute-start.6 = (bf16[1040,256]{1,0:T(8,128)(2,1)S(1)}, bf16[1040,256]{1,0:T(8,128)(2,1)}, u32[]{:S(2)}, u32[]{:S(2)}) collective-permute-start(bf16[1040,256]{1,0:T(8,128)(2,1)S(1)} %join.2.refs_1_), channel_id=1, source_target_pairs={{0,9},{6,15},{1,8},{7,14},{16,25},{22,31},{17,24},{23,30},{8,10},{... | collective-permute-start | bytes 1597448 | tf_op jit(solution)/shard_map/ppermute | solution.py:366
  6.5 1.4 %collective-permute-start.12 = (bf16[2,512,512]{2,1,0:T(8,128)(2,1)}, bf16[2,512,512]{2,1,0:T(8,128)(2,1)S(1)}, u32[]{:S(2)}, u32[]{:S(2)}) collective-permute-start(bf16[2,512,512]{2,1,0:T(8,128)(2,1)} %refs_8_.1), channel_id=1, source_target_pairs={{0,16},{2,18},{4,20},{6,22},{1,17},{3,19},{5,21},{7,23},{8,24},{10... | collective-permute-start | bytes 3145736 | tf_op jit(solution)/shard_map/ppermute | solution.py:366
  7.9 4.5 %collective-permute-done.mine = bf16[528,256]{1,0:T(8,128)(2,1)S(1)} collective-permute-done((bf16[528,256]{1,0:T(8,128)(2,1)S(1)}, bf16[528,256]{1,0:T(8,128)(2,1)S(1)}, u32[]{:S(2)}, u32[]{:S(2)}) %collective-permute-start) | collective-permute-done | bytes 270368 | tf_op jit(solution)/shard_map/ppermute | solution.py:366
  12.4 1.5 %collective-permute-done.2.other = bf16[528,256]{1,0:T(8,128)(2,1)S(1)} collective-permute-done((bf16[528,256]{1,0:T(8,128)(2,1)S(1)}, bf16[528,256]{1,0:T(8,128)(2,1)S(1)}, u32[]{:S(2)}, u32[]{:S(2)}) %collective-permute-start.2) | collective-permute-done | bytes 270368 | tf_op jit(solution)/shard_map/ppermute | solution.py:366
  14.0 1.8 %collective-permute-start.3 = (bf16[1040,256]{1,0:T(8,128)(2,1)S(1)}, bf16[1040,256]{1,0:T(8,128)(2,1)}, u32[]{:S(2)}, u32[]{:S(2)}) collective-permute-start(bf16[1040,256]{1,0:T(8,128)(2,1)S(1)} %join.3.refs_1_), channel_id=1, source_target_pairs={{0,9},{6,15},{1,8},{7,14},{16,25},{22,31},{17,24},{23,30},{8,10},{... | collective-permute-start | bytes 1597448 | tf_op jit(solution)/shard_map/ppermute | solution.py:366
  15.8 0.0 collective-permute-done.6.refs_0_
  15.8 1.3 %collective-permute-start.7 = (bf16[1040,256]{1,0:T(8,128)(2,1)}, bf16[1040,256]{1,0:T(8,128)(2,1)}, u32[]{:S(2)}, u32[]{:S(2)}) collective-permute-start(bf16[1040,256]{1,0:T(8,128)(2,1)} %collective-permute-done.6.refs_0_), channel_id=1, source_target_pairs={{0,9},{6,15},{1,8},{7,14},{16,25},{22,31},{17,24},{23,30},{8,2},{1... | collective-permute-start | bytes 1597448 | tf_op jit(solution)/shard_map/ppermute | solution.py:366
  17.1 0.7 dynamic-slice_bitcast_fusion
  17.8 0.1 copy.8
  17.9 0.1 reshape.20
  18.0 5.5 %collective-permute-done.3.refs_1_ = bf16[1040,256]{1,0:T(8,128)(2,1)} collective-permute-done((bf16[1040,256]{1,0:T(8,128)(2,1)S(1)}, bf16[1040,256]{1,0:T(8,128)(2,1)}, u32[]{:S(2)}, u32[]{:S(2)}) %collective-permute-start.3) | collective-permute-done | bytes 532512 | tf_op jit(solution)/shard_map/ppermute | solution.py:366
  23.5 1.4 %collective-permute-start.4 = (bf16[1040,256]{1,0:T(8,128)(2,1)}, bf16[1040,256]{1,0:T(8,128)(2,1)S(1)}, u32[]{:S(2)}, u32[]{:S(2)}) collective-permute-start(bf16[1040,256]{1,0:T(8,128)(2,1)} %collective-permute-done.3.refs_1_), channel_id=1, source_target_pairs={{0,9},{6,15},{1,8},{7,14},{16,25},{22,31},{17,24},{23,30},{8,2},{1... | collective-permute-start | bytes 1597448 | tf_op jit(solution)/shard_map/ppermute | solution.py:366
  24.9 4.3 %collective-permute-done.7.refs_0_ = bf16[1040,256]{1,0:T(8,128)(2,1)} collective-permute-done((bf16[1040,256]{1,0:T(8,128)(2,1)}, bf16[1040,256]{1,0:T(8,128)(2,1)}, u32[]{:S(2)}, u32[]{:S(2)}) %collective-permute-start.7) | collective-permute-done | bytes 532512 | tf_op jit(solution)/shard_map/ppermute | solution.py:366
  29.2 1.4 %collective-permute-start.8 = (bf16[1040,256]{1,0:T(8,128)(2,1)}, bf16[1040,256]{1,0:T(8,128)(2,1)S(1)}, u32[]{:S(2)}, u32[]{:S(2)}) collective-permute-start(bf16[1040,256]{1,0:T(8,128)(2,1)} %collective-permute-done.7.refs_0_), channel_id=1, source_target_pairs={{0,9},{6,15},{1,8},{7,14},{16,25},{22,31},{17,24},{23,30},{8,10},{... | collective-permute-start | bytes 1597448 | tf_op jit(solution)/shard_map/ppermute | solution.py:366
  30.6 0.1 pad_add_fusion.1.place
  30.7 0.0 collective-permute-start.11
  30.7 0.0 copy-start.1
  30.7 1.2 %copy-done.1 = bf16[2,512,512]{2,1,0:T(8,128)(2,1)S(1)} copy-done((bf16[2,512,512]{2,1,0:T(8,128)(2,1)S(1)}, bf16[2,512,512]{2,1,0:T(8,128)(2,1)}, u32[]{:S(2)}) %copy-start.1) | copy-done | bytes 1048600
  31.9 0.1 halves.1
  32.0 3.5 %residual.4.refs_0_ = bf16[2048,256]{1,0:T(8,128)(2,1)S(1)} custom-call(s32[10]{0:T(128)S(1)} %pad_add_fusion.1.place, bf16[1040,256]{1,0:T(8,128)(2,1)} %collective-permute-done.6.refs_0_, bf16[1040,256]{1,0:T(8,128)(2,1)} %collective-permute-done.3.refs_1_), custom_call_target="tpu_custom_call" | custom-call | flops 1000 | bytes 1000 | tf_op jit(solution)/shard_map/residual/pallas_call | solution.py:186
  35.6 0.6 collective-permute-start.14
  36.1 0.1 collective-permute-start.13
  36.2 0.9 %collective-permute-done.4.refs_1_ = bf16[1040,256]{1,0:T(8,128)(2,1)S(1)} collective-permute-done((bf16[1040,256]{1,0:T(8,128)(2,1)}, bf16[1040,256]{1,0:T(8,128)(2,1)S(1)}, u32[]{:S(2)}, u32[]{:S(2)}) %collective-permute-start.4) | collective-permute-done | bytes 532512 | tf_op jit(solution)/shard_map/ppermute | solution.py:366
  37.1 0.0 collective-permute-start.5
  37.1 0.5 collective-permute-done.14.refs_3_.refs_5_
  37.7 2.8 %collective-permute-done.8.refs_0_ = bf16[1040,256]{1,0:T(8,128)(2,1)S(1)} collective-permute-done((bf16[1040,256]{1,0:T(8,128)(2,1)}, bf16[1040,256]{1,0:T(8,128)(2,1)S(1)}, u32[]{:S(2)}, u32[]{:S(2)}) %collective-permute-start.8) | collective-permute-done | bytes 532512 | tf_op jit(solution)/shard_map/ppermute | solution.py:366
  40.5 1.9 %collective-permute-start.15 = (bf16[2,2,128,512]{3,2,1,0:T(8,128)(2,1)S(1)}, bf16[2,2,128,512]{3,2,1,0:T(8,128)(2,1)S(1)}, u32[]{:S(2)}, u32[]{:S(2)}) collective-permute-start(bf16[2,2,128,512]{3,2,1,0:T(8,128)(2,1)S(1)} %get-tuple-element.37), channel_id=1, source_target_pairs={{0,16},{2,18},{4,20},{6,22},{1,17},{3,19},{5,21},{7,23},{8,24},{10... | collective-permute-start | bytes 1572872 | tf_op jit(solution)/shard_map/ppermute | solution.py:366
  42.4 2.6 %collective-permute-start.10 = (bf16[1040,256]{1,0:T(8,128)(2,1)S(1)}, bf16[1040,256]{1,0:T(8,128)(2,1)S(1)}, u32[]{:S(2)}, u32[]{:S(2)}) collective-permute-start(bf16[1040,256]{1,0:T(8,128)(2,1)S(1)} %collective-permute-done.8.refs_0_), channel_id=1, source_target_pairs={{0,9},{6,15},{1,8},{7,14},{16,25},{22,31},{17,24},{23,30},{10,12},... | collective-permute-start | bytes 1597448 | tf_op jit(solution)/shard_map/ppermute | solution.py:366
  45.1 3.4 %residual.3.refs_1_ = bf16[2048,256]{1,0:T(8,128)(2,1)S(1)} custom-call(s32[10]{0:T(128)S(1)} %pad_add_fusion.1.place, bf16[1040,256]{1,0:T(8,128)(2,1)} %collective-permute-done.7.refs_0_, bf16[1040,256]{1,0:T(8,128)(2,1)S(1)} %collective-permute-done.4.refs_1_), custom_call_target="tpu_custom_call" | custom-call | flops 1000 | bytes 1000 | tf_op jit(solution)/shard_map/residual/pallas_call | solution.py:186
  48.5 0.7 collective-permute-start.9
  49.2 2.4 %correlate.2.refs_0_ = f32[2,2,128,512]{3,2,1,0:T(8,128)S(1)} custom-call(bf16[2048,256]{1,0:T(8,128)(2,1)S(1)} %residual.4.refs_0_, bf16[2048,256]{1,0:T(8,128)(2,1)S(1)} %residual.3.refs_1_, bf16[2,512,512]{2,1,0:T(8,128)(2,1)S(1)} %copy-done, bf16[2,512,512]{2,1,0:T(8,128)(2,1)S(1)} %collective-permute-done.11.refs_3_.refs_2_.refs_9_, ...), custom_call_target="tpu_custom_call" | custom-call | flops 1000 | bytes 1000 | tf_op jit(solution)/shard_map/correlate/pallas_call | solution.py:252
  51.6 2.9 %residual.5.refs_0_ = bf16[2048,256]{1,0:T(8,128)(2,1)S(1)} custom-call(s32[10]{0:T(128)S(1)} %pad_add_fusion.1.place, bf16[1040,256]{1,0:T(8,128)(2,1)S(1)} %collective-permute-done.8.refs_0_, bf16[1040,256]{1,0:T(8,128)(2,1)S(1)} %collective-permute-done.5.refs_1_), custom_call_target="tpu_custom_call" | custom-call | flops 1000 | bytes 1000 | tf_op jit(solution)/shard_map/residual/pallas_call | solution.py:186
  54.5 2.2 %collective-permute-start.16 = (bf16[2,2,128,512]{3,2,1,0:T(8,128)(2,1)S(1)}, bf16[2,2,128,512]{3,2,1,0:T(8,128)(2,1)S(1)}, u32[]{:S(2)}, u32[]{:S(2)}) collective-permute-start(bf16[2,2,128,512]{3,2,1,0:T(8,128)(2,1)S(1)} %collective-permute-done.15.refs_4_.refs_6_), channel_id=1, source_target_pairs={{0,8},{2,10},{4,12},{6,14},{1,9},{3,11},{5,13},{7,15},{8,0},{10,2}... | collective-permute-start | bytes 1572872 | tf_op jit(solution)/shard_map/ppermute | solution.py:366
  56.6 1.3 %correlate.3.refs_1_ = f32[1,2,128,512]{3,2,1,0:T(8,128)S(1)} custom-call(bf16[2048,256]{1,0:T(8,128)(2,1)S(1)} %residual.5.refs_0_, bf16[2,512,512]{2,1,0:T(8,128)(2,1)S(1)} %copy-done, bf16[2,512,512]{2,1,0:T(8,128)(2,1)S(1)} %collective-permute-done.11.refs_3_.refs_2_.refs_9_, bf16[2,512,512]{2,1,0:T(8,128)(2,1)S(1)} %collective-permute-done.12.refs_4_.refs_3_.refs_10_, ...), custom_call_target="tpu_custom_call" | custom-call | flops 1000 | bytes 1000 | tf_op jit(solution)/shard_map/correlate/pallas_call | solution.py:252
  57.9 1.8 %begin.1.refs_2_ = f32[2048,256]{1,0:T(8,128)S(1)} custom-call(s32[10]{0:T(128)S(1)} %pad_add_fusion.1.place, bf16[1040,256]{1,0:T(8,128)(2,1)S(1)} %collective-permute-done.10.refs_0_, bf16[1040,256]{1,0:T(8,128)(2,1)S(1)} %join.2.refs_1_), custom_call_target="tpu_custom_call" | custom-call | flops 1000 | bytes 1000 | tf_op jit(solution)/shard_map/begin/pallas_call | solution.py:209
  59.7 2.0 %fold.1.refs_3_ = f32[1,512]{1,0:T(1,128)S(1)} custom-call(s32[10]{0:T(128)S(1)} %pad_add_fusion.1.place, f32[2,2,128,512]{3,2,1,0:T(8,128)S(1)} %correlate.2.refs_0_, f32[1,2,128,512]{3,2,1,0:T(8,128)S(1)} %correlate.3.refs_1_, bf16[2,2,128,512]{3,2,1,0:T(8,128)(2,1)S(1)} %get-tuple-element.35.refs_2_.refs_4_, ...), custom_call_target="tpu_custom_call" | custom-call | flops 1000 | bytes 1000 | tf_op jit(solution)/shard_map/fold/pallas_call | solution.py:297
  61.7 3.4 %last.1 = f32[1,512]{1,0:T(1,128)S(1)} custom-call(s32[10]{0:T(128)S(1)} %pad_add_fusion.1.place, bf16[1040,256]{1,0:T(8,128)(2,1)S(1)} %collective-permute-done.9.refs_0_, bf16[1040,256]{1,0:T(8,128)(2,1)S(1)} %join.3.refs_1_, f32[2048,256]{1,0:T(8,128)S(1)} %begin.1.refs_2_, f32[1,512]{1,0:T(1,128)S(1)} %fold.1.refs_3_, ...), custom_call_target="tpu_custom_call" | custom-call | flops 1000 | bytes 1000 | tf_op jit(solution)/shard_map/last/pallas_call | solution.py:336
  65.2 0.1 collective-permute-start.17
  65.3 1.1 %collective-permute-done.17 = f32[512]{0:T(512)S(1)} collective-permute-done((f32[512]{0:T(512)S(1)}, f32[512]{0:T(512)S(1)}, u32[]{:S(2)}, u32[]{:S(2)}) %collective-permute-start.17) | collective-permute-done | bytes 2080 | tf_op jit(solution)/shard_map/ppermute | solution.py:366
  66.4 0.5 collective-permute-start.18
  66.9 3.0 %collective-permute-done.18 = f32[512]{0:T(512)S(1)} collective-permute-done((f32[512]{0:T(512)S(1)}, f32[512]{0:T(512)S(1)}, u32[]{:S(2)}, u32[]{:S(2)}) %collective-permute-start.18) | collective-permute-done | bytes 2080 | tf_op jit(solution)/shard_map/ppermute | solution.py:366
  70.0 0.6 add.49
  (18 shorter events, 0.1 us)
Async XLA Ops:
  0.0 30.7 %copy-start = (bf16[2,512,512]{2,1,0:T(8,128)(2,1)S(1)}, bf16[2,512,512]{2,1,0:T(8,128)(2,1)}, u32[]{:S(2)}) copy-start(bf16[2,512,512]{2,1,0:T(8,128)(2,1)} %refs_8_.1) | copy-start | bytes 3145732
  0.8 1.0 %copy-start.2 = (bf16[1,512,512]{2,1,0:T(8,128)(2,1)S(1)}, bf16[1,512,512]{2,1,0:T(8,128)(2,1)}, u32[]{:S(2)}) copy-start(bf16[1,512,512]{2,1,0:T(8,128)(2,1)} %param.6) | copy-start | bytes 1572868
  2.0 3.1 %collective-permute-start.1 = (bf16[528,256]{1,0:T(8,128)(2,1)S(1)}, bf16[528,256]{1,0:T(8,128)(2,1)S(1)}, u32[]{:S(2)}, u32[]{:S(2)}) collective-permute-start(bf16[528,256]{1,0:T(8,128)(2,1)S(1)} %get-tuple-element.23.mine), channel_id=1, source_target_pairs={{0,8},{2,10},{4,12},{6,14},{1,9},{3,11},{5,13},{7,15},{8,0},{10,2}... | collective-permute-start | bytes 811016 | tf_op jit(solution)/shard_map/ppermute | solution.py:366
  2.5 9.9 %collective-permute-start = (bf16[528,256]{1,0:T(8,128)(2,1)S(1)}, bf16[528,256]{1,0:T(8,128)(2,1)S(1)}, u32[]{:S(2)}, u32[]{:S(2)}) collective-permute-start(bf16[528,256]{1,0:T(8,128)(2,1)S(1)} %get-tuple-element.22), channel_id=1, source_target_pairs={{0,16},{2,18},{4,20},{6,22},{1,17},{3,19},{5,21},{7,23},{8,24},{10... | collective-permute-start | bytes 811016 | tf_op jit(solution)/shard_map/ppermute | solution.py:366
  5.2 10.7 %collective-permute-start.6 = (bf16[1040,256]{1,0:T(8,128)(2,1)S(1)}, bf16[1040,256]{1,0:T(8,128)(2,1)}, u32[]{:S(2)}, u32[]{:S(2)}) collective-permute-start(bf16[1040,256]{1,0:T(8,128)(2,1)S(1)} %join.2.refs_1_), channel_id=1, source_target_pairs={{0,9},{6,15},{1,8},{7,14},{16,25},{22,31},{17,24},{23,30},{8,10},{... | collective-permute-start | bytes 1597448 | tf_op jit(solution)/shard_map/ppermute | solution.py:366
  6.5 29.1 %collective-permute-start.12 = (bf16[2,512,512]{2,1,0:T(8,128)(2,1)}, bf16[2,512,512]{2,1,0:T(8,128)(2,1)S(1)}, u32[]{:S(2)}, u32[]{:S(2)}) collective-permute-start(bf16[2,512,512]{2,1,0:T(8,128)(2,1)} %refs_8_.1), channel_id=1, source_target_pairs={{0,16},{2,18},{4,20},{6,22},{1,17},{3,19},{5,21},{7,23},{8,24},{10... | collective-permute-start | bytes 3145736 | tf_op jit(solution)/shard_map/ppermute | solution.py:366
  12.4 1.5 %collective-permute-start.2 = (bf16[528,256]{1,0:T(8,128)(2,1)S(1)}, bf16[528,256]{1,0:T(8,128)(2,1)S(1)}, u32[]{:S(2)}, u32[]{:S(2)}) collective-permute-start(bf16[528,256]{1,0:T(8,128)(2,1)S(1)} %collective-permute-done.mine), channel_id=1, source_target_pairs={{0,8},{2,10},{4,12},{6,14},{1,9},{3,11},{5,13},{7,15},{8,0},{10,2}... | collective-permute-start | bytes 811016 | tf_op jit(solution)/shard_map/ppermute | solution.py:366
  14.0 9.5 %collective-permute-start.3 = (bf16[1040,256]{1,0:T(8,128)(2,1)S(1)}, bf16[1040,256]{1,0:T(8,128)(2,1)}, u32[]{:S(2)}, u32[]{:S(2)}) collective-permute-start(bf16[1040,256]{1,0:T(8,128)(2,1)S(1)} %join.3.refs_1_), channel_id=1, source_target_pairs={{0,9},{6,15},{1,8},{7,14},{16,25},{22,31},{17,24},{23,30},{8,10},{... | collective-permute-start | bytes 1597448 | tf_op jit(solution)/shard_map/ppermute | solution.py:366
  15.8 13.4 %collective-permute-start.7 = (bf16[1040,256]{1,0:T(8,128)(2,1)}, bf16[1040,256]{1,0:T(8,128)(2,1)}, u32[]{:S(2)}, u32[]{:S(2)}) collective-permute-start(bf16[1040,256]{1,0:T(8,128)(2,1)} %collective-permute-done.6.refs_0_), channel_id=1, source_target_pairs={{0,9},{6,15},{1,8},{7,14},{16,25},{22,31},{17,24},{23,30},{8,2},{1... | collective-permute-start | bytes 1597448 | tf_op jit(solution)/shard_map/ppermute | solution.py:366
  23.5 13.6 %collective-permute-start.4 = (bf16[1040,256]{1,0:T(8,128)(2,1)}, bf16[1040,256]{1,0:T(8,128)(2,1)S(1)}, u32[]{:S(2)}, u32[]{:S(2)}) collective-permute-start(bf16[1040,256]{1,0:T(8,128)(2,1)} %collective-permute-done.3.refs_1_), channel_id=1, source_target_pairs={{0,9},{6,15},{1,8},{7,14},{16,25},{22,31},{17,24},{23,30},{8,2},{1... | collective-permute-start | bytes 1597448 | tf_op jit(solution)/shard_map/ppermute | solution.py:366
  29.2 11.3 %collective-permute-start.8 = (bf16[1040,256]{1,0:T(8,128)(2,1)}, bf16[1040,256]{1,0:T(8,128)(2,1)S(1)}, u32[]{:S(2)}, u32[]{:S(2)}) collective-permute-start(bf16[1040,256]{1,0:T(8,128)(2,1)} %collective-permute-done.7.refs_0_), channel_id=1, source_target_pairs={{0,9},{6,15},{1,8},{7,14},{16,25},{22,31},{17,24},{23,30},{8,10},{... | collective-permute-start | bytes 1597448 | tf_op jit(solution)/shard_map/ppermute | solution.py:366
  30.7 18.5 %collective-permute-start.11 = (bf16[2,512,512]{2,1,0:T(8,128)(2,1)S(1)}, bf16[2,512,512]{2,1,0:T(8,128)(2,1)S(1)}, u32[]{:S(2)}, u32[]{:S(2)}) collective-permute-start(bf16[2,512,512]{2,1,0:T(8,128)(2,1)S(1)} %copy-done), channel_id=1, source_target_pairs={{0,8},{2,10},{4,12},{6,14},{1,9},{3,11},{5,13},{7,15},{8,0},{10,2}... | collective-permute-start | bytes 3145736 | tf_op jit(solution)/shard_map/ppermute | solution.py:366
  30.7 1.2 %copy-start.1 = (bf16[2,512,512]{2,1,0:T(8,128)(2,1)S(1)}, bf16[2,512,512]{2,1,0:T(8,128)(2,1)}, u32[]{:S(2)}) copy-start(bf16[2,512,512]{2,1,0:T(8,128)(2,1)} %param.10) | copy-start | bytes 3145732
  35.6 2.1 %collective-permute-start.14 = (bf16[2,2,128,512]{3,2,1,0:T(8,128)(2,1)S(1)}, bf16[2,2,128,512]{3,2,1,0:T(8,128)(2,1)S(1)}, u32[]{:S(2)}, u32[]{:S(2)}) collective-permute-start(bf16[2,2,128,512]{3,2,1,0:T(8,128)(2,1)S(1)} %get-tuple-element.35.refs_2_.refs_4_), channel_id=1, source_target_pairs={{0,8},{2,10},{4,12},{6,14},{1,9},{3,11},{5,13},{7,15},{8,0},{10,2}... | collective-permute-start | bytes 1572872 | tf_op jit(solution)/shard_map/ppermute | solution.py:366
  36.1 13.0 %collective-permute-start.13 = (bf16[2,512,512]{2,1,0:T(8,128)(2,1)S(1)}, bf16[2,512,512]{2,1,0:T(8,128)(2,1)S(1)}, u32[]{:S(2)}, u32[]{:S(2)}) collective-permute-start(bf16[2,512,512]{2,1,0:T(8,128)(2,1)S(1)} %collective-permute-done.12.refs_4_.refs_3_.refs_10_), channel_id=1, source_target_pairs={{0,8},{2,10},{4,12},{6,14},{1,9},{3,11},{5,13},{7,15},{8,0},{10,2}... | collective-permute-start | bytes 3145736 | tf_op jit(solution)/shard_map/ppermute | solution.py:366
  37.1 11.3 %collective-permute-start.5 = (bf16[1040,256]{1,0:T(8,128)(2,1)S(1)}, bf16[1040,256]{1,0:T(8,128)(2,1)S(1)}, u32[]{:S(2)}, u32[]{:S(2)}) collective-permute-start(bf16[1040,256]{1,0:T(8,128)(2,1)S(1)} %collective-permute-done.4.refs_1_), channel_id=1, source_target_pairs={{0,9},{6,15},{1,8},{7,14},{16,25},{22,31},{17,24},{23,30},{8,10},{... | collective-permute-start | bytes 1597448 | tf_op jit(solution)/shard_map/ppermute | solution.py:366
  40.5 14.0 %collective-permute-start.15 = (bf16[2,2,128,512]{3,2,1,0:T(8,128)(2,1)S(1)}, bf16[2,2,128,512]{3,2,1,0:T(8,128)(2,1)S(1)}, u32[]{:S(2)}, u32[]{:S(2)}) collective-permute-start(bf16[2,2,128,512]{3,2,1,0:T(8,128)(2,1)S(1)} %get-tuple-element.37), channel_id=1, source_target_pairs={{0,16},{2,18},{4,20},{6,22},{1,17},{3,19},{5,21},{7,23},{8,24},{10... | collective-permute-start | bytes 1572872 | tf_op jit(solution)/shard_map/ppermute | solution.py:366
  42.4 15.5 %collective-permute-start.10 = (bf16[1040,256]{1,0:T(8,128)(2,1)S(1)}, bf16[1040,256]{1,0:T(8,128)(2,1)S(1)}, u32[]{:S(2)}, u32[]{:S(2)}) collective-permute-start(bf16[1040,256]{1,0:T(8,128)(2,1)S(1)} %collective-permute-done.8.refs_0_), channel_id=1, source_target_pairs={{0,9},{6,15},{1,8},{7,14},{16,25},{22,31},{17,24},{23,30},{10,12},... | collective-permute-start | bytes 1597448 | tf_op jit(solution)/shard_map/ppermute | solution.py:366
  48.5 13.3 %collective-permute-start.9 = (bf16[1040,256]{1,0:T(8,128)(2,1)S(1)}, bf16[1040,256]{1,0:T(8,128)(2,1)S(1)}, u32[]{:S(2)}, u32[]{:S(2)}) collective-permute-start(bf16[1040,256]{1,0:T(8,128)(2,1)S(1)} %collective-permute-done.5.refs_1_), channel_id=1, source_target_pairs={{8,10},{14,12},{9,11},{15,13},{24,26},{30,28},{25,27},{31,29},{2,8... | collective-permute-start | bytes 1597448 | tf_op jit(solution)/shard_map/ppermute | solution.py:366
  54.5 5.3 %collective-permute-start.16 = (bf16[2,2,128,512]{3,2,1,0:T(8,128)(2,1)S(1)}, bf16[2,2,128,512]{3,2,1,0:T(8,128)(2,1)S(1)}, u32[]{:S(2)}, u32[]{:S(2)}) collective-permute-start(bf16[2,2,128,512]{3,2,1,0:T(8,128)(2,1)S(1)} %collective-permute-done.15.refs_4_.refs_6_), channel_id=1, source_target_pairs={{0,8},{2,10},{4,12},{6,14},{1,9},{3,11},{5,13},{7,15},{8,0},{10,2}... | collective-permute-start | bytes 1572872 | tf_op jit(solution)/shard_map/ppermute | solution.py:366
  65.2 1.2 %collective-permute-start.17 = (f32[512]{0:T(512)S(1)}, f32[512]{0:T(512)S(1)}, u32[]{:S(2)}, u32[]{:S(2)}) collective-permute-start(f32[512]{0:T(512)S(1)} %bitcast.14), channel_id=1, source_target_pairs={{0,8},{2,10},{4,12},{6,14},{1,9},{3,11},{5,13},{7,15},{8,0},{10,2}... | collective-permute-start | bytes 6152 | tf_op jit(solution)/shard_map/ppermute | solution.py:366
  66.4 3.6 %collective-permute-start.18 = (f32[512]{0:T(512)S(1)}, f32[512]{0:T(512)S(1)}, u32[]{:S(2)}, u32[]{:S(2)}) collective-permute-start(f32[512]{0:T(512)S(1)} %add.48), channel_id=1, source_target_pairs={{0,16},{2,18},{4,20},{6,22},{1,17},{3,19},{5,21},{7,23},{8,24},{10... | collective-permute-start | bytes 6152 | tf_op jit(solution)/shard_map/ppermute | solution.py:366
